TPU v7x, 32 devices: a whole 2x2x4 slice. The times are simulated.
32 devices in a mesh: blk: 8 (over z, y), grp: 4 (over x, core).
Axes of the slice: x: 2, y: 2, z: 4, core: 2. Of those that a mesh axis runs over, the one named last changes fastest.
Arguments:
- token_ids: int32 [128, 2, 128], P(('blk', 'grp')), may hold values from 0 to 30719
- lengths: int32 [128, 2], P(('blk', 'grp')), may hold values from 32 to 128, as said below
- valid: int32 [128], P(('blk', 'grp')), may hold values from 0 to 1
- false_neg: int32 [128, 128], P(('blk', 'grp')), may hold values from 0 to 1, as said below
- word_table: bfloat16 [30720, 768], P('grp'), may hold values from -1.75 to 1.75
- qkv_weight: bfloat16 [768, 2304], replicated, may hold values from -0.21875 to 0.21875
- out_weight: bfloat16 [768, 768], replicated, may hold values from -1.75 to 1.75
- up_weight: bfloat16 [768, 3072], replicated, may hold values from -0.21875 to 0.21875
- down_weight: bfloat16 [3072, 768], replicated, may hold values from -0.109375 to 0.109375
- word_master: float32 [30720, 768], P('blk'), may hold values from -1.75 to 1.75
- qkv_master: float32 [768, 2304], P('blk'), may hold values from -0.21875 to 0.21875
- out_master: float32 [768, 768], P('blk'), may hold values from -1.75 to 1.75
- up_master: float32 [768, 3072], P('blk'), may hold values from -0.21875 to 0.21875
- down_master: float32 [3072, 768], P('blk'), may hold values from -0.109375 to 0.109375
- word_moments: float32 [2, 30720, 768], P(None, 'blk'), as said below
- qkv_moments: float32 [2, 768, 2304], P(None, 'blk'), as said below
- out_moments: float32 [2, 768, 768], P(None, 'blk'), as said below
- up_moments: float32 [2, 768, 3072], P(None, 'blk'), as said below
- down_moments: float32 [2, 3072, 768], P(None, 'blk'), as said below
- small_rows: float32 [142, 768], replicated
- small_moments: float32 [2, 142, 768], replicated, as said below
Outputs:
- loss_sum: float32 [], replicated
- pair_count: float32 [], replicated
- grad_norm: float32 [], replicated
- word_first: float32 [30720, 768], P('blk')
- word_second: float32 [30720, 768], P('blk')
- word_updated: float32 [30720, 768], P('blk')
- qkv_first: float32 [768, 2304], P('blk')
- qkv_second: float32 [768, 2304], P('blk')
- qkv_updated: float32 [768, 2304], P('blk')
- out_first: float32 [768, 768], P('blk')
- out_second: float32 [768, 768], P('blk')
- out_updated: float32 [768, 768], P('blk')
- up_first: float32 [768, 3072], P('blk')
- up_second: float32 [768, 3072], P('blk')
- up_updated: float32 [768, 3072], P('blk')
- down_first: float32 [3072, 768], P('blk')
- down_second: float32 [3072, 768], P('blk')
- down_updated: float32 [3072, 768], P('blk')
- small_first: float32 [142, 768], replicated
- small_second: float32 [142, 768], replicated
- small_updated: float32 [142, 768], replicated
Inputs may be any that keep to these rules, and one draw needn't show every extreme that they name: `lengths`: at least one sequence has length exactly 128. `false_neg`: symmetric, zero on the diagonal. `word_moments`: the second of the two stacked moments is positive. `qkv_moments`: the second of the two stacked moments is positive. `out_moments`: the second of the two stacked moments is positive. `up_moments`: the second of the two stacked moments is positive. `down_moments`: the second of the two stacked moments is positive. `small_moments`: the second of the two stacked moments is positive.
All inputs are finite; a program needn't handle non-finite values.
Results may differ from a plain program's by a relative error of at most 0.011.
Values may be sent and summed in bfloat16 or wider, within the bound.
No kernel may reach another device: no remote copies, remote signals or barrier semaphores. Data moves between devices by JAX's collectives and lax.ppermute only.
A program may use at most 384 MiB of HBM per device.

v0:
```python
import jax
import jax.numpy as jnp
from jax import lax
from jax.sharding import PartitionSpec as P

HEADS = 12
STEP = 5


logit_divisor_constant = 0.01
clip_bound = 0.001
beta_first = 0.5
beta_second = 0.5
decay_weight = 0.01
epsilon = 1e-08
rate_table = (0.1, 0.02, 0.1, 0.02, 0.01, 0.2)
finest_arithmetic = lax.Precision.HIGHEST


def layer_norm(states, gain, shift):
    mean = jnp.mean(states, -1, keepdims=True)
    centered = states - mean
    variance = jnp.mean(centered * centered, -1, keepdims=True)
    return centered * lax.rsqrt(variance + 1e-06) * gain + shift


def exact_gelu(values):
    return jax.nn.gelu(values, approximate=False)


def pool_unit(states, lengths_flat):
    positions = jnp.arange(states.shape[1])
    weights = (positions[None, :] < lengths_flat[:, None]).astype(jnp.float32)
    pooled = jnp.sum(states * weights[:, :, None], 1) / lengths_flat[:, None].astype(jnp.float32)
    return pooled * lax.rsqrt(jnp.sum(pooled * pooled, -1, keepdims=True) + 1e-06)


def contract_rows(left, right):
    return lax.dot_general(
        left, right, (((0,), (0,)), ((), ())), preferred_element_type=jnp.float32
    )


def contract_cols(left, right):
    return lax.dot_general(
        left, right, (((1,), (1,)), ((), ())), preferred_element_type=jnp.float32
    )


def adam_update(grad, moments, master, rate):
    first = beta_first * moments[0] + (1.0 - beta_first) * grad
    second = beta_second * moments[1] + (1.0 - beta_second) * grad * grad
    first_hat = first / (1.0 - beta_first**STEP)
    second_hat = second / (1.0 - beta_second**STEP)
    updated = master - rate * (first_hat / (jnp.sqrt(second_hat) + epsilon) + decay_weight * master)
    return (first, second, updated)


def masked_softmax(pairwise_affinity_matrix, allowed):
    masked = jnp.where(allowed, pairwise_affinity_matrix, -1000000000.0)
    top = jnp.max(masked, -1, keepdims=True)
    expo = jnp.where(allowed, jnp.exp(masked - top), 0.0)
    total = jnp.sum(expo, -1, keepdims=True)
    return (top[:, 0] + jnp.log(total[:, 0]), expo / total)


def reduce_matrices(flat_ids, token_grads, table_rows, qkv_grad, out_grad, up_grad, down_grad):
    width = token_grads.shape[1]
    shard_rows = table_rows // lax.axis_size("blk")
    first_row = lax.axis_index("blk") * shard_rows
    id_floats = lax.all_gather(flat_ids.astype(jnp.float32), "blk", axis=0, tiled=True)
    grad_rows = lax.all_gather(token_grads, "blk", axis=0, tiled=True)
    local = id_floats.astype(jnp.int32) - first_row
    inside = (local >= 0) & (local < shard_rows)
    word_rows = (
        jnp.zeros((shard_rows, width), jnp.float32)
        .at[jnp.where(inside, local, shard_rows)]
        .add(grad_rows, mode="drop")
    )
    qkv_rows, out_rows, up_rows, down_rows = (
        lax.psum_scatter(qkv_grad, "blk", scatter_dimension=0, tiled=True),
        lax.psum_scatter(out_grad, "blk", scatter_dimension=0, tiled=True),
        lax.psum_scatter(up_grad, "blk", scatter_dimension=0, tiled=True),
        lax.psum_scatter(down_grad, "blk", scatter_dimension=0, tiled=True),
    )
    return lax.psum((word_rows, qkv_rows, out_rows, up_rows, down_rows), "grp")


def on_device(
    token_ids,
    lengths,
    valid,
    false_neg,
    word_table,
    qkv_weight,
    out_weight,
    up_weight,
    down_weight,
    word_master,
    qkv_master,
    out_master,
    up_master,
    down_master,
    word_moments,
    qkv_moments,
    out_moments,
    up_moments,
    down_moments,
    small_rows,
    small_moments,
):
    word_whole = lax.all_gather(word_table, "grp", axis=0, tiled=True)
    pairs_here = token_ids.shape[0]
    seq_count = 2 * pairs_here
    seq_len = token_ids.shape[2]
    width = word_whole.shape[1]
    head_dim = width // HEADS
    scale = head_dim ** (-0.5)
    flat_ids = token_ids.reshape(-1)
    lengths_flat = lengths.reshape(-1)
    vectors = small_rows[seq_len:]
    embedded = (
        word_whole[flat_ids].astype(jnp.float32).reshape(seq_count, seq_len, width)
        + small_rows[:seq_len]
    )
    normed, first_back = jax.vjp(layer_norm, embedded, vectors[0], vectors[1])
    normed_low = normed.reshape(-1, width).astype(jnp.bfloat16)
    qkv_bias = jnp.concatenate([vectors[2], jnp.zeros((width,), jnp.float32), vectors[3]])
    projected = (
        jnp.dot(normed_low, qkv_weight, preferred_element_type=jnp.float32) + qkv_bias
    ).astype(jnp.bfloat16)
    shape = (seq_count, seq_len, HEADS, head_dim)
    query = projected[:, :width].reshape(shape)
    keys = projected[:, width : 2 * width].reshape(shape)
    values = projected[:, 2 * width :].reshape(shape)
    key_live = (jnp.arange(seq_len)[None, :] < lengths_flat[:, None])[:, None, None, :]

    def masked_logits():
        unnormalized_affinity = (
            jnp.einsum("sqhe,skhe->shqk", query, keys, preferred_element_type=jnp.float32) * scale
        )
        return jnp.where(key_live, unnormalized_affinity, -1000000000.0)

    unnormalized_affinity = masked_logits()
    top = jnp.max(unnormalized_affinity, -1, keepdims=True)
    log_total = top + jnp.log(jnp.sum(jnp.exp(unnormalized_affinity - top), -1, keepdims=True))
    probs_low = jnp.exp(unnormalized_affinity - log_total).astype(jnp.bfloat16)
    attended = jnp.einsum("shqk,skhe->sqhe", probs_low, values, preferred_element_type=jnp.float32)
    attended = attended.reshape(-1, width).astype(jnp.bfloat16)
    branch = jnp.dot(attended, out_weight, preferred_element_type=jnp.float32) + vectors[4]
    middle, second_back = jax.vjp(
        layer_norm, normed.reshape(-1, width) + branch, vectors[5], vectors[6]
    )
    middle_low = middle.astype(jnp.bfloat16)
    lifted = jnp.dot(middle_low, up_weight, preferred_element_type=jnp.float32) + vectors[
        10:14
    ].reshape(-1)
    activated, gelu_back = jax.vjp(exact_gelu, lifted)
    activated_low = activated.astype(jnp.bfloat16)
    lowered = jnp.dot(activated_low, down_weight, preferred_element_type=jnp.float32) + vectors[7]
    final, third_back = jax.vjp(layer_norm, middle + lowered, vectors[8], vectors[9])
    unit, pool_back = jax.vjp(
        lambda states: pool_unit(states.reshape(seq_count, seq_len, width), lengths_flat), final
    )
    own_embed = unit.astype(jnp.bfloat16).reshape(pairs_here, 2, width)
    gathered, live_cols = (
        lax.all_gather(own_embed, ("blk", "grp"), axis=0, tiled=True),
        lax.all_gather(valid, ("blk", "grp"), axis=0, tiled=True),
    )
    total_pairs = gathered.shape[0]
    row_start = (lax.axis_index("blk") * lax.axis_size("grp") + lax.axis_index("grp")) * pairs_here
    row_ids = row_start + jnp.arange(pairs_here)
    diagonal = row_ids[:, None] == jnp.arange(total_pairs)[None, :]
    allowed = (live_cols[None, :] > 0) & ((false_neg == 0) | diagonal)
    query_scores = (
        jnp.einsum("pd,jd->pj", own_embed[:, 0], gathered[:, 1], preferred_element_type=jnp.float32)
        / logit_divisor_constant
    )
    doc_scores = (
        jnp.einsum("pd,jd->pj", own_embed[:, 1], gathered[:, 0], preferred_element_type=jnp.float32)
        / logit_divisor_constant
    )
    query_lse, query_probs = masked_softmax(query_scores, allowed)
    doc_lse, doc_probs = masked_softmax(doc_scores, allowed)
    own_diag = jnp.sum(jnp.where(diagonal, query_scores, 0.0), -1)
    own_valid = valid.astype(jnp.float32)
    pair_count = jnp.maximum(jnp.sum(live_cols.astype(jnp.float32)), 1.0)
    loss_part = jnp.sum(own_valid * (query_lse + doc_lse - 2.0 * own_diag)) / 2.0
    row_weight = own_valid / (2.0 * pair_count)
    identity_mask = diagonal.astype(jnp.float32)
    query_score_gradient = row_weight[:, None] * (query_probs - identity_mask)
    document_score_gradient = row_weight[:, None] * (doc_probs - identity_mask)
    column_floats = gathered.astype(jnp.float32)
    matched_floats = own_embed.astype(jnp.float32)
    matched_query_gradient = (
        jnp.dot(query_score_gradient, column_floats[:, 1], precision=finest_arithmetic)
        / logit_divisor_constant
    )
    matched_document_gradient = (
        jnp.dot(document_score_gradient, column_floats[:, 0], precision=finest_arithmetic)
        / logit_divisor_constant
    )
    to_doc = (
        jnp.einsum(
            "hk,hy->ky", query_score_gradient, matched_floats[:, 0], precision=finest_arithmetic
        )
        / logit_divisor_constant
    )
    to_query = (
        jnp.einsum(
            "hk,hy->ky", document_score_gradient, matched_floats[:, 1], precision=finest_arithmetic
        )
        / logit_divisor_constant
    )
    returned = lax.psum_scatter(
        jnp.stack([to_query, to_doc], 1), ("blk", "grp"), scatter_dimension=0, tiled=True
    )
    embed_grad = jnp.stack([matched_query_gradient, matched_document_gradient], 1) + returned
    (final_grad,) = pool_back(embed_grad.reshape(seq_count, width))
    third_input_grad, third_gain_grad, third_shift_grad = third_back(final_grad)
    lowered_grad = third_input_grad.astype(jnp.bfloat16)
    down_bias_grad = jnp.sum(lowered_grad.astype(jnp.float32), 0)
    down_grad = contract_rows(activated_low, lowered_grad)
    (lifted_grad,) = gelu_back(contract_cols(lowered_grad, down_weight))
    lifted_low = lifted_grad.astype(jnp.bfloat16)
    up_bias_grad = jnp.sum(lifted_low.astype(jnp.float32), 0)
    up_grad = contract_rows(middle_low, lifted_low)
    middle_grad = third_input_grad + contract_cols(lifted_low, up_weight)
    second_input_grad, second_gain_grad, second_shift_grad = second_back(middle_grad)
    branch_grad = second_input_grad.astype(jnp.bfloat16)
    out_bias_grad = jnp.sum(branch_grad.astype(jnp.float32), 0)
    out_grad = contract_rows(attended, branch_grad)
    attended_grad = contract_cols(branch_grad, out_weight).astype(jnp.bfloat16).reshape(shape)
    probs = jnp.exp(masked_logits() - log_total)
    probs_low = probs.astype(jnp.bfloat16)
    probs_grad = jnp.einsum(
        "sqhe,skhe->shqk", attended_grad, values, preferred_element_type=jnp.float32
    )
    values_grad = jnp.einsum(
        "shqk,sqhe->skhe", probs_low, attended_grad, preferred_element_type=jnp.float32
    )
    logits_grad = probs * (probs_grad - jnp.sum(probs * probs_grad, -1, keepdims=True)) * scale
    query_grad = jnp.einsum(
        "shqk,skhe->sqhe", logits_grad, keys.astype(jnp.float32), precision=finest_arithmetic
    )
    keys_grad = jnp.einsum(
        "shqk,sqhe->skhe", logits_grad, query.astype(jnp.float32), precision=finest_arithmetic
    )
    projected_grad = jnp.concatenate(
        [
            query_grad.reshape(-1, width),
            keys_grad.reshape(-1, width),
            values_grad.reshape(-1, width),
        ],
        1,
    ).astype(jnp.bfloat16)
    qkv_bias_grad = jnp.sum(projected_grad.astype(jnp.float32), 0)
    qkv_grad = contract_rows(normed_low, projected_grad)
    normed_grad = second_input_grad + contract_cols(projected_grad, qkv_weight)
    embedded_grad, first_gain_grad, first_shift_grad = first_back(
        normed_grad.reshape(seq_count, seq_len, width)
    )
    position_grad = jnp.sum(embedded_grad, 0)
    token_grads = embedded_grad.reshape(-1, width)
    vector_grads = jnp.stack(
        [
            first_gain_grad,
            first_shift_grad,
            qkv_bias_grad[:width],
            qkv_bias_grad[2 * width :],
            out_bias_grad,
            second_gain_grad,
            second_shift_grad,
            down_bias_grad,
            third_gain_grad,
            third_shift_grad,
        ]
    )
    small_grad = jnp.concatenate([position_grad, vector_grads, up_bias_grad.reshape(-1, width)], 0)
    table_rows = word_whole.shape[0]
    small_total, loss_total = lax.psum((small_grad, loss_part), ("blk", "grp"))
    shards = reduce_matrices(
        flat_ids, token_grads, table_rows, qkv_grad, out_grad, up_grad, down_grad
    )
    local_squares = jnp.sum(jnp.stack([jnp.sum(shard * shard) for shard in shards]))
    matrix_squares = lax.psum(local_squares, "blk")
    grad_norm = jnp.sqrt(matrix_squares + jnp.sum(small_total * small_total))
    factor = clip_bound / jnp.maximum(grad_norm, clip_bound)
    grads = tuple(shards) + (small_total,)
    parameter_replicas_full = (
        word_master,
        qkv_master,
        out_master,
        up_master,
        down_master,
        small_rows,
    )
    moments = (word_moments, qkv_moments, out_moments, up_moments, down_moments, small_moments)
    results = []
    for grad, moment, master, rate in zip(grads, moments, parameter_replicas_full, rate_table):
        first, second, updated = adam_update(grad * factor, moment, master, rate)
        results.append(first)
        results.append(second)
        results.append(updated)
    return (
        loss_total,
        pair_count,
        grad_norm,
        results[0],
        results[1],
        results[2],
        results[3],
        results[4],
        results[5],
        results[6],
        results[7],
        results[8],
        results[9],
        results[10],
        results[11],
        results[12],
        results[13],
        results[14],
        results[15],
        results[16],
        results[17],
    )


def solution(mesh):
    in_specs = (
        P(("blk", "grp"), None, None),
        P(("blk", "grp"), None),
        P(("blk", "grp")),
        P(("blk", "grp"), None),
        P("grp", None),
        P(),
        P(),
        P(),
        P(),
        P("blk", None),
        P("blk", None),
        P("blk", None),
        P("blk", None),
        P("blk", None),
        P(None, "blk", None),
        P(None, "blk", None),
        P(None, "blk", None),
        P(None, "blk", None),
        P(None, "blk", None),
        P(),
        P(),
    )
    out_specs = (
        P(),
        P(),
        P(),
        P("blk", None),
        P("blk", None),
        P("blk", None),
        P("blk", None),
        P("blk", None),
        P("blk", None),
        P("blk", None),
        P("blk", None),
        P("blk", None),
        P("blk", None),
        P("blk", None),
        P("blk", None),
        P("blk", None),
        P("blk", None),
        P("blk", None),
        P(),
        P(),
        P(),
    )
    return jax.shard_map(
        on_device, mesh=mesh, in_specs=in_specs, out_specs=out_specs, check_vma=False
    )
```

profile of v0, /device:TPU:0, one launch (start us, length us, event | category | flops | bytes accessed | tf_op | source)
XLA Modules:
  0.0 2180.4 jit_solution(2802323078133134552)
XLA Ops:
  16.1 42.3 %all-reduce = s32[128]{0:T(128)S(1)} all-reduce(s32[128]{0:T(128)S(1)} %dynamic-update-slice), channel_id=1, replica_groups=mesh['blk'=8,'grp'=4] {'blk','grp'}, use_global_device_ids=true, to_apply=%add | all-reduce | flops 128 | bytes 1024
  65.7 226.7 %all-gather.3.cloned.1.call-done = bf16[30720,768]{1,0:T(8,128)(2,1)} async-done(((bf16[7680,768]{1,0:T(8,128)(2,1)}), bf16[30720,768]{1,0:T(8,128)(2,1)}) %all-gather.3.cloned.1.call-update) | async-done | bytes 47185936 | tf_op jit(solution)/shard_map/all_gather | solution.py:112
  292.5 18.8 gather_fusion
  346.5 4.9 fusion.25
  357.7 35.6 %multiply_convert_fusion = (bf16[1024,3072]{1,0:T(8,128)(2,1)S(1)}, f32[1024,3072]{1,0:T(8,128)}, f32[1024,3072]{1,0:T(8,128)}) fusion(f32[3072]{0:T(1024)S(1)} %copy-done.77, bf16[768,3072]{1,0:T(8,128)(2,1)S(1)} %bitcast.235, f32[1024,768]{1,0:T(8,128)S(1)} %get-tuple-element.108, f32[768]{0:T(1024)S(1)} %copy-done.48, f32[768]{0:T(1024)S(1)} %get-tuple-element.32, ...), kind=kOutput, calls=%fused_computation.8 | convolution fusion | flops 5043388416 | bytes 39348224 | tf_op jit(solution)/shard_map/dot_general | solution.py:155
  393.3 5.5 fusion.105
  409.3 41.7 %all_gather.17 = bf16[128,2,768]{2,1,0:T(2,128)(2,1)S(1)} all-gather(bf16[4,2,768]{2,1,0:T(2,128)(2,1)S(1)} %copy.123), channel_id=1, replica_groups=mesh['blk'=8,'grp'=4] {'blk','grp'}, dimensions={0}, use_global_device_ids=true | all-gather | bytes 405504 | tf_op jit(solution)/shard_map/all_gather | solution.py:167
  462.4 121.4 %all-reduce.9.cloned.1.call-done = f32[128,2,768]{2,0,1:T(8,128)} async-done(((f32[128,2,768]{2,0,1:T(8,128)}), f32[128,2,768]{2,0,1:T(8,128)}) %all-reduce.9.cloned.1.call-update) | async-done | bytes 786448
  601.2 18.8 convert_reduce_fusion
  620.1 10.6 multiply_reduce_fusion.3
  643.2 5.3 fusion.26
  651.8 6.8 fusion.28
  658.6 4.8 fusion.27
  670.2 6.0 multiply_reduce_fusion.4
  680.5 4.7 fusion.22
  685.5 10.2 fusion.107
  695.8 11.0 fusion.85
  706.9 9.9 fusion.108
  717.5 36.5 %all_gather.18 = f32[8192]{0:T(1024)S(1)} all-gather(f32[1024]{0:T(1024)S(1)} %bitcast.229), channel_id=1, replica_groups=mesh['blk'=8,'grp'=4] {'blk'}, dimensions={0}, use_global_device_ids=true | all-gather | bytes 36864 | tf_op jit(solution)/shard_map/all_gather | solution.py:71
  754.7 406.0 %all-gather.5.cloned.1.call-done = f32[8192,768]{1,0:T(8,128)} async-done(((f32[1024,768]{1,0:T(8,128)}), f32[8192,768]{1,0:T(8,128)}) %all-gather.5.cloned.1.call-update) | async-done | bytes 25165840 | tf_op jit(solution)/shard_map/all_gather | solution.py:72
  1160.7 58.8 %scatter_custom_fusion = f32[3840,768]{1,0:T(8,128)} fusion(s32[8192]{0:T(1024)} %compare_select_fusion, f32[8192,768]{1,0:T(8,128)} %all-gather.5.cloned.1.call-done, f32[]{:T(128)} %constant.58.clone.1), kind=kCustom, calls=%fused_computation.32 | custom fusion | flops 6291456 | bytes 11796992 | tf_op jit(solution)/shard_map/scatter-add | solution.py:78
  1219.5 14.1 reduce-scatter.8.cloned.1.call-done
  1233.6 132.0 %reduce-scatter.6.cloned.1.call-done = f32[96,2304]{1,0:T(8,128)} async-done(((f32[768,2304]{1,0:T(8,128)}), f32[96,2304]{1,0:T(8,128)}) %reduce-scatter.6.cloned.1.call-update) | async-done | bytes 884752 | tf_op jit(solution)/shard_map/reduce_scatter | solution.py:81
  1365.7 166.6 %reduce-scatter.10.cloned.1.call-done = f32[96,3072]{1,0:T(8,128)} async-done(((f32[768,3072]{1,0:T(8,128)}), f32[96,3072]{1,0:T(8,128)}) %reduce-scatter.10.cloned.1.call-update) | async-done | bytes 1179664 | tf_op jit(solution)/shard_map/reduce_scatter | solution.py:83
  1532.2 166.7 %reduce-scatter.12.cloned.1.call-done = f32[384,768]{1,0:T(8,128)} async-done(((f32[3072,768]{1,0:T(8,128)}), f32[384,768]{1,0:T(8,128)}) %reduce-scatter.12.cloned.1.call-update) | async-done | bytes 1179664 | tf_op jit(solution)/shard_map/reduce_scatter | solution.py:84
  1703.1 40.2 %psum.56 = f32[]{:T(128)} all-reduce(f32[]{:T(128)S(6)} %div.202), channel_id=1, replica_groups=mesh['blk'=8,'grp'=4] {'blk','grp'}, use_global_device_ids=true, to_apply=%region_16.17 | all-reduce | flops 1 | bytes 8 | tf_op jit(solution)/shard_map/psum | solution.py:281
  1766.5 202.7 %all-reduce.11.cloned.1.call-done = (f32[3840,768]{1,0:T(8,128)}, f32[96,2304]{1,0:T(8,128)}, f32[96,768]{1,0:T(8,128)}, f32[96,3072]{1,0:T(8,128)}, f32[384,768]{1,0:T(8,128)}) async-done(((f32[3840,768]{1,0:T(8,128)}, f32[96,2304]{1,0:T(8,128)}, f32[96,768]{1,0:T(8,128)}, f32[96,3072]{1,0:T(8,128)}, f32[384,768]{1,0:T(8,128)}), (f32[3840,768]{1,0:T(8,128)}, f32[96,2304]{1,0:T(8,128)}, ...) | async-done | bytes 15335440 | tf_op jit(solution)/shard_map/psum | solution.py:86
  1969.2 8.1 multiply_reduce_fusion
  1986.2 115.9 %all-reduce.7.cloned.1.call-done = f32[142,768]{1,0:T(8,128)} async-done(((f32[142,768]{1,0:T(8,128)}), f32[142,768]{1,0:T(8,128)}) %all-reduce.7.cloned.1.call-update) | async-done | bytes 436240 | tf_op jit(solution)/shard_map/psum | solution.py:281
  2103.8 22.9 %psum.62 = f32[]{:T(128)} all-reduce(f32[]{:T(128)S(6)} %reduce_sum.457), channel_id=1, replica_groups=mesh['blk'=8,'grp'=4] {'blk'}, use_global_device_ids=true, to_apply=%region_42.43 | all-reduce | flops 1 | bytes 8 | tf_op jit(solution)/shard_map/psum | solution.py:286
  2128.2 4.9 multiply_subtract_fusion.1
  2138.8 29.9 %multiply_subtract_fusion = (f32[3840,768]{1,0:T(8,128)}, f32[3840,768]{1,0:T(8,128)}, f32[3840,768]{1,0:T(8,128)}) fusion(f32[3840,768]{1,0:T(8,128)} %param.30, f32[3840,768]{1,0:T(8,128)} %get-tuple-element.42, f32[]{:T(128)S(6)} %div.227, f32[2,3840,768]{2,1,0:T(8,128)} %param.35), kind=kLoop, calls=%fused_computation.23 | loop fusion | flops 44236800 | bytes 82575360 | tf_op jit(solution)/shard_map/sub | solution.py:55
  (346 shorter events, 166.2 us)
Async XLA Ops:
  7.2 312.6 %copy-start = (bf16[768,2304]{1,0:T(8,128)(2,1)S(1)}, bf16[768,2304]{1,0:T(8,128)(2,1)}, u32[]{:S(2)}) copy-start(bf16[768,2304]{1,0:T(8,128)(2,1)} %param.26) | copy-start | bytes 10616836
  7.2 285.3 %all-gather.3.cloned.1.call-start = ((), (), s32[]{:S(2)}) async-start(), calls=%async_computation.4 | async-start | bytes 58982400 | tf_op jit(solution)/shard_map/all_gather | solution.py:112
  7.9 575.9 %all-reduce.9.cloned.1.call-start = ((), (), s32[]{:S(2)}) async-start(), calls=%async_computation.11 | async-start | bytes 1572864
  61.9 290.8 %copy-start.42 = (f32[768]{0:T(1024)}, f32[768]{0:T(1024)S(1)}, u32[]{:S(2)}) copy-start(f32[768]{0:T(1024)S(1)} %get-tuple-element.37) | copy-start | bytes 9220
  315.6 37.1 %copy-start.46 = (f32[1024]{0:T(1024)}, f32[1024]{0:T(1024)S(1)}, u32[]{:S(2)}) copy-start(f32[1024]{0:T(1024)S(1)} %bitcast_rsqrt_fusion) | copy-start | bytes 12292
  346.5 6.3 copy-start.89
  346.5 6.3 copy-start.93
  353.4 39.9 %slice-start.2 = ((s8[4718592]{0:T(1024)(128)(4,1)}), s8[4194304]{0:T(1024)(128)(4,1)S(1)}, s32[]{:S(2)}) async-start(s8[4718592]{0:T(1024)(128)(4,1)} %bitcast.232), calls=%async_computation.15 | async-start | bytes 8388608
  355.3 37.9 %copy-start.6 = (f32[1024,768]{1,0:T(8,128)}, f32[1024,768]{1,0:T(8,128)S(1)}, u32[]{:S(2)}) copy-start(f32[1024,768]{1,0:T(8,128)S(1)} %get-tuple-element.108) | copy-start | bytes 9437188
  357.7 35.6 %copy-start.88 = (f32[768]{0:T(1024)S(1)}, f32[768]{0:T(1024)}, u32[]{:S(2)}) copy-start(f32[768]{0:T(1024)} %get-tuple-element.30) | copy-start | bytes 9220
  357.7 35.6 %slice-start.3 = ((s8[4718592]{0:T(1024)(128)(4,1)}), s8[524288]{0:T(1024)(128)(4,1)S(1)}, s32[]{:S(2)}) async-start(s8[4718592]{0:T(1024)(128)(4,1)} %bitcast.232), calls=%async_computation.16 | async-start | bytes 1048576
  458.5 702.1 %all-gather.5.cloned.1.call-start = ((), (), s32[]{:S(2)}) async-start(), calls=%async_computation.5 | async-start | bytes 28311552 | tf_op jit(solution)/shard_map/all_gather | solution.py:72
  601.2 18.8 copy-start.7
  620.1 10.6 copy-start.62
  632.2 6.3 copy-start.59
  641.1 7.3 slice-start
  651.8 6.8 copy-start.19
  670.1 6.1 copy-start.12
  680.5 553.2 %reduce-scatter.8.cloned.1.call-start = ((), (), s32[]{:S(2)}) async-start(), calls=%async_computation.7 | async-start | bytes 2654208 | tf_op jit(solution)/shard_map/reduce_scatter | solution.py:82
  685.3 680.4 %reduce-scatter.6.cloned.1.call-start = ((), (), s32[]{:S(2)}) async-start(), calls=%async_computation.6 | async-start | bytes 7962624 | tf_op jit(solution)/shard_map/reduce_scatter | solution.py:81
  695.8 836.5 %reduce-scatter.10.cloned.1.call-start = ((), (), s32[]{:S(2)}) async-start(), calls=%async_computation.8 | async-start | bytes 10616832 | tf_op jit(solution)/shard_map/reduce_scatter | solution.py:83
  706.9 992.1 %reduce-scatter.12.cloned.1.call-start = ((), (), s32[]{:S(2)}) async-start(), calls=%async_computation.9 | async-start | bytes 10616832 | tf_op jit(solution)/shard_map/reduce_scatter | solution.py:84
  716.9 1252.4 %all-reduce.11.cloned.1.call-start = ((), (), s32[]{:S(2)}) async-start(), calls=%async_computation.12 | async-start | bytes 30670848 | tf_op jit(solution)/shard_map/psum | solution.py:86
  1699.0 403.1 %all-reduce.7.cloned.1.call-start = ((), (), s32[]{:S(2)}) async-start(), calls=%async_computation.10 | async-start | bytes 884736 | tf_op jit(solution)/shard_map/psum | solution.py:281
  1699.7 57.5 %copy-start.55 = (f32[8,128]{1,0:T(8,128)S(1)}, f32[8,128]{1,0:T(8,128)}, u32[]{:S(2)}) copy-start(f32[8,128]{1,0:T(8,128)} %copy-done.53) | copy-start | bytes 12292
  1699.7 57.5 %copy-start.66 = (f32[1024]{0:T(1024)S(1)}, f32[1024]{0:T(1024)}, u32[]{:S(2)}) copy-start(f32[1024]{0:T(1024)} %copy-done.65) | copy-start | bytes 12292
  1699.8 57.5 %copy-start.57 = (f32[8,128]{1,0:T(8,128)S(1)}, f32[8,128]{1,0:T(8,128)}, u32[]{:S(2)}) copy-start(f32[8,128]{1,0:T(8,128)} %copy-done.56) | copy-start | bytes 12292
  1743.2 6.8 copy-start.73
  1743.2 7.4 copy-start.91
  1743.3 7.9 copy-start.90
  1969.2 8.1 copy-start.24
  1969.2 9.0 copy-start.22
  (80 other events, 243.5 us)
Sparse Core Ops, SparseCore 0:
  9.6 282.7 all-gather.2
  458.6 125.1 all-reduce.8
  680.6 480.0 all-gather.4
  1164.4 69.1 reduce-scatter.7
  1237.6 128.0 reduce-scatter.5
  1369.7 162.5 reduce-scatter.9
  1536.4 162.5 reduce-scatter.11
  1702.5 266.7 all-reduce.10
  1976.0 126.0 all-reduce.6
where the time goes:
time: 2190 us; the launch traced here: 2180 us
  waiting for transfers between devices  1550 us (71%)
  blocking collectives  184 us (8%)
  other arithmetic  168 us (8%)
  matrix products  155 us (7%)
  local copies, waits for them, and re-layouts  96.1 us (4%)
  between operations  23.6 us (1%)
    all_gather x1, waiting for transfers between devices, reduce_matrices(): grad_rows = lax.all_gather(token_grads, 'blk', axis=0, tiled=True)  406 us
    all_gather x1, waiting for transfers between devices, on_device(): word_whole = lax.all_gather(word_table, 'grp', axis=0, tiled=True)  227 us
    psum x1, waiting for transfers between devices, reduce_matrices(): return lax.psum((word_rows, qkv_rows, out_rows, up_rows, down_rows), 'grp')  203 us
    reduce_scatter x1, waiting for transfers between devices, reduce_matrices(): lax.psum_scatter(down_grad, 'blk', scatter_dimension=0, tiled=True)  167 us
    reduce_scatter x1, waiting for transfers between devices, reduce_matrices(): lax.psum_scatter(up_grad, 'blk', scatter_dimension=0, tiled=True)  167 us
    reduce_scatter x1, waiting for transfers between devices, reduce_matrices(): lax.psum_scatter(qkv_grad, 'blk', scatter_dimension=0, tiled=True)  132 us
    unnamed x10, waiting for transfers between devices  122 us
    psum x1, waiting for transfers between devices, on_device(): small_total, loss_total = lax.psum((small_grad, loss_part), ('blk', 'grp'))  116 us
  transfers between devices with their start and end apart: 9, of which 9 were waited for; matrix products, arithmetic and copies ran while one was open for 7% of the time, Pallas kernels for 0%

commit v1 on v0

v1 whole, which is shorter than its diff:
```python
import jax
import jax.numpy as jnp
from jax import lax
from jax.sharding import PartitionSpec as P

HEADS = 12
STEP = 5


logit_divisor_constant = 0.01
clip_bound = 0.001
beta_first = 0.5
beta_second = 0.5
decay_weight = 0.01
epsilon = 1e-08
rate_table = (0.1, 0.02, 0.1, 0.02, 0.01, 0.2)
finest_arithmetic = lax.Precision.HIGHEST
both = ("blk", "grp")
strip = 384


def layer_norm(states, gain, shift):
    mean = jnp.mean(states, -1, keepdims=True)
    centered = states - mean
    variance = jnp.mean(centered * centered, -1, keepdims=True)
    return centered * lax.rsqrt(variance + 1e-06) * gain + shift


def exact_gelu(values):
    return jax.nn.gelu(values, approximate=False)


def pool_unit(states, lengths_flat):
    positions = jnp.arange(states.shape[1])
    weights = (positions[None, :] < lengths_flat[:, None]).astype(jnp.float32)
    pooled = jnp.sum(states * weights[:, :, None], 1) / lengths_flat[:, None].astype(jnp.float32)
    return pooled * lax.rsqrt(jnp.sum(pooled * pooled, -1, keepdims=True) + 1e-06)


def contract_rows(left, right):
    return lax.dot_general(
        left, right, (((0,), (0,)), ((), ())), preferred_element_type=jnp.float32
    )


def contract_cols(left, right):
    return lax.dot_general(
        left, right, (((1,), (1,)), ((), ())), preferred_element_type=jnp.float32
    )


def adam_update(grad, moments, master, rate):
    first = beta_first * moments[0] + (1.0 - beta_first) * grad
    second = beta_second * moments[1] + (1.0 - beta_second) * grad * grad
    first_hat = first / (1.0 - beta_first**STEP)
    second_hat = second / (1.0 - beta_second**STEP)
    updated = master - rate * (first_hat / (jnp.sqrt(second_hat) + epsilon) + decay_weight * master)
    return (first, second, updated)


def masked_softmax(pairwise_affinity_matrix, allowed):
    masked = jnp.where(allowed, pairwise_affinity_matrix, -1000000000.0)
    top = jnp.max(masked, -1, keepdims=True)
    expo = jnp.where(allowed, jnp.exp(masked - top), 0.0)
    total = jnp.sum(expo, -1, keepdims=True)
    return (top[:, 0] + jnp.log(total[:, 0]), expo / total)


class Place:
    def __init__(self):
        self.blk, self.grp = lax.axis_size("blk"), lax.axis_size("grp")
        self.count = self.blk * self.grp
        self.b, self.g = lax.axis_index("blk"), lax.axis_index("grp")
        self.xs, self.far = self.grp // 2, self.blk // 2
        self.core, self.x = self.g % 2, self.g // 2
        self.y, self.z = self.b % 2, self.b // 2
        self.core_masks = [0, 1]
        self.x_masks = [2 * i for i in range(self.xs)]
        self.y_masks = [0, self.grp]
        self.z_masks = [2 * self.grp * i for i in range(self.far)]

    def send(self, value, mask):
        pairs = [(i, i ^ mask) for i in range(self.count)]
        return lax.ppermute(value, both, pairs)


def in_order(pieces, index):
    step = 1
    while step < len(pieces):
        odd = (index & step) != 0
        pieces = [jnp.where(odd, pieces[i ^ step], pieces[i]) for i in range(len(pieces))]
        step *= 2
    return pieces


def gather_stage(place, value, masks, index):
    pieces = [value] + [place.send(value, mask) for mask in masks[1:]]
    return jnp.stack(in_order(pieces, index))


def gather_far_first(place, value):
    shape = value.shape
    value = gather_stage(place, value, place.z_masks, place.z)
    middle = [a + b for a in place.y_masks for b in place.x_masks]
    value = gather_stage(place, value, middle, place.y * place.xs + place.x)
    value = gather_stage(place, value, place.core_masks, place.core)
    value = value.reshape((2, 2, place.xs, place.far) + shape)
    return jnp.transpose(value, (3, 1, 2, 0) + tuple(range(4, 4 + len(shape)))).reshape(
        (place.blk, place.grp) + shape
    )


def reduce_stage(place, value, masks, index):
    total = lax.dynamic_index_in_dim(value, index, 0, keepdims=False)
    arrived = [
        place.send(lax.dynamic_index_in_dim(value, index ^ k, 0, keepdims=False), masks[k])
        for k in range(1, len(masks))
    ]
    terms = [total.astype(jnp.float32)] + [a.astype(jnp.float32) for a in arrived]
    while len(terms) > 1:
        terms = [terms[i] + terms[i + 1] for i in range(0, len(terms), 2)]
    return terms[0]


def reduce_rest(place, value, x_first):
    rows = value.shape[2]
    value = value.reshape(place.far, 2, place.xs, rows, value.shape[3])
    low = jnp.bfloat16
    if x_first:
        value = reduce_stage(
            place, jnp.moveaxis(value, 2, 0), place.x_masks, place.x
        ).astype(low)
        value = reduce_stage(
            place, jnp.moveaxis(value, 1, 0), place.y_masks, place.y
        ).astype(low)
    else:
        value = reduce_stage(
            place, jnp.moveaxis(value, 1, 0), place.y_masks, place.y
        ).astype(low)
        value = reduce_stage(
            place, jnp.moveaxis(value, 1, 0), place.x_masks, place.x
        ).astype(low)
    return reduce_stage(place, value, place.z_masks, place.z)


def half_gradient(place, left, right, core):
    width = right.shape[1] // 2
    part = lax.dynamic_slice_in_dim(right, core * width, width, 1)
    grad = contract_rows(left, part).astype(jnp.bfloat16)
    rows = grad.shape[0] // place.blk // place.xs
    strips = width // strip
    grad = grad.reshape(place.blk, place.xs, rows, strips, strip)
    return jnp.transpose(grad, (0, 1, 3, 2, 4)).reshape(
        place.blk, place.xs, strips * rows, strip
    )


def reduce_group(place, pairs, extra):
    mine = [half_gradient(place, a, b, place.core) for a, b in pairs]
    theirs = [half_gradient(place, a, b, 1 - place.core) for a, b in pairs]
    for item in extra:
        mine.append(lax.dynamic_index_in_dim(item, place.core, 2, keepdims=False))
        theirs.append(lax.dynamic_index_in_dim(item, 1 - place.core, 2, keepdims=False))
    mine, theirs = jnp.concatenate(mine, 2), jnp.concatenate(theirs, 2)
    arrived = place.send(theirs, 1)
    value = (mine.astype(jnp.float32) + arrived.astype(jnp.float32)).astype(jnp.bfloat16)
    cut = value.shape[2] // 32 * 16
    return jnp.concatenate(
        [
            reduce_rest(place, value[:, :, :cut], True),
            reduce_rest(place, value[:, :, cut:], False),
        ]
    )


def whole_rows(place, pieces, rows, width):
    strips = width // 2 // strip
    pieces = pieces.reshape(place.xs, 2, strips, rows, strip)
    return jnp.transpose(pieces, (0, 3, 1, 2, 4)).reshape(place.xs * rows, width)


def on_device(
    token_ids,
    lengths,
    valid,
    false_neg,
    word_table,
    qkv_weight,
    out_weight,
    up_weight,
    down_weight,
    word_master,
    qkv_master,
    out_master,
    up_master,
    down_master,
    word_moments,
    qkv_moments,
    out_moments,
    up_moments,
    down_moments,
    small_rows,
    small_moments,
):
    place = Place()
    pairs_here = token_ids.shape[0]
    total_pairs = pairs_here * place.count
    seq_count = 2 * pairs_here
    seq_len = token_ids.shape[2]
    width = word_table.shape[1]
    head_dim = width // HEADS
    scale = head_dim ** (-0.5)
    flat_ids = token_ids.reshape(-1)
    tokens = flat_ids.shape[0]
    lengths_flat = lengths.reshape(-1)
    vectors = small_rows[seq_len:]

    shard_rows = word_master.shape[0]
    table_rows = word_table.shape[0]
    per_owner = table_rows // shard_rows
    room = max(16, tokens // place.blk)
    shard = flat_ids // shard_rows
    same_id = flat_ids[:, None] == flat_ids[None, :]
    before = jnp.arange(tokens)[:, None] < jnp.arange(tokens)[None, :]
    first = ~jnp.any(same_id & before, 0)
    smaller = (
        (shard[:, None] == shard[None, :])
        & (flat_ids[None, :] < flat_ids[:, None])
        & first[None, :]
    )
    rank = jnp.sum(smaller.astype(jnp.int32), 1)
    slots = place.blk * room

    def slot_ids_of(round_number):
        at = rank - round_number * room
        slot = jnp.where((at >= 0) & (at < room), shard * room + at, slots)
        hit = slot[None, :] == jnp.arange(slots)[:, None]
        return jnp.max(jnp.where(hit, flat_ids[None, :], -1), 1)

    def lookup_slots(round_number):
        at = rank - round_number * room
        owner = shard // per_owner
        relative = ((owner ^ place.g) * per_owner + shard % per_owner) * room + at
        return jnp.where((at >= 0) & (at < room), relative, slots)

    def gradient_slots(round_number):
        at = rank - round_number * room
        relative = (shard ^ place.b) * room + at
        return jnp.where((at >= 0) & (at < room), relative, slots)

    def fetch(grp_ids, round_number):
        span = per_owner * room
        asked = [lax.dynamic_slice_in_dim(ids, place.g * span, span) for ids in grp_ids]
        local = jnp.concatenate(asked) - place.g * table_rows
        found = word_table.at[jnp.clip(local, 0, table_rows - 1)].get(mode="clip")
        parts = [found[k * span : (k + 1) * span] for k in range(place.grp)]
        rows = [parts[0]] + [place.send(parts[k], k) for k in range(1, place.grp)]
        rows = jnp.concatenate(rows)
        pick = lookup_slots(round_number)[:, None] == jnp.arange(slots)[None, :]
        return jnp.dot(pick.astype(jnp.bfloat16), rows, preferred_element_type=jnp.float32)

    def pack(values, length):
        return jnp.concatenate([values, jnp.zeros((length - values.shape[0],), values.dtype)])

    slot_ids = slot_ids_of(0)
    early = jnp.concatenate(
        [slot_ids, false_neg.reshape(-1), valid, jnp.max(rank)[None]]
    )
    early = pack(early, -(-early.shape[0] // 1024) * 1024).reshape(-1, 128)
    grp_early = [early] + [place.send(early, k) for k in range(1, place.grp)]
    grp_ids = [item.reshape(-1)[:slots] for item in grp_early]
    looked_up = fetch(grp_ids, 0)
    early_all = jnp.stack(in_order(grp_early, place.g))
    early_all = gather_stage(place, early_all, place.y_masks, place.y)
    early_all = gather_stage(place, early_all, place.z_masks, place.z)
    early_all = early_all.reshape(place.count, -1)
    ids_all = early_all[:, :slots]
    at = slots
    false_neg_all = early_all[:, at : at + pairs_here * total_pairs].reshape(
        total_pairs, total_pairs
    )
    at += pairs_here * total_pairs
    valid_all = early_all[:, at : at + pairs_here].reshape(-1)
    at += pairs_here
    rounds = jnp.max(early_all[:, at]) // room + 1

    def more_lookups(carry):
        number, held = carry
        ids = slot_ids_of(number)
        ids = [ids] + [place.send(ids, k) for k in range(1, place.grp)]
        return (number + 1, held + fetch(ids, number))

    _, looked_up = lax.while_loop(
        lambda carry: carry[0] < rounds, more_lookups, (jnp.int32(1), looked_up)
    )

    embedded = looked_up.reshape(seq_count, seq_len, width) + small_rows[:seq_len]
    normed, first_back = jax.vjp(layer_norm, embedded, vectors[0], vectors[1])
    normed_low = normed.reshape(-1, width).astype(jnp.bfloat16)
    qkv_bias = jnp.concatenate([vectors[2], jnp.zeros((width,), jnp.float32), vectors[3]])
    projected = (
        jnp.dot(normed_low, qkv_weight, preferred_element_type=jnp.float32) + qkv_bias
    ).astype(jnp.bfloat16)
    shape = (seq_count, seq_len, HEADS, head_dim)
    query = projected[:, :width].reshape(shape)
    keys = projected[:, width : 2 * width].reshape(shape)
    values = projected[:, 2 * width :].reshape(shape)
    key_live = (jnp.arange(seq_len)[None, :] < lengths_flat[:, None])[:, None, None, :]

    def masked_logits():
        unnormalized_affinity = (
            jnp.einsum("sqhe,skhe->shqk", query, keys, preferred_element_type=jnp.float32) * scale
        )
        return jnp.where(key_live, unnormalized_affinity, -1000000000.0)

    unnormalized_affinity = masked_logits()
    top = jnp.max(unnormalized_affinity, -1, keepdims=True)
    log_total = top + jnp.log(jnp.sum(jnp.exp(unnormalized_affinity - top), -1, keepdims=True))
    probs_low = jnp.exp(unnormalized_affinity - log_total).astype(jnp.bfloat16)
    attended = jnp.einsum("shqk,skhe->sqhe", probs_low, values, preferred_element_type=jnp.float32)
    attended = attended.reshape(-1, width).astype(jnp.bfloat16)
    branch = jnp.dot(attended, out_weight, preferred_element_type=jnp.float32) + vectors[4]
    middle, second_back = jax.vjp(
        layer_norm, normed.reshape(-1, width) + branch, vectors[5], vectors[6]
    )
    middle_low = middle.astype(jnp.bfloat16)
    lifted = jnp.dot(middle_low, up_weight, preferred_element_type=jnp.float32) + vectors[
        10:14
    ].reshape(-1)
    activated, gelu_back = jax.vjp(exact_gelu, lifted)
    activated_low = activated.astype(jnp.bfloat16)
    lowered = jnp.dot(activated_low, down_weight, preferred_element_type=jnp.float32) + vectors[7]
    final, third_back = jax.vjp(layer_norm, middle + lowered, vectors[8], vectors[9])
    unit, pool_back = jax.vjp(
        lambda states: pool_unit(states.reshape(seq_count, seq_len, width), lengths_flat), final
    )
    own_embed = unit.astype(jnp.bfloat16)

    gathered = gather_far_first(place, own_embed).reshape(total_pairs, 2, width)
    queries, documents = gathered[:, 0], gathered[:, 1]
    diagonal = jnp.arange(total_pairs)[:, None] == jnp.arange(total_pairs)[None, :]
    allowed = (valid_all[None, :] > 0) & ((false_neg_all == 0) | diagonal)
    scores = contract_cols(queries, documents) / logit_divisor_constant
    query_lse, query_probs = masked_softmax(scores, allowed)
    doc_lse, doc_probs = masked_softmax(scores.T, allowed)
    diag = jnp.sum(jnp.where(diagonal, scores, 0.0), -1)
    valid_floats = valid_all.astype(jnp.float32)
    pair_count = jnp.maximum(jnp.sum(valid_floats), 1.0)
    loss_total = jnp.sum(valid_floats * (query_lse + doc_lse - 2.0 * diag)) / 2.0
    row_weight = valid_floats / (2.0 * pair_count)
    identity_mask = diagonal.astype(jnp.float32)
    score_grad = (
        row_weight[:, None] * (query_probs - identity_mask)
        + (row_weight[:, None] * (doc_probs - identity_mask)).T
    )
    row_start = (place.b * place.grp + place.g) * pairs_here
    query_grad_rows = lax.dynamic_slice_in_dim(score_grad, row_start, pairs_here, 0)
    doc_grad_rows = lax.dynamic_slice_in_dim(score_grad, row_start, pairs_here, 1).T
    embed_grad = (
        jnp.stack(
            [
                jnp.dot(
                    query_grad_rows, documents.astype(jnp.float32), precision=finest_arithmetic
                ),
                jnp.dot(doc_grad_rows, queries.astype(jnp.float32), precision=finest_arithmetic),
            ],
            1,
        )
        / logit_divisor_constant
    )

    (final_grad,) = pool_back(embed_grad.reshape(seq_count, width))
    third_input_grad, third_gain_grad, third_shift_grad = third_back(final_grad)
    lowered_grad = third_input_grad.astype(jnp.bfloat16)
    down_bias_grad = jnp.sum(lowered_grad.astype(jnp.float32), 0)
    (lifted_grad,) = gelu_back(contract_cols(lowered_grad, down_weight))
    lifted_low = lifted_grad.astype(jnp.bfloat16)
    up_bias_grad = jnp.sum(lifted_low.astype(jnp.float32), 0)
    group_one = reduce_group(
        place, [(activated_low, lowered_grad), (middle_low, lifted_low)], []
    )
    middle_grad = third_input_grad + contract_cols(lifted_low, up_weight)
    second_input_grad, second_gain_grad, second_shift_grad = second_back(middle_grad)
    branch_grad = second_input_grad.astype(jnp.bfloat16)
    out_bias_grad = jnp.sum(branch_grad.astype(jnp.float32), 0)
    attended_grad = contract_cols(branch_grad, out_weight).astype(jnp.bfloat16).reshape(shape)
    probs = jnp.exp(masked_logits() - log_total)
    probs_low = probs.astype(jnp.bfloat16)
    probs_grad = jnp.einsum(
        "sqhe,skhe->shqk", attended_grad, values, preferred_element_type=jnp.float32
    )
    values_grad = jnp.einsum(
        "shqk,sqhe->skhe", probs_low, attended_grad, preferred_element_type=jnp.float32
    )
    logits_grad = probs * (probs_grad - jnp.sum(probs * probs_grad, -1, keepdims=True)) * scale
    logits_grad = logits_grad.astype(jnp.bfloat16)
    query_grad = jnp.einsum(
        "shqk,skhe->sqhe", logits_grad, keys, preferred_element_type=jnp.float32
    )
    keys_grad = jnp.einsum(
        "shqk,sqhe->skhe", logits_grad, query, preferred_element_type=jnp.float32
    )
    projected_grad = jnp.concatenate(
        [
            query_grad.reshape(-1, width),
            keys_grad.reshape(-1, width),
            values_grad.reshape(-1, width),
        ],
        1,
    ).astype(jnp.bfloat16)
    qkv_bias_grad = jnp.sum(projected_grad.astype(jnp.float32), 0)
    normed_grad = second_input_grad + contract_cols(projected_grad, qkv_weight)
    embedded_grad, first_gain_grad, first_shift_grad = first_back(
        normed_grad.reshape(seq_count, seq_len, width)
    )
    position_grad = jnp.sum(embedded_grad, 0)
    token_grads = embedded_grad.reshape(-1, width).astype(jnp.bfloat16)

    grid_ids = lax.dynamic_slice_in_dim(
        ids_all.reshape(place.blk, place.grp, place.blk, room), place.b, 1, 2
    )[:, :, 0]

    def word_rows_of(round_number, source_ids, held):
        hit = gradient_slots(round_number)[None, :] == jnp.arange(slots)[:, None]
        rows = jnp.dot(hit.astype(jnp.bfloat16), token_grads, preferred_element_type=jnp.float32)
        rows = rows.astype(jnp.bfloat16).reshape(place.blk, room, width)
        arrived = [rows[0]] + [
            place.send(rows[k], k * place.grp) for k in range(1, place.blk)
        ]
        arrived = jnp.concatenate(arrived)
        arrived = gather_stage(place, arrived, place.x_masks, place.x)
        arrived = gather_stage(place, arrived, place.core_masks, place.core)
        arrived = jnp.swapaxes(arrived, 0, 1).reshape(-1, width)
        ids = jnp.stack(in_order([source_ids[i] for i in range(place.blk)], place.b))
        local = jnp.swapaxes(ids, 0, 1).reshape(-1) - place.b * shard_rows
        inside = (local >= 0) & (local < shard_rows)
        return held.at[jnp.where(inside, local, shard_rows)].add(
            arrived.astype(jnp.float32), mode="drop"
        )

    word_rows = word_rows_of(0, grid_ids, jnp.zeros((shard_rows, width), jnp.float32))

    def more_rows(carry):
        number, held = carry
        ids = gather_far_first(place, slot_ids_of(number).reshape(place.blk, room))
        ids = lax.dynamic_index_in_dim(ids, place.b, 2, keepdims=False)
        return (number + 1, word_rows_of(number, ids, held))

    _, word_rows = lax.while_loop(
        lambda carry: carry[0] < rounds, more_rows, (jnp.int32(1), word_rows)
    )

    vector_grads = jnp.stack(
        [
            first_gain_grad,
            first_shift_grad,
            qkv_bias_grad[:width],
            qkv_bias_grad[2 * width :],
            out_bias_grad,
            second_gain_grad,
            second_shift_grad,
            down_bias_grad,
            third_gain_grad,
            third_shift_grad,
        ]
    )
    small_grad = jnp.concatenate([position_grad, vector_grads, up_bias_grad.reshape(-1, width)], 0)
    small_flat = small_grad.reshape(-1, strip)
    small_piece = -(-small_flat.shape[0] // (16 * place.count)) * 16
    small_padded = jnp.concatenate(
        [
            small_flat,
            jnp.zeros((small_piece * place.count - small_flat.shape[0], strip), jnp.float32),
        ]
    ).astype(jnp.bfloat16)
    small_parts = small_padded.reshape(place.blk, place.xs, 2, small_piece, strip)
    group_two = reduce_group(
        place, [(normed_low, projected_grad), (attended, branch_grad)], [small_parts]
    )
    cut = group_two.shape[0] - small_piece
    small_own = group_two[cut:]
    matrix_own = jnp.concatenate([group_one, group_two[:cut]]).astype(jnp.bfloat16)
    gathered_grads = gather_stage(place, matrix_own, place.x_masks, place.x)
    gathered_grads = gather_stage(place, gathered_grads, place.core_masks, place.core)
    gathered_grads = jnp.swapaxes(gathered_grads, 0, 1)
    masters = (down_master, up_master, qkv_master, out_master)
    shards, at = [], 0
    for master in masters:
        rows, columns = master.shape[0] // place.xs, master.shape[1]
        length = rows * (columns // 2 // strip)
        shards.append(
            whole_rows(place, gathered_grads[:, :, at : at + length], rows, columns).astype(
                jnp.float32
            )
        )
        at += length

    matrix_floats = matrix_own.astype(jnp.float32)
    squares = (
        jnp.sum(matrix_floats * matrix_floats)
        + jnp.sum(small_own * small_own)
        + jnp.sum(word_rows * word_rows) / place.grp
    )
    late = jnp.concatenate([small_own, jnp.full((8, strip), squares)])
    late = gather_far_first(place, late).reshape(place.count, -1, strip)
    small_total = late[:, :small_piece].reshape(-1, strip)[: small_flat.shape[0]]
    small_total = small_total.reshape(small_grad.shape)
    grad_norm = jnp.sqrt(jnp.sum(late[:, small_piece, 0]))
    factor = clip_bound / jnp.maximum(grad_norm, clip_bound)
    down_shard, up_shard, qkv_shard, out_shard = shards
    grads = (word_rows, qkv_shard, out_shard, up_shard, down_shard, small_total)
    parameters = (word_master, qkv_master, out_master, up_master, down_master, small_rows)
    moments = (word_moments, qkv_moments, out_moments, up_moments, down_moments, small_moments)
    results = []
    for grad, moment, master, rate in zip(grads, moments, parameters, rate_table):
        results.extend(adam_update(grad * factor, moment, master, rate))
    return (loss_total, pair_count, grad_norm, *results)


def solution(mesh):
    in_specs = (
        P(both, None, None),
        P(both, None),
        P(both),
        P(both, None),
        P("grp", None),
        P(),
        P(),
        P(),
        P(),
        P("blk", None),
        P("blk", None),
        P("blk", None),
        P("blk", None),
        P("blk", None),
        P(None, "blk", None),
        P(None, "blk", None),
        P(None, "blk", None),
        P(None, "blk", None),
        P(None, "blk", None),
        P(),
        P(),
    )
    out_specs = (P(), P(), P()) + (P("blk", None),) * 15 + (P(), P(), P())
    return jax.shard_map(
        on_device, mesh=mesh, in_specs=in_specs, out_specs=out_specs, check_vma=False
    )
```

time: 2190 us -> 754 us (0.34)
  waiting for transfers between devices: 1550 us -> 126 us
  blocking collectives: 184 us -> 0 us
  starting transfers between devices: 0.58 us -> 81.9 us
  local copies, waits for them, and re-layouts: 96.1 us -> 155 us
    all_gather x2 -> x0, waiting for transfers between devices: 633 us -> none  [the longest x1 406 us: reduce_matrices(): grad_rows = lax.all_gather(token_grads, 'blk', axis=0, tiled=True)]
    reduce_scatter x4 -> x0, waiting for transfers between devices: 479 us -> none  [the longest x1 167 us: reduce_matrices(): lax.psum_scatter(down_grad, 'blk', scatter_dimension=0, tiled=True)]
    psum x2 -> x0, waiting for transfers between devices: 319 us -> none  [the longest x1 203 us: reduce_matrices(): return lax.psum((word_rows, qkv_rows, out_rows, up_rows, down_rows), 'grp')]
    ppermute x0 -> x57, waiting for transfers between devices: none -> 126 us  [send(): return lax.ppermute(value, both, pairs)]
    unnamed x10 -> x0, waiting for transfers between devices: 122 us -> none
    ppermute x0 -> x57, starting transfers between devices: none -> 81.9 us  [send(): return lax.ppermute(value, both, pairs)]
    all_gather x2 -> x0, blocking collectives: 78.2 us -> none  [the longest x1 41.7 us: on_device(): lax.all_gather(own_embed, ('blk', 'grp'), axis=0, tiled=True)]
    psum x2 -> x0, blocking collectives: 63.1 us -> none  [the longest x1 40.2 us: on_device(): small_total, loss_total = lax.psum((small_grad, loss_part), ('blk', 'grp'))]
  transfers between devices with their start and end apart: 9 -> 57, of which waited for: 9 -> 27; matrix products, arithmetic and copies ran while one was open for 7% -> 25% of each run, Pallas kernels for 0% -> 0%
where the time goes in v1:
time: 754 us; the launch traced here: 744 us
  other arithmetic  188 us (25%)
  matrix products  171 us (23%)
  local copies, waits for them, and re-layouts  155 us (21%)
  waiting for transfers between devices  126 us (17%)
  starting transfers between devices  81.9 us (11%)
  between operations  13.2 us (2%)
  loops' own time  9.1 us (1%)
    ppermute x57, waiting for transfers between devices, send(): return lax.ppermute(value, both, pairs)  126 us
    ppermute x57, starting transfers between devices, send(): return lax.ppermute(value, both, pairs)  81.9 us
    unnamed x316, local copies, waits for them, and re-layouts  41.1 us
    sub x6, other arithmetic, adam_update(): master - rate * (first_hat / (jnp.sqrt(second_hat) + epsilon) + decay_wei...  40.5 us
    dot_general x5, matrix products, contract_cols(): lax.dot_general(left, right, (((1,), (1,)), ((), ())), preferred_element_...  38.1 us
    dot_general x8, matrix products, contract_rows(): lax.dot_general(left, right, (((0,), (0,)), ((), ())), preferred_element_...  37.6 us
    dot_general x1, matrix products, on_device(): jnp.dot(middle_low, up_weight, preferred_element_type=jnp.float32)  33.3 us
    scatter-add x1, other arithmetic, word_rows_of(): held.at[jnp.where(inside, local, shard_rows)]  32.8 us
  transfers between devices with their start and end apart: 57, of which 27 were waited for; matrix products, arithmetic and copies ran while one was open for 25% of the time, Pallas kernels for 0%

profile of v1, /device:TPU:0, one launch (start us, length us, event | category | flops | bytes accessed | tf_op | source)
XLA Modules:
  0.0 744.1 jit_solution(16256326543631203372)
XLA Ops:
  38.0 11.4 %gather_fusion.1 = bf16[1024,768]{1,0:T(8,128)(2,1)} fusion(bf16[7680,768]{1,0:T(8,128)(2,1)} %param.29, s32[1024]{0:T(1024)S(1)} %broadcast_clamp_fusion.1), kind=kCustom, calls=%fused_computation.1 | custom fusion | bytes 3149824 | tf_op jit(solution)/shard_map/gather | solution.py:255
  63.8 5.2 collective-permute-done.31
  68.9 8.5 %collective-permute-done.30 = bf16[256,768]{1,0:T(8,128)(2,1)} collective-permute-done((bf16[256,768]{1,0:T(8,128)(2,1)}, bf16[256,768]{1,0:T(8,128)(2,1)}, u32[]{:S(2)}, u32[]{:S(2)}) %collective-permute-start.30) | collective-permute-done | bytes 393248 | tf_op jit(solution)/shard_map/ppermute | solution.py:84
  77.4 5.0 fusion.39
  82.4 8.7 %while.26 = (s32[]{:T(128)}, f32[1024,768]{1,0:T(8,128)}, s32[]{:T(128)}, s32[1024]{0:T(1024)S(1)}, s32[1024,1]{0,1:T(1,128)S(1)}, /*index=5*/s32[1024]{0:T(1024...) while((s32[]{:T(128)}, f32[1024,768]{1,0:T(8,128)}, ...), condition=%wide.region_7.8_spmd, body=%wide.region_5.7_spmd.sunk | while | flops 1621928960 | bytes 19032540 | solution.py:293
  133.5 33.3 %multiply_convert_fusion = (bf16[1024,3072]{1,0:T(8,128)(2,1)S(1)}, f32[1024,3072]{1,0:T(8,128)}, f32[1024,3072]{1,0:T(8,128)}) fusion(f32[3072]{0:T(1024)S(1)} %copy-done.126, bf16[1024,768]{1,0:T(8,128)(2,1)S(1)} %fusion.62, bf16[768,3072]{1,0:T(8,128)(2,1)S(1)} %bitcast.764), kind=kOutput, calls=%fused_computation.120 | convolution fusion | flops 5039456256 | bytes 37761024 | tf_op jit(solution)/shard_map/dot_general | solution.py:327
  166.8 5.5 fusion.231
  238.5 18.8 %fusion.232 = (bf16[3072]{0:T(1024)(128)(2,1)}, bf16[1024,3072]{1,0:T(8,128)(2,1)}) fusion(f32[1024,3072]{1,0:T(8,128)} %get-tuple-element.589, bf16[1024,768]{1,0:T(8,128)(2,1)} %get-tuple-element.579, bf16[3072,768]{1,0:T(8,128)(2,1)} %param.33, f32[1024,3072]{1,0:T(8,128)} %get-tuple-element.747, f32[3072]{0:T(1024)S(1)} %copy-done.127), kind=kOutput, calls=%fused_computation.626 | convolution fusion | flops 4882166784 | bytes 37767168 | tf_op jit(solution)/shard_map/dot_general | solution.py:47
  257.4 10.6 %multiply_reduce_fusion.3 = (bf16[768]{0:T(1024)(128)(2,1)}, f32[1024]{0:T(1024)S(1)}, bf16[768]{0:T(1024)(128)(2,1)}, f32[1024,768]{1,0:T(8,128)S(1)}) fusion(f32[1024,768]{1,0:T(8,128)S(1)} %copy-done.12, f32[1024]{0:T(1024)S(1)} %copy-done.113, f32[1024]{0:T(1024)S(1)} %copy-done.101, f32[768]{0:T(1024)S(1)} %copy-done.110, ...), kind=kOutput, calls=%fused_computation.189 | convolution fusion | flops 4839699456 | bytes 20469760 | tf_op jit(solution)/shard_map/dot_general | solution.py:47
  285.4 13.5 %fusion.92 = bf16[8,128,12,64]{1,3,2,0:T(8,128)(2,1)} fusion(f32[8,12,128,128]{2,3,1,0:T(8,128)} %fusion.98, f32[8,12,128]{2,1,0:T(8,128)} %copy-done.106, f32[8,12,128,128]{2,3,1,0:T(8,128)} %copy-done.27, pred[8,128]{1,0:T(8,128)(4,1)S(1)} %copy-done.139, bf16[8,128,12,64]{1,0,3,2:T(8,128)(2,1)} %bitcast.688), kind=kOutput, calls=%fused_computation.251 | convolution fusion | flops 219426944 | bytes 15778816 | tf_op jit(solution)/shard_map/shqk,skhe->sqhe/dot_general | solution.py:397
  298.9 13.9 %fusion.89 = bf16[8,128,12,64]{1,3,2,0:T(8,128)(2,1)} fusion(f32[8,12,128,128]{2,3,1,0:T(8,128)} %fusion.98, f32[8,12,128]{2,1,0:T(8,128)} %copy-done.106, f32[8,12,128,128]{2,3,1,0:T(8,128)} %copy-done.27, pred[8,128]{1,0:T(8,128)(4,1)S(1)} %copy-done.139, bf16[8,128,12,64]{1,0,3,2:T(8,128)(2,1)} %bitcast.691), kind=kOutput, calls=%fused_computation.250 | convolution fusion | flops 219426944 | bytes 15778816 | tf_op jit(solution)/shard_map/shqk,sqhe->skhe/dot_general | solution.py:400
  312.9 5.8 fusion.96
  325.6 4.8 multiply_reduce_fusion.5
  348.6 5.2 collective-permute-done.62
  357.6 14.0 %collective-permute-done.65 = bf16[128,768]{1,0:T(8,128)(2,1)S(1)} collective-permute-done((bf16[128,768]{1,0:T(8,128)(2,1)S(1)}, bf16[128,768]{1,0:T(8,128)(2,1)S(1)}, u32[]{:S(2)}, u32[]{:S(2)}) %collective-permute-start.65) | collective-permute-done | bytes 196640 | tf_op jit(solution)/shard_map/ppermute | solution.py:84
  372.8 32.1 %collective-permute-done.68 = bf16[1024,768]{1,0:T(8,128)(2,1)} collective-permute-done((bf16[1024,768]{1,0:T(8,128)(2,1)S(1)}, bf16[1024,768]{1,0:T(8,128)(2,1)}, u32[]{:S(2)}, u32[]{:S(2)}) %collective-permute-start.68) | collective-permute-done | bytes 1572896 | tf_op jit(solution)/shard_map/ppermute | solution.py:84
  432.4 5.6 convolution_convert_fusion.4
  446.3 7.9 %convolution_convert_fusion = bf16[3072,384]{1,0:T(8,128)(2,1)} fusion(bf16[1024,3072]{1,0:T(8,128)(2,1)} %copy-done.144, bf16[1024,768]{1,0:T(8,128)(2,1)S(1)} %copy-done.38, s32[]{:T(128)S(6)} %select_n.1934), kind=kOutput, calls=%fused_computation.154 | convolution fusion | flops 2417098752 | bytes 9437188 | tf_op jit(solution)/shard_map/dot_general | solution.py:41
  456.3 5.4 convert_bitcast_fusion.1
  461.7 10.5 %copy.306 = f32[2,2,1024,768]{3,2,1,0:T(8,128)} copy(f32[2,2,1024,768]{3,2,0,1:T(8,128)} %convert_bitcast_fusion.1) | data formatting | bytes 25165824 | tf_op jit(solution)/shard_map/convert_element_type | solution.py:438
  472.2 32.8 %scatter_custom_fusion.1 = f32[3840,768]{1,0:T(8,128)} fusion(s32[4096]{0:T(1024)} %bitcast.737, f32[4096,768]{1,0:T(8,128)} %bitcast.640, f32[]{:T(128)} %constant.466.clone.1), kind=kCustom, calls=%fused_computation.145 | custom fusion | flops 3145728 | bytes 11796992 | tf_op jit(solution)/shard_map/scatter-add | solution.py:437
  505.9 6.4 convolution_convert_fusion.2
  520.9 5.1 convolution_convert_fusion.5
  532.6 7.7 %convolution_convert_fusion.1 = bf16[3072,384]{1,0:T(8,128)(2,1)} fusion(bf16[1024,3072]{1,0:T(8,128)(2,1)} %copy-done.144, bf16[1024,768]{1,0:T(8,128)(2,1)S(1)} %copy-done.39, s32[]{:T(128)S(6)} %select_n.1931), kind=kOutput, calls=%fused_computation.155 | convolution fusion | flops 2417098752 | bytes 9437188 | tf_op jit(solution)/shard_map/dot_general | solution.py:41
  554.7 5.5 collective-permute-done.56
  566.5 4.8 collective-permute-done.57
  575.1 7.5 %collective-permute-start.59 = (bf16[96,384]{1,0:T(8,128)(2,1)S(1)}, bf16[96,384]{1,0:T(8,128)(2,1)S(1)}, u32[]{:S(2)}, u32[]{:S(2)}) collective-permute-start(bf16[96,384]{1,0:T(8,128)(2,1)S(1)} %get-tuple-element.680), channel_id=1, source_target_pairs={{0,16},{1,17},{2,18},{3,19},{4,20},{5,21},{6,22},{7,23},{8,24},{9,... | collective-permute-start | bytes 221192 | tf_op jit(solution)/shard_map/ppermute | solution.py:84
  601.9 12.2 %collective-permute-done.51 = bf16[4,2,192,384]{3,2,0,1:T(8,128)(2,1)S(1)} collective-permute-done((bf16[4,2,192,384]{3,2,0,1:T(8,128)(2,1)S(1)}, bf16[4,2,192,384]{3,2,0,1:T(8,128)(2,1)S(1)}, u32[]{:S(2)}, u32[]{:S(2)}) %collective-permute-start.51) | collective-permute-done | bytes 1179680 | tf_op jit(solution)/shard_map/ppermute | solution.py:84
  621.9 6.4 collective-permute-done.52
  638.2 7.8 %collective-permute-start.48 = (bf16[192,384]{1,0:T(8,128)(2,1)S(1)}, bf16[192,384]{1,0:T(8,128)(2,1)S(1)}, u32[]{:S(2)}, u32[]{:S(2)}) collective-permute-start(bf16[192,384]{1,0:T(8,128)(2,1)S(1)} %get-tuple-element.663), channel_id=1, source_target_pairs={{0,8},{1,9},{2,10},{3,11},{4,12},{5,13},{6,14},{7,15},{8,0},{9,1},... | collective-permute-start | bytes 442376 | tf_op jit(solution)/shard_map/ppermute | solution.py:84
  650.6 5.2 collective-permute-done.49
  688.0 30.1 %multiply_subtract_fusion = (f32[3840,768]{1,0:T(8,128)}, f32[3840,768]{1,0:T(8,128)}, f32[3840,768]{1,0:T(8,128)}) fusion(f32[3840,768]{1,0:T(8,128)} %param.34, f32[3840,768]{1,0:T(8,128)} %get-tuple-element.1177, f32[]{:T(128)S(6)} %div.330, f32[2,3840,768]{2,1,0:T(8,128)} %param.39), kind=kLoop, calls=%fused_computation.135 | loop fusion | flops 44236800 | bytes 82575360 | tf_op jit(solution)/shard_map/sub | solution.py:57
  (662 shorter events, 374.0 us)
Async XLA Ops:
  10.4 20.9 %collective-permute-start.22 = (s32[16,128]{1,0:T(8,128)}, s32[16,128]{1,0:T(8,128)}, u32[]{:S(2)}, u32[]{:S(2)}) collective-permute-start(s32[16,128]{1,0:T(8,128)} %bitcast.734), channel_id=1, source_target_pairs={{0,3},{1,2},{2,1},{3,0},{4,7},{5,6},{6,5},{7,4},{8,11},{9,10},{10,... | collective-permute-start | bytes 24584 | tf_op jit(solution)/shard_map/ppermute | solution.py:84
  12.8 18.5 %collective-permute-start.23 = (s32[16,128]{1,0:T(8,128)}, s32[16,128]{1,0:T(8,128)}, u32[]{:S(2)}, u32[]{:S(2)}) collective-permute-start(s32[16,128]{1,0:T(8,128)} %bitcast.735), channel_id=1, source_target_pairs={{0,2},{1,3},{2,0},{3,1},{4,6},{5,7},{6,4},{7,5},{8,10},{9,11},{10,... | collective-permute-start | bytes 24584 | tf_op jit(solution)/shard_map/ppermute | solution.py:84
  13.3 17.9 %collective-permute-start.24 = (s32[16,128]{1,0:T(8,128)}, s32[16,128]{1,0:T(8,128)}, u32[]{:S(2)}, u32[]{:S(2)}) collective-permute-start(s32[16,128]{1,0:T(8,128)} %bitcast.736), channel_id=1, source_target_pairs={{0,1},{1,0},{2,3},{3,2},{4,5},{5,4},{6,7},{7,6},{8,9},{9,8},{10,11... | collective-permute-start | bytes 24584 | tf_op jit(solution)/shard_map/ppermute | solution.py:84
  33.3 16.2 %collective-permute-start.25 = (s32[4,16,128]{2,1,0:T(8,128)}, s32[4,16,128]{2,1,0:T(8,128)}, u32[]{:S(2)}, u32[]{:S(2)}) collective-permute-start(s32[4,16,128]{2,1,0:T(8,128)} %pad_add_fusion.4), channel_id=1, source_target_pairs={{0,4},{1,5},{2,6},{3,7},{4,0},{5,1},{6,2},{7,3},{8,12},{9,13},{10,... | collective-permute-start | bytes 98312 | tf_op jit(solution)/shard_map/ppermute | solution.py:84
  57.5 19.9 %collective-permute-start.30 = (bf16[256,768]{1,0:T(8,128)(2,1)}, bf16[256,768]{1,0:T(8,128)(2,1)}, u32[]{:S(2)}, u32[]{:S(2)}) collective-permute-start(bf16[256,768]{1,0:T(8,128)(2,1)} %get-tuple-element.649), channel_id=1, source_target_pairs={{0,2},{1,3},{2,0},{3,1},{4,6},{5,7},{6,4},{7,5},{8,10},{9,11},{10,... | collective-permute-start | bytes 1179656 | tf_op jit(solution)/shard_map/ppermute | solution.py:84
  58.8 18.6 %collective-permute-start.29 = (bf16[256,768]{1,0:T(8,128)(2,1)}, bf16[256,768]{1,0:T(8,128)(2,1)}, u32[]{:S(2)}, u32[]{:S(2)}) collective-permute-start(bf16[256,768]{1,0:T(8,128)(2,1)} %get-tuple-element.650), channel_id=1, source_target_pairs={{0,1},{1,0},{2,3},{3,2},{4,5},{5,4},{6,7},{7,6},{8,9},{9,8},{10,11... | collective-permute-start | bytes 1179656 | tf_op jit(solution)/shard_map/ppermute | solution.py:84
  338.9 14.9 %collective-permute-start.62 = (bf16[128,768]{1,0:T(8,128)(2,1)S(1)}, bf16[128,768]{1,0:T(8,128)(2,1)S(1)}, u32[]{:S(2)}, u32[]{:S(2)}) collective-permute-start(bf16[128,768]{1,0:T(8,128)(2,1)S(1)} %get-tuple-element.645), channel_id=1, source_target_pairs={{0,8},{1,9},{2,10},{3,11},{4,12},{5,13},{6,14},{7,15},{8,0},{9,1},... | collective-permute-start | bytes 589832 | tf_op jit(solution)/shard_map/ppermute | solution.py:84
  340.2 17.4 %collective-permute-start.63 = (bf16[128,768]{1,0:T(8,128)(2,1)S(1)}, bf16[128,768]{1,0:T(8,128)(2,1)S(1)}, u32[]{:S(2)}, u32[]{:S(2)}) collective-permute-start(bf16[128,768]{1,0:T(8,128)(2,1)S(1)} %get-tuple-element.644), channel_id=1, source_target_pairs={{0,12},{1,13},{2,14},{3,15},{4,8},{5,9},{6,10},{7,11},{8,4},{9,5},... | collective-permute-start | bytes 589832 | tf_op jit(solution)/shard_map/ppermute | solution.py:84
  341.5 16.1 %collective-permute-start.64 = (bf16[128,768]{1,0:T(8,128)(2,1)S(1)}, bf16[128,768]{1,0:T(8,128)(2,1)S(1)}, u32[]{:S(2)}, u32[]{:S(2)}) collective-permute-start(bf16[128,768]{1,0:T(8,128)(2,1)S(1)} %get-tuple-element.643), channel_id=1, source_target_pairs={{0,16},{1,17},{2,18},{3,19},{4,20},{5,21},{6,22},{7,23},{8,24},{9,... | collective-permute-start | bytes 589832 | tf_op jit(solution)/shard_map/ppermute | solution.py:84
  343.6 27.9 %collective-permute-start.65 = (bf16[128,768]{1,0:T(8,128)(2,1)S(1)}, bf16[128,768]{1,0:T(8,128)(2,1)S(1)}, u32[]{:S(2)}, u32[]{:S(2)}) collective-permute-start(bf16[128,768]{1,0:T(8,128)(2,1)S(1)} %get-tuple-element.642), channel_id=1, source_target_pairs={{0,20},{1,21},{2,22},{3,23},{4,16},{5,17},{6,18},{7,19},{8,28},{9,... | collective-permute-start | bytes 589832 | tf_op jit(solution)/shard_map/ppermute | solution.py:84
  345.0 26.6 %collective-permute-start.66 = (bf16[128,768]{1,0:T(8,128)(2,1)S(1)}, bf16[128,768]{1,0:T(8,128)(2,1)S(1)}, u32[]{:S(2)}, u32[]{:S(2)}) collective-permute-start(bf16[128,768]{1,0:T(8,128)(2,1)S(1)} %get-tuple-element.641), channel_id=1, source_target_pairs={{0,24},{1,25},{2,26},{3,27},{4,28},{5,29},{6,30},{7,31},{8,16},{9,... | collective-permute-start | bytes 589832 | tf_op jit(solution)/shard_map/ppermute | solution.py:84
  353.8 17.8 %collective-permute-start.67 = (bf16[128,768]{1,0:T(8,128)(2,1)S(1)}, bf16[128,768]{1,0:T(8,128)(2,1)S(1)}, u32[]{:S(2)}, u32[]{:S(2)}) collective-permute-start(bf16[128,768]{1,0:T(8,128)(2,1)S(1)} %get-tuple-element.640), channel_id=1, source_target_pairs={{0,28},{1,29},{2,30},{3,31},{4,24},{5,25},{6,26},{7,27},{8,20},{9,... | collective-permute-start | bytes 589832 | tf_op jit(solution)/shard_map/ppermute | solution.py:84
  371.7 33.2 %collective-permute-start.68 = (bf16[1024,768]{1,0:T(8,128)(2,1)S(1)}, bf16[1024,768]{1,0:T(8,128)(2,1)}, u32[]{:S(2)}, u32[]{:S(2)}) collective-permute-start(bf16[1024,768]{1,0:T(8,128)(2,1)S(1)} %constant_dynamic-update-slice_fusion.15), channel_id=1, source_target_pairs={{0,2},{1,3},{2,0},{3,1},{4,6},{5,7},{6,4},{7,5},{8,10},{9,11},{10,... | collective-permute-start | bytes 4718600 | tf_op jit(solution)/shard_map/ppermute | solution.py:84
  410.6 43.6 %collective-permute-start.69 = (bf16[2,1024,768]{2,1,0:T(8,128)(2,1)}, bf16[2,1024,768]{2,1,0:T(8,128)(2,1)}, u32[]{:S(2)}, u32[]{:S(2)}) collective-permute-start(bf16[2,1024,768]{2,1,0:T(8,128)(2,1)} %pad_maximum_fusion.2), channel_id=1, source_target_pairs={{0,1},{1,0},{2,3},{3,2},{4,5},{5,4},{6,7},{7,6},{8,9},{9,8},{10,11... | collective-permute-start | bytes 9437192 | tf_op jit(solution)/shard_map/ppermute | solution.py:84
  505.4 35.0 %collective-permute-start.39 = (bf16[8,2,208,384]{3,2,1,0:T(8,128)(2,1)}, bf16[8,2,208,384]{3,2,1,0:T(8,128)(2,1)}, u32[]{:S(2)}, u32[]{:S(2)}) collective-permute-start(bf16[8,2,208,384]{3,2,1,0:T(8,128)(2,1)} %pad_maximum_fusion.3), channel_id=1, source_target_pairs={{0,1},{1,0},{2,3},{3,2},{4,5},{5,4},{6,7},{7,6},{8,9},{9,8},{10,11... | collective-permute-start | bytes 7667720 | tf_op jit(solution)/shard_map/ppermute | solution.py:84
  520.9 62.3 %collective-permute-start.45 = (bf16[8,2,384,384]{3,2,1,0:T(8,128)(2,1)}, bf16[8,2,384,384]{3,2,1,0:T(8,128)(2,1)}, u32[]{:S(2)}, u32[]{:S(2)}) collective-permute-start(bf16[8,2,384,384]{3,2,1,0:T(8,128)(2,1)} %pad_maximum_fusion.1), channel_id=1, source_target_pairs={{0,1},{1,0},{2,3},{3,2},{4,5},{5,4},{6,7},{7,6},{8,9},{9,8},{10,11... | collective-permute-start | bytes 14155784 | tf_op jit(solution)/shard_map/ppermute | solution.py:84
  544.3 15.9 %collective-permute-start.56 = (bf16[4,2,96,384]{3,2,0,1:T(8,128)(2,1)}, bf16[4,2,96,384]{3,2,0,1:T(8,128)(2,1)S(1)}, u32[]{:S(2)}, u32[]{:S(2)}) collective-permute-start(bf16[4,2,96,384]{3,2,0,1:T(8,128)(2,1)} %bitcast.553), channel_id=1, source_target_pairs={{0,2},{1,3},{2,0},{3,1},{4,6},{5,7},{6,4},{7,5},{8,10},{9,11},{10,... | collective-permute-start | bytes 1769480 | tf_op jit(solution)/shard_map/ppermute | solution.py:84
  546.7 17.9 %collective-permute-start.40 = (bf16[4,2,112,384]{3,2,1,0:T(8,128)(2,1)}, bf16[4,2,112,384]{3,2,1,0:T(8,128)(2,1)}, u32[]{:S(2)}, u32[]{:S(2)}) collective-permute-start(bf16[4,2,112,384]{3,2,1,0:T(8,128)(2,1)} %dynamic-slice_bitcast_fusion), channel_id=1, source_target_pairs={{0,4},{1,5},{2,6},{3,7},{4,0},{5,1},{6,2},{7,3},{8,12},{9,13},{10,... | collective-permute-start | bytes 2064392 | tf_op jit(solution)/shard_map/ppermute | solution.py:84
  565.9 23.1 %collective-permute-start.41 = (bf16[4,112,384]{2,1,0:T(8,128)(2,1)S(1)}, bf16[4,112,384]{2,1,0:T(8,128)(2,1)S(1)}, u32[]{:S(2)}, u32[]{:S(2)}) collective-permute-start(bf16[4,112,384]{2,1,0:T(8,128)(2,1)S(1)} %dynamic-slice_bitcast_fusion.3), channel_id=1, source_target_pairs={{0,2},{1,3},{2,0},{3,1},{4,6},{5,7},{6,4},{7,5},{8,10},{9,11},{10,... | collective-permute-start | bytes 1032200 | tf_op jit(solution)/shard_map/ppermute | solution.py:84
  571.4 19.7 %collective-permute-start.60 = (bf16[96,384]{1,0:T(8,128)(2,1)S(1)}, bf16[96,384]{1,0:T(8,128)(2,1)S(1)}, u32[]{:S(2)}, u32[]{:S(2)}) collective-permute-start(bf16[96,384]{1,0:T(8,128)(2,1)S(1)} %get-tuple-element.679), channel_id=1, source_target_pairs={{0,24},{1,25},{2,26},{3,27},{4,28},{5,29},{6,30},{7,31},{8,16},{9,... | collective-permute-start | bytes 221192 | tf_op jit(solution)/shard_map/ppermute | solution.py:84
  575.1 18.3 %collective-permute-start.59 = (bf16[96,384]{1,0:T(8,128)(2,1)S(1)}, bf16[96,384]{1,0:T(8,128)(2,1)S(1)}, u32[]{:S(2)}, u32[]{:S(2)}) collective-permute-start(bf16[96,384]{1,0:T(8,128)(2,1)S(1)} %get-tuple-element.680), channel_id=1, source_target_pairs={{0,16},{1,17},{2,18},{3,19},{4,20},{5,21},{6,22},{7,23},{8,24},{9,... | collective-permute-start | bytes 221192 | tf_op jit(solution)/shard_map/ppermute | solution.py:84
  587.8 26.3 %collective-permute-start.51 = (bf16[4,2,192,384]{3,2,0,1:T(8,128)(2,1)S(1)}, bf16[4,2,192,384]{3,2,0,1:T(8,128)(2,1)S(1)}, u32[]{:S(2)}, u32[]{:S(2)}) collective-permute-start(bf16[4,2,192,384]{3,2,0,1:T(8,128)(2,1)S(1)} %bitcast.693), channel_id=1, source_target_pairs={{0,4},{1,5},{2,6},{3,7},{4,0},{5,1},{6,2},{7,3},{8,12},{9,13},{10,... | collective-permute-start | bytes 3538952 | tf_op jit(solution)/shard_map/ppermute | solution.py:84
  589.5 26.8 %collective-permute-start.46 = (bf16[4,2,192,384]{3,2,0,1:T(8,128)(2,1)S(1)}, bf16[4,2,192,384]{3,2,0,1:T(8,128)(2,1)S(1)}, u32[]{:S(2)}, u32[]{:S(2)}) collective-permute-start(bf16[4,2,192,384]{3,2,0,1:T(8,128)(2,1)S(1)} %bitcast.694), channel_id=1, source_target_pairs={{0,2},{1,3},{2,0},{3,1},{4,6},{5,7},{6,4},{7,5},{8,10},{9,11},{10,... | collective-permute-start | bytes 3538952 | tf_op jit(solution)/shard_map/ppermute | solution.py:84
  614.5 13.7 %collective-permute-start.52 = (bf16[4,192,384]{2,1,0:T(8,128)(2,1)S(1)}, bf16[4,192,384]{2,1,0:T(8,128)(2,1)}, u32[]{:S(2)}, u32[]{:S(2)}) collective-permute-start(bf16[4,192,384]{2,1,0:T(8,128)(2,1)S(1)} %dynamic-slice_bitcast_fusion.1), channel_id=1, source_target_pairs={{0,2},{1,3},{2,0},{3,1},{4,6},{5,7},{6,4},{7,5},{8,10},{9,11},{10,... | collective-permute-start | bytes 1769480 | tf_op jit(solution)/shard_map/ppermute | solution.py:84
  616.7 17.3 %collective-permute-start.47 = (bf16[4,192,384]{2,1,0:T(8,128)(2,1)S(1)}, bf16[4,192,384]{2,1,0:T(8,128)(2,1)}, u32[]{:S(2)}, u32[]{:S(2)}) collective-permute-start(bf16[4,192,384]{2,1,0:T(8,128)(2,1)S(1)} %dynamic-slice_bitcast_fusion.2), channel_id=1, source_target_pairs={{0,4},{1,5},{2,6},{3,7},{4,0},{5,1},{6,2},{7,3},{8,12},{9,13},{10,... | collective-permute-start | bytes 1769480 | tf_op jit(solution)/shard_map/ppermute | solution.py:84
  632.0 18.6 %collective-permute-start.54 = (bf16[192,384]{1,0:T(8,128)(2,1)S(1)}, bf16[192,384]{1,0:T(8,128)(2,1)S(1)}, u32[]{:S(2)}, u32[]{:S(2)}) collective-permute-start(bf16[192,384]{1,0:T(8,128)(2,1)S(1)} %get-tuple-element.668), channel_id=1, source_target_pairs={{0,16},{1,17},{2,18},{3,19},{4,20},{5,21},{6,22},{7,23},{8,24},{9,... | collective-permute-start | bytes 442376 | tf_op jit(solution)/shard_map/ppermute | solution.py:84
  632.6 17.9 %collective-permute-start.53 = (bf16[192,384]{1,0:T(8,128)(2,1)S(1)}, bf16[192,384]{1,0:T(8,128)(2,1)S(1)}, u32[]{:S(2)}, u32[]{:S(2)}) collective-permute-start(bf16[192,384]{1,0:T(8,128)(2,1)S(1)} %get-tuple-element.666), channel_id=1, source_target_pairs={{0,8},{1,9},{2,10},{3,11},{4,12},{5,13},{6,14},{7,15},{8,0},{9,1},... | collective-permute-start | bytes 442376 | tf_op jit(solution)/shard_map/ppermute | solution.py:84
  635.3 15.3 %collective-permute-start.50 = (bf16[192,384]{1,0:T(8,128)(2,1)S(1)}, bf16[192,384]{1,0:T(8,128)(2,1)S(1)}, u32[]{:S(2)}, u32[]{:S(2)}) collective-permute-start(bf16[192,384]{1,0:T(8,128)(2,1)S(1)} %get-tuple-element.664), channel_id=1, source_target_pairs={{0,24},{1,25},{2,26},{3,27},{4,28},{5,29},{6,30},{7,31},{8,16},{9,... | collective-permute-start | bytes 442376 | tf_op jit(solution)/shard_map/ppermute | solution.py:84
  637.7 18.2 %collective-permute-start.49 = (bf16[192,384]{1,0:T(8,128)(2,1)S(1)}, bf16[192,384]{1,0:T(8,128)(2,1)S(1)}, u32[]{:S(2)}, u32[]{:S(2)}) collective-permute-start(bf16[192,384]{1,0:T(8,128)(2,1)S(1)} %get-tuple-element.665), channel_id=1, source_target_pairs={{0,16},{1,17},{2,18},{3,19},{4,20},{5,21},{6,22},{7,23},{8,24},{9,... | collective-permute-start | bytes 442376 | tf_op jit(solution)/shard_map/ppermute | solution.py:84
  638.2 17.6 %collective-permute-start.48 = (bf16[192,384]{1,0:T(8,128)(2,1)S(1)}, bf16[192,384]{1,0:T(8,128)(2,1)S(1)}, u32[]{:S(2)}, u32[]{:S(2)}) collective-permute-start(bf16[192,384]{1,0:T(8,128)(2,1)S(1)} %get-tuple-element.663), channel_id=1, source_target_pairs={{0,8},{1,9},{2,10},{3,11},{4,12},{5,13},{6,14},{7,15},{8,0},{9,1},... | collective-permute-start | bytes 442376 | tf_op jit(solution)/shard_map/ppermute | solution.py:84
  669.3 14.9 %collective-permute-start.77 = (bf16[576,384]{1,0:T(8,128)(2,1)S(1)}, bf16[576,384]{1,0:T(8,128)(2,1)S(1)}, u32[]{:S(2)}, u32[]{:S(2)}) collective-permute-start(bf16[576,384]{1,0:T(8,128)(2,1)S(1)} %get-tuple-element.575), channel_id=1, source_target_pairs={{0,2},{1,3},{2,0},{3,1},{4,6},{5,7},{6,4},{7,5},{8,10},{9,11},{10,... | collective-permute-start | bytes 1327112 | tf_op jit(solution)/shard_map/ppermute | solution.py:84
  685.3 35.6 %collective-permute-start.78 = (bf16[2,576,384]{2,1,0:T(8,128)(2,1)}, bf16[2,576,384]{2,1,0:T(8,128)(2,1)}, u32[]{:S(2)}, u32[]{:S(2)}) collective-permute-start(bf16[2,576,384]{2,1,0:T(8,128)(2,1)} %pad_maximum_fusion.5), channel_id=1, source_target_pairs={{0,1},{1,0},{2,3},{3,2},{4,5},{5,4},{6,7},{7,6},{8,9},{9,8},{10,11... | collective-permute-start | bytes 2654216 | tf_op jit(solution)/shard_map/ppermute | solution.py:84
  (174 other events, 1429.1 us)

commit v2 on v1

v2 whole, which is shorter than its diff:
```python
import functools

import jax
import jax.numpy as jnp
from jax import lax
from jax.experimental import pallas as pl
from jax.experimental.pallas import tpu as pltpu
from jax.sharding import PartitionSpec as P

HEADS = 12
STEP = 5


logit_divisor_constant = 0.01
clip_bound = 0.001
beta_first = 0.5
beta_second = 0.5
decay_weight = 0.01
epsilon = 1e-08
rate_table = (0.1, 0.02, 0.1, 0.02, 0.01, 0.2)
finest_arithmetic = lax.Precision.HIGHEST
both = ("blk", "grp")
strip = 384


def contract_rows(left, right):
    return lax.dot_general(
        left, right, (((0,), (0,)), ((), ())), preferred_element_type=jnp.float32
    )


def contract_cols(left, right):
    return lax.dot_general(
        left, right, (((1,), (1,)), ((), ())), preferred_element_type=jnp.float32
    )


def adam_update(grad, moments, master, rate):
    first = beta_first * moments[0] + (1.0 - beta_first) * grad
    second = beta_second * moments[1] + (1.0 - beta_second) * grad * grad
    first_hat = first / (1.0 - beta_first**STEP)
    second_hat = second / (1.0 - beta_second**STEP)
    updated = master - rate * (first_hat / (jnp.sqrt(second_hat) + epsilon) + decay_weight * master)
    return (first, second, updated)


def masked_softmax(pairwise_affinity_matrix, allowed):
    masked = jnp.where(allowed, pairwise_affinity_matrix, -1000000000.0)
    top = jnp.max(masked, -1, keepdims=True)
    expo = jnp.where(allowed, jnp.exp(masked - top), 0.0)
    total = jnp.sum(expo, -1, keepdims=True)
    return (top[:, 0] + jnp.log(total[:, 0]), expo / total)


VMEM_ALLOWED = 56 * 1024 * 1024
low = jnp.bfloat16


def whole_block(shape):
    return pl.BlockSpec(shape, lambda *_: (0,) * len(shape), pipeline_mode=pl.Buffered(1))


def rows_block(rows, columns):
    return pl.BlockSpec((rows, columns), lambda i, *_: (i, 0))


def normalize(states):
    mean = jnp.mean(states, -1, keepdims=True)
    centered = states - mean
    inverse = lax.rsqrt(jnp.mean(centered * centered, -1, keepdims=True) + 1e-06)
    return centered * inverse, inverse


def normalize_back(grad, gain, unit_states, inverse):
    scaled = grad * gain
    inner = jnp.mean(scaled * unit_states, -1, keepdims=True)
    back = inverse * (scaled - jnp.mean(scaled, -1, keepdims=True) - unit_states * inner)
    return back, jnp.sum(grad * unit_states, 0, keepdims=True), jnp.sum(grad, 0, keepdims=True)


def gelu_and_slope(values):
    size = jnp.abs(values) * 0.7071067811865476
    t = 1.0 / (1.0 + 0.3275911 * size)
    series = t * (
        0.254829592
        + t * (-0.284496736 + t * (1.421413741 + t * (-1.453152027 + t * 1.061405429)))
    )
    bell = jnp.exp(-size * size)
    tail = 0.5 * series * bell
    below = jnp.where(values >= 0.0, 1.0 - tail, tail)
    return values * below, below + values * (0.3989422804014327 * bell)


def dot_rows(left, right):
    return lax.dot_general(
        left, right, (((0,), (0,)), ((), ())), preferred_element_type=jnp.float32
    )


def dot_cols(left, right):
    return lax.dot_general(
        left, right, (((1,), (1,)), ((), ())), preferred_element_type=jnp.float32
    )


def dot_plain(left, right):
    return jnp.dot(left, right, preferred_element_type=jnp.float32)


def head_masks(lanes, head_dim):
    even = (lax.broadcasted_iota(jnp.int32, (1, lanes), 1) < head_dim).astype(low)
    return even, (1.0 - even.astype(jnp.float32)).astype(low)


def forward_kernel(
    lengths_ref,
    slots_ref,
    found_ref,
    small_ref,
    qkv_ref,
    out_ref,
    up_ref,
    down_ref,
    unit1_ref,
    inverse1_ref,
    normed_ref,
    projected_ref,
    probs_ref,
    attended_ref,
    unit2_ref,
    inverse2_ref,
    middle_ref,
    activated_ref,
    slope_ref,
    unit3_ref,
    inverse3_ref,
    pooled_ref,
    embed_ref,
    *,
    seq_len,
    seqs,
    head_dim,
):
    step = pl.program_id(0)
    width = found_ref.shape[1]
    rows = seqs * seq_len
    slots = found_ref.shape[0]

    def vector(index):
        return small_ref[seq_len + index : seq_len + index + 1, :]

    pick = slots_ref[...] == lax.broadcasted_iota(jnp.int32, (rows, slots), 1)
    pick = jnp.where(pick, 1.0, 0.0).astype(low)
    embedded = dot_plain(pick, found_ref[...])
    positions = small_ref[:seq_len, :]
    embedded = embedded + jnp.concatenate([positions] * seqs, 0)
    unit1, inverse1 = normalize(embedded)
    unit1_ref[...] = unit1
    inverse1_ref[...] = inverse1
    normed = unit1 * vector(0) + vector(1)
    normed_low = normed.astype(low)
    normed_ref[...] = normed_low
    zeros = jnp.zeros((1, width), jnp.float32)
    for part, bias in enumerate((vector(2), zeros, vector(3))):
        at = slice(part * width, (part + 1) * width)
        projected_ref[:, at] = (dot_plain(normed_low, qkv_ref[:, at]) + bias).astype(low)
    lanes = 2 * head_dim
    even, odd = head_masks(lanes, head_dim)
    key_at = lax.broadcasted_iota(jnp.int32, (2 * seq_len, seq_len), 1)
    for s in range(seqs):
        at = slice(s * seq_len, (s + 1) * seq_len)
        live = key_at < lengths_ref[step * seqs + s]
        for p in range(width // lanes):
            query = projected_ref[at, p * lanes : (p + 1) * lanes]
            keys = projected_ref[at, width + p * lanes : width + (p + 1) * lanes]
            values = projected_ref[at, 2 * width + p * lanes : 2 * width + (p + 1) * lanes]
            query = jnp.concatenate([query * even, query * odd], 0)
            logits = dot_cols(query, keys) * head_dim ** (-0.5)
            logits = jnp.where(live, logits, -1000000000.0)
            expo = jnp.exp(logits - jnp.max(logits, -1, keepdims=True))
            probs = (expo / jnp.sum(expo, -1, keepdims=True)).astype(low)
            probs_ref[s, p] = probs
            both_probs = jnp.concatenate([probs[:seq_len], probs[seq_len:]], 1)
            both_values = jnp.concatenate([values * even, values * odd], 0)
            attended_ref[at, p * lanes : (p + 1) * lanes] = dot_plain(
                both_probs, both_values
            ).astype(low)
    branch = dot_plain(attended_ref[...], out_ref[...]) + vector(4)
    unit2, inverse2 = normalize(normed + branch)
    unit2_ref[...] = unit2
    inverse2_ref[...] = inverse2
    middle = unit2 * vector(5) + vector(6)
    middle_low = middle.astype(low)
    middle_ref[...] = middle_low
    lowered = middle + vector(7)
    for j in range(up_ref.shape[1] // width):
        at = slice(j * width, (j + 1) * width)
        lifted = dot_plain(middle_low, up_ref[:, at]) + vector(10 + j)
        activated, slope = gelu_and_slope(lifted)
        activated = activated.astype(low)
        activated_ref[:, at] = activated
        slope_ref[:, at] = slope.astype(low)
        lowered = lowered + dot_plain(activated, down_ref[at, :])
    unit3, inverse3 = normalize(lowered)
    unit3_ref[...] = unit3
    inverse3_ref[...] = inverse3
    final = unit3 * vector(8) + vector(9)
    row_at = lax.broadcasted_iota(jnp.int32, (seq_len, 1), 0)
    pooled = []
    for s in range(seqs):
        length = lengths_ref[step * seqs + s]
        weights = (row_at < length).astype(jnp.float32)
        total = jnp.sum(final[s * seq_len : (s + 1) * seq_len] * weights, 0, keepdims=True)
        pooled.append(total / length.astype(jnp.float32))
    pooled = jnp.concatenate(pooled, 0)
    pooled_ref[0] = pooled
    squares = jnp.sum(pooled * pooled, -1, keepdims=True)
    embed_ref[0] = (pooled * lax.rsqrt(squares + 1e-06)).astype(low)


def forward(lengths_flat, slot, found, small_rows, weights, seq_len, head_dim):
    tokens, width = slot.shape[0], found.shape[1]
    seqs = 2
    rows = seqs * seq_len
    steps = tokens // rows
    lifted = weights[2].shape[1]
    f32 = jnp.float32
    outs = [
        ((tokens, width), f32),
        ((tokens, 1), f32),
        ((tokens, width), low),
        ((tokens, 3 * width), low),
        ((steps * seqs, width // (2 * head_dim), 2 * seq_len, seq_len), low),
        ((tokens, width), low),
        ((tokens, width), f32),
        ((tokens, 1), f32),
        ((tokens, width), low),
        ((tokens, lifted), low),
        ((tokens, lifted), low),
        ((tokens, width), f32),
        ((tokens, 1), f32),
        ((steps, seqs, width), f32),
        ((steps, seqs, width), low),
    ]

    def spec(shape):
        if shape[0] == tokens:
            return rows_block(rows, shape[1])
        block = (shape[0] // steps,) + shape[1:]
        return pl.BlockSpec(block, lambda i, *_: (i,) + (0,) * (len(shape) - 1))

    return pl.pallas_call(
        functools.partial(forward_kernel, seq_len=seq_len, seqs=seqs, head_dim=head_dim),
        out_shape=[jax.ShapeDtypeStruct(*item) for item in outs],
        grid_spec=pltpu.PrefetchScalarGridSpec(
            num_scalar_prefetch=1,
            grid=(steps,),
            in_specs=[rows_block(rows, 1), whole_block(found.shape), whole_block(small_rows.shape)]
            + [whole_block(item.shape) for item in weights],
            out_specs=[spec(item[0]) for item in outs],
        ),
        compiler_params=pltpu.CompilerParams(vmem_limit_bytes=VMEM_ALLOWED),
        cost_estimate=pl.CostEstimate(
            flops=20 * 10**9, bytes_accessed=50 * 10**6, transcendentals=10**7
        ),
        name="encoder_forward",
    )(lengths_flat, slot, found, small_rows, *weights)


def feed_back_kernel(
    lengths_ref,
    embed_grad_ref,
    pooled_ref,
    small_ref,
    unit3_ref,
    inverse3_ref,
    slope_ref,
    unit2_ref,
    inverse2_ref,
    up_ref,
    down_ref,
    lowered_ref,
    lifted_ref,
    second_ref,
    sums_ref,
    *,
    seq_len,
    seqs,
):
    step = pl.program_id(0)
    width = unit3_ref.shape[1]

    @pl.when(step == 0)
    def _():
        sums_ref[...] = jnp.zeros_like(sums_ref)

    def vector(index):
        return small_ref[seq_len + index : seq_len + index + 1, :]

    pooled, grad = pooled_ref[0], embed_grad_ref[0]
    inverse = lax.rsqrt(jnp.sum(pooled * pooled, -1, keepdims=True) + 1e-06)
    inner = jnp.sum(pooled * grad, -1, keepdims=True)
    pooled_grad = inverse * (grad - pooled * (inverse * inverse * inner))
    row_at = lax.broadcasted_iota(jnp.int32, (seq_len, 1), 0)
    final_grad = []
    for s in range(seqs):
        length = lengths_ref[step * seqs + s]
        weights = (row_at < length).astype(jnp.float32)
        final_grad.append(weights * (pooled_grad[s : s + 1] / length.astype(jnp.float32)))
    final_grad = jnp.concatenate(final_grad, 0)
    third, gain3, shift3 = normalize_back(
        final_grad, vector(8), unit3_ref[...], inverse3_ref[...]
    )
    lowered_grad = third.astype(low)
    lowered_ref[...] = lowered_grad
    middle_grad = third
    up_sums = []
    for j in range(up_ref.shape[1] // width):
        at = slice(j * width, (j + 1) * width)
        grad = dot_cols(lowered_grad, down_ref[at, :]) * slope_ref[:, at].astype(jnp.float32)
        grad = grad.astype(low)
        lifted_ref[:, at] = grad
        up_sums.append(jnp.sum(grad.astype(jnp.float32), 0, keepdims=True))
        middle_grad = middle_grad + dot_cols(grad, up_ref[:, at])
    second, gain2, shift2 = normalize_back(
        middle_grad, vector(5), unit2_ref[...], inverse2_ref[...]
    )
    second_ref[...] = second
    branch_sum = jnp.sum(second.astype(low).astype(jnp.float32), 0, keepdims=True)
    lowered_sum = jnp.sum(lowered_grad.astype(jnp.float32), 0, keepdims=True)
    sums = [branch_sum, gain2, shift2, lowered_sum, gain3, shift3] + up_sums
    sums_ref[: len(sums), :] += jnp.concatenate(sums, 0)


def feed_back(lengths_flat, embed_grad, kept, small_rows, weights, seq_len):
    unit2, inverse2, slope, unit3, inverse3, pooled = kept
    tokens, width = unit2.shape
    lifted = slope.shape[1]
    seqs = 2
    rows = seqs * seq_len
    steps = tokens // rows
    pair = pl.BlockSpec((1, seqs, width), lambda i, *_: (i, 0, 0))
    return pl.pallas_call(
        functools.partial(feed_back_kernel, seq_len=seq_len, seqs=seqs),
        out_shape=[
            jax.ShapeDtypeStruct((tokens, width), low),
            jax.ShapeDtypeStruct((tokens, lifted), low),
            jax.ShapeDtypeStruct((tokens, width), jnp.float32),
            jax.ShapeDtypeStruct((16, width), jnp.float32),
        ],
        grid_spec=pltpu.PrefetchScalarGridSpec(
            num_scalar_prefetch=1,
            grid=(steps,),
            in_specs=[
                pair,
                pair,
                whole_block(small_rows.shape),
                rows_block(rows, width),
                rows_block(rows, 1),
                rows_block(rows, lifted),
                rows_block(rows, width),
                rows_block(rows, 1),
                whole_block(weights[0].shape),
                whole_block(weights[1].shape),
            ],
            out_specs=[
                rows_block(rows, width),
                rows_block(rows, lifted),
                rows_block(rows, width),
                pl.BlockSpec((16, width), lambda i, *_: (0, 0)),
            ],
        ),
        compiler_params=pltpu.CompilerParams(vmem_limit_bytes=VMEM_ALLOWED),
        cost_estimate=pl.CostEstimate(
            flops=10 * 10**9, bytes_accessed=40 * 10**6, transcendentals=0
        ),
        name="feed_back",
    )(
        lengths_flat,
        embed_grad,
        pooled,
        small_rows,
        unit3,
        inverse3,
        slope,
        unit2,
        inverse2,
        *weights,
    )


def attention_back_kernel(
    slots_ref,
    second_ref,
    projected_ref,
    probs_ref,
    unit1_ref,
    inverse1_ref,
    small_ref,
    qkv_ref,
    out_ref,
    branch_ref,
    projected_grad_ref,
    rows_ref,
    positions_ref,
    sums_ref,
    total_ref,
    *,
    seq_len,
    seqs,
    head_dim,
):
    step = pl.program_id(0)
    width = second_ref.shape[1]
    lanes = 2 * head_dim
    scale = head_dim ** (-0.5)

    @pl.when(step == 0)
    def _():
        sums_ref[...] = jnp.zeros_like(sums_ref)
        positions_ref[...] = jnp.zeros_like(positions_ref)
        total_ref[...] = jnp.zeros_like(total_ref)

    second = second_ref[...]
    branch = second.astype(low)
    branch_ref[...] = branch
    attended_grad = dot_cols(branch, out_ref[...]).astype(low)
    even, odd = head_masks(lanes, head_dim)
    for s in range(seqs):
        at = slice(s * seq_len, (s + 1) * seq_len)
        for p in range(width // lanes):
            here = slice(p * lanes, (p + 1) * lanes)
            there = slice(width + p * lanes, width + (p + 1) * lanes)
            yonder = slice(2 * width + p * lanes, 2 * width + (p + 1) * lanes)
            query = projected_ref[at, here]
            keys = projected_ref[at, there]
            values = projected_ref[at, yonder]
            grad = attended_grad[at, here]
            grad = jnp.concatenate([grad * even, grad * odd], 0)
            query = jnp.concatenate([query * even, query * odd], 0)
            keys = jnp.concatenate([keys * even, keys * odd], 0)
            probs_low = probs_ref[s, p]
            probs = probs_low.astype(jnp.float32)
            probs_grad = dot_cols(grad, values)
            weighted = probs * probs_grad
            inner = jnp.sum(weighted, -1, keepdims=True)
            logits_grad = ((weighted - probs * inner) * scale).astype(low)
            both_grads = jnp.concatenate([logits_grad[:seq_len], logits_grad[seq_len:]], 1)
            projected_grad_ref[at, here] = dot_plain(both_grads, keys).astype(low)
            projected_grad_ref[at, there] = dot_rows(logits_grad, query).astype(low)
            projected_grad_ref[at, yonder] = dot_rows(probs_low, grad).astype(low)
    projected_grad = projected_grad_ref[...]
    query_sum = jnp.sum(projected_grad[:, :width].astype(jnp.float32), 0, keepdims=True)
    value_sum = jnp.sum(projected_grad[:, 2 * width :].astype(jnp.float32), 0, keepdims=True)
    normed_grad = second + dot_cols(projected_grad, qkv_ref[...])
    gain = small_ref[seq_len : seq_len + 1, :]
    embedded_grad, gain1, shift1 = normalize_back(
        normed_grad, gain, unit1_ref[...], inverse1_ref[...]
    )
    for s in range(seqs):
        positions_ref[...] += embedded_grad[s * seq_len : (s + 1) * seq_len]
    sums_ref[:4, :] += jnp.concatenate([gain1, shift1, query_sum, value_sum], 0)
    slots, rows = total_ref.shape[0], seqs * seq_len
    hit = slots_ref[0] == lax.broadcasted_iota(jnp.int32, (slots, rows), 0)
    hit = jnp.where(hit, 1.0, 0.0).astype(low)
    total_ref[...] += dot_plain(hit, embedded_grad.astype(low))

    @pl.when(step == pl.num_programs(0) - 1)
    def _():
        rows_ref[...] = total_ref[...].astype(low)


def attention_back(slot, second, kept, small_rows, weights, seq_len, head_dim, slots):
    projected, probs, unit1, inverse1 = kept
    tokens, width = second.shape
    seqs = 2
    rows = seqs * seq_len
    steps = tokens // rows
    probs_block = (seqs,) + probs.shape[1:]

    def fixed(shape):
        return pl.BlockSpec(shape, lambda i, *_: (0, 0))

    return pl.pallas_call(
        functools.partial(
            attention_back_kernel, seq_len=seq_len, seqs=seqs, head_dim=head_dim
        ),
        out_shape=[
            jax.ShapeDtypeStruct((tokens, width), low),
            jax.ShapeDtypeStruct((tokens, 3 * width), low),
            jax.ShapeDtypeStruct((slots, width), low),
            jax.ShapeDtypeStruct((seq_len, width), jnp.float32),
            jax.ShapeDtypeStruct((8, width), jnp.float32),
        ],
        grid=(steps,),
        in_specs=[
            pl.BlockSpec((1, 1, rows), lambda i: (i, 0, 0)),
            rows_block(rows, width),
            rows_block(rows, 3 * width),
            pl.BlockSpec(probs_block, lambda i: (i, 0, 0, 0)),
            rows_block(rows, width),
            rows_block(rows, 1),
            whole_block(small_rows.shape),
            whole_block(weights[0].shape),
            whole_block(weights[1].shape),
        ],
        out_specs=[
            rows_block(rows, width),
            rows_block(rows, 3 * width),
            fixed((slots, width)),
            fixed((seq_len, width)),
            fixed((8, width)),
        ],
        scratch_shapes=[pltpu.VMEM((slots, width), jnp.float32)],
        compiler_params=pltpu.CompilerParams(vmem_limit_bytes=VMEM_ALLOWED),
        cost_estimate=pl.CostEstimate(
            flops=10 * 10**9, bytes_accessed=30 * 10**6, transcendentals=0
        ),
        name="attention_back",
    )(slot.reshape(steps, 1, rows), second, projected, probs, unit1, inverse1, small_rows, *weights)


def weight_grad_kernel(core_ref, *refs, jobs, xs):
    theirs_ref, mine_ref, turned_ref = refs[-3:]
    step = pl.program_id(0)
    start, base = 0, 0
    for n, (tiles, tall, piece, strips) in enumerate(jobs):
        left_ref, right_ref = refs[2 * n], refs[2 * n + 1]

        def work(start=start, base=base, left_ref=left_ref, right_ref=right_ref, job=jobs[n]):
            tiles, tall, piece, strips = job
            tile = step - start
            if tall or tiles == 1:
                grad = dot_rows(left_ref[...], right_ref[...])
            else:

                @pl.when(tile == 0)
                def _():
                    turned_ref[...] = left_ref[...].T

                grad = dot_plain(turned_ref[...], right_ref[...])
            count = grad.shape[0] // piece // xs
            for j in range(2):
                part = grad[:, j * strip : (j + 1) * strip]
                part = part.reshape(count, xs, piece, strip)
                if tall:
                    half = j
                    at = (pl.ds(tile * count, count), slice(None), pl.ds(base, piece))
                else:
                    number = 2 * tile + j
                    half = number // strips
                    row = pl.multiple_of(base + (number % strips) * piece, 16)
                    at = (slice(None), slice(None), pl.ds(row, piece))

                @pl.when(core_ref[0] == half)
                def _(at=at, part=part):
                    mine_ref[at] = part

                @pl.when(core_ref[0] != half)
                def _(at=at, part=part):
                    theirs_ref[at] = part.astype(low)

        pl.when((step >= start) & (step < start + tiles))(work)
        start += tiles
        base += piece * strips


def weight_grads(place, pairs):
    tile_rows = 2 * strip
    jobs, in_specs, operands = [], [], []
    start, rows = 0, 0
    tokens = pairs[0][0].shape[0]
    for left, right in pairs:
        strips = right.shape[1] // 2 // strip
        tall = left.shape[1] > tile_rows
        tiles = left.shape[1] // tile_rows if tall else strips
        piece = left.shape[1] // place.blk // place.xs

        def tile_of(i, start=start, tiles=tiles):
            return jnp.clip(i - start, 0, tiles - 1)

        def block(varies, f=tile_of):
            if varies:
                return pl.BlockSpec((tokens, tile_rows), lambda i, h: (0, f(i)))
            return whole_block((tokens, tile_rows))

        in_specs += [block(tall), block(not tall and tiles > 1)]
        jobs.append((tiles, tall, piece, strips))
        operands += [left, right]
        start += tiles
        rows += piece * strips
    shape = (place.blk, place.xs, rows, strip)
    return pl.pallas_call(
        functools.partial(weight_grad_kernel, jobs=jobs, xs=place.xs),
        out_shape=[
            jax.ShapeDtypeStruct(shape, low),
            jax.ShapeDtypeStruct(shape, jnp.float32),
        ],
        grid_spec=pltpu.PrefetchScalarGridSpec(
            num_scalar_prefetch=1,
            grid=(start,),
            in_specs=in_specs,
            out_specs=[whole_block(shape), whole_block(shape)],
            scratch_shapes=[pltpu.VMEM((tile_rows, tokens), low)],
        ),
        compiler_params=pltpu.CompilerParams(vmem_limit_bytes=VMEM_ALLOWED),
        cost_estimate=pl.CostEstimate(
            flops=start * 2 * tokens * tile_rows * tile_rows,
            bytes_accessed=16 * 10**6,
            transcendentals=0,
        ),
        name="weight_grads",
    )(place.core.reshape(1).astype(jnp.int32), *operands)


def word_sum_kernel(place_ref, count_ref, id_ref, *refs, grp, blk, room, span):
    sources = refs[:grp]
    out_ref, squares_ref, total_ref, rows_ref, chunk_ref, in_sems, out_sem = refs[grp:]
    batch = 8
    copies = [
        pltpu.make_async_copy(sources[k], rows_ref.at[k], in_sems.at[k]) for k in range(grp)
    ]
    for copy in copies:
        copy.start()
    zeros = jnp.zeros((batch, total_ref.shape[1]), jnp.float32)

    def clear(i, _):
        total_ref[pl.ds(pl.multiple_of(i * batch, batch), batch), :] = zeros
        return 0

    lax.fori_loop(0, total_ref.shape[0] // batch, clear, 0, unroll=4)
    for copy in copies:
        copy.wait()

    def one_source(n, _):
        slot = (n // blk) ^ place_ref[0]
        start = (n % blk) * room
        count = count_ref[n]

        def widen(i, _):
            at = pl.ds(pl.multiple_of(start + i * 16, 16), 16)
            to = pl.ds(pl.multiple_of(i * 16, 16), 16)
            chunk_ref[to, :] = rows_ref[slot, at, :].astype(jnp.float32)
            return 0

        lax.fori_loop(0, (count + 15) // 16, widen, 0)

        def add(i, _):
            at = [id_ref[n * room + i * batch + j] for j in range(batch)]
            sums = [
                total_ref[pl.ds(at[j], 1), :] + chunk_ref[pl.ds(i * batch + j, 1), :]
                for j in range(batch)
            ]
            for j in range(batch):
                total_ref[pl.ds(at[j], 1), :] = sums[j]
            return 0

        lax.fori_loop(0, (count + batch - 1) // batch, add, 0)
        return 0

    lax.fori_loop(0, grp * blk, one_source, 0)
    shard_rows = out_ref.shape[0]

    def finish(i, squares):
        at = pl.ds(pl.multiple_of(i * span, span), span)
        part = total_ref[at, :]
        pltpu.make_async_copy(total_ref.at[at], out_ref.at[at], out_sem).start()
        part = part * part
        return squares + jnp.sum(part.reshape(span // 8, 8, part.shape[1]), 0)

    squares = lax.fori_loop(
        0, shard_rows // span, finish, jnp.zeros((8, total_ref.shape[1]), jnp.float32)
    )
    squares_ref[...] = jnp.sum(squares, 0, keepdims=True)
    pltpu.make_async_copy(total_ref.at[pl.ds(0, shard_rows)], out_ref, out_sem).wait()


def word_sum(grp_index, counts, ids, sources, shard_rows, blk, room):
    grp, width = len(sources), sources[0].shape[1]
    span = next(size for size in (128, 64, 32, 16, 8) if shard_rows % size == 0)
    anywhere = pl.BlockSpec(memory_space=pl.ANY)
    return pl.pallas_call(
        functools.partial(word_sum_kernel, grp=grp, blk=blk, room=room, span=span),
        out_shape=[
            jax.ShapeDtypeStruct((shard_rows, width), jnp.float32),
            jax.ShapeDtypeStruct((1, width), jnp.float32),
        ],
        grid_spec=pltpu.PrefetchScalarGridSpec(
            num_scalar_prefetch=3,
            grid=(1,),
            in_specs=[anywhere] * grp,
            out_specs=[anywhere, whole_block((1, width))],
            scratch_shapes=[
                pltpu.VMEM((shard_rows + 32, width), jnp.float32),
                pltpu.VMEM((grp,) + sources[0].shape, low),
                pltpu.VMEM((room, width), jnp.float32),
                pltpu.SemaphoreType.DMA((grp,)),
                pltpu.SemaphoreType.DMA,
            ],
        ),
        compiler_params=pltpu.CompilerParams(vmem_limit_bytes=VMEM_ALLOWED),
        cost_estimate=pl.CostEstimate(
            flops=10**7, bytes_accessed=40 * 10**6, transcendentals=0
        ),
        name="word_sum",
    )(grp_index.reshape(1), counts, ids, *sources)


class Place:
    def __init__(self):
        self.blk, self.grp = lax.axis_size("blk"), lax.axis_size("grp")
        self.count = self.blk * self.grp
        self.b, self.g = lax.axis_index("blk"), lax.axis_index("grp")
        self.xs, self.far = self.grp // 2, self.blk // 2
        self.core, self.x = self.g % 2, self.g // 2
        self.y, self.z = self.b % 2, self.b // 2
        self.core_masks = [0, 1]
        self.x_masks = [2 * i for i in range(self.xs)]
        self.y_masks = [0, self.grp]
        self.z_masks = [2 * self.grp * i for i in range(self.far)]

    def send(self, value, mask):
        pairs = [(i, i ^ mask) for i in range(self.count)]
        return lax.ppermute(value, both, pairs)


def in_order(pieces, index):
    step = 1
    while step < len(pieces):
        odd = (index & step) != 0
        pieces = [jnp.where(odd, pieces[i ^ step], pieces[i]) for i in range(len(pieces))]
        step *= 2
    return pieces


def gather_stage(place, value, masks, index):
    pieces = [value] + [place.send(value, mask) for mask in masks[1:]]
    return jnp.stack(in_order(pieces, index))


def gather_far_first(place, value):
    shape = value.shape
    value = gather_stage(place, value, place.z_masks, place.z)
    middle = [a + b for a in place.y_masks for b in place.x_masks]
    value = gather_stage(place, value, middle, place.y * place.xs + place.x)
    value = gather_stage(place, value, place.core_masks, place.core)
    value = value.reshape((2, 2, place.xs, place.far) + shape)
    return jnp.transpose(value, (3, 1, 2, 0) + tuple(range(4, 4 + len(shape)))).reshape(
        (place.blk, place.grp) + shape
    )


def to_send(value, fine):
    high = value.astype(low)
    if not fine:
        return high
    rows = value.shape[-2]
    rest = value[..., rows - fine :, :] - high[..., rows - fine :, :].astype(jnp.float32)
    return jnp.concatenate([high, rest.astype(low)], -2)


def from_sent(value, fine):
    value = value.astype(jnp.float32)
    if not fine:
        return value
    rows = value.shape[-2] - fine
    tail = value[..., rows - fine : rows, :] + value[..., rows:, :]
    return jnp.concatenate([value[..., : rows - fine, :], tail], -2)


def reduce_stage(place, value, masks, index, fine):
    terms = [lax.dynamic_index_in_dim(value, index, 0, keepdims=False).astype(jnp.float32)]
    for k in range(1, len(masks)):
        part = lax.dynamic_index_in_dim(value, index ^ k, 0, keepdims=False)
        terms.append(from_sent(place.send(to_send(part, fine), masks[k]), fine))
    while len(terms) > 1:
        terms = [terms[i] + terms[i + 1] for i in range(0, len(terms), 2)]
    return terms[0]


def reduce_rest(place, value, x_first, fine):
    rows = value.shape[2]
    value = value.reshape(place.far, 2, place.xs, rows, value.shape[3])
    if x_first:
        value = jnp.moveaxis(value, 2, 0)
        value = reduce_stage(place, value, place.x_masks, place.x, fine)
        value = jnp.moveaxis(value, 1, 0)
        value = reduce_stage(place, value, place.y_masks, place.y, fine)
    else:
        value = jnp.moveaxis(value, 1, 0)
        value = reduce_stage(place, value, place.y_masks, place.y, fine)
        value = jnp.moveaxis(value, 1, 0)
        value = reduce_stage(place, value, place.x_masks, place.x, fine)
    return reduce_stage(place, value, place.z_masks, place.z, fine)


def half_gradient(place, left, right, core):
    width = right.shape[1] // 2
    part = lax.dynamic_slice_in_dim(right, core * width, width, 1)
    grad = contract_rows(left, part).astype(jnp.bfloat16)
    rows = grad.shape[0] // place.blk // place.xs
    strips = width // strip
    grad = grad.reshape(place.blk, place.xs, rows, strips, strip)
    return jnp.transpose(grad, (0, 1, 3, 2, 4)).reshape(
        place.blk, place.xs, strips * rows, strip
    )


def reduce_group(place, pairs, extra):
    if all(a.shape[1] % (16 * place.blk * place.xs) == 0 for a, _ in pairs):
        theirs, mine = weight_grads(place, pairs)
    else:
        mine = [half_gradient(place, a, b, place.core) for a, b in pairs]
        theirs = [half_gradient(place, a, b, 1 - place.core) for a, b in pairs]
        mine, theirs = jnp.concatenate(mine, 2), jnp.concatenate(theirs, 2)
    fine = 0
    if extra is not None:
        fine = extra.shape[3]
        own = lax.dynamic_index_in_dim(extra, place.core, 2, keepdims=False)
        mine = jnp.concatenate([mine.astype(jnp.float32), own], 2)
        other = lax.dynamic_index_in_dim(extra, 1 - place.core, 2, keepdims=False)
        theirs = jnp.concatenate([theirs, to_send(other, fine)], 2)
    arrived = from_sent(place.send(theirs, 1), fine)
    return mine.astype(jnp.float32) + arrived, fine


def reduce_group_rest(place, value, fine):
    cut = value.shape[2] // 32 * 16
    return jnp.concatenate(
        [
            reduce_rest(place, value[:, :, :cut], True, 0),
            reduce_rest(place, value[:, :, cut:], False, fine),
        ]
    )


def whole_rows(place, pieces, rows, width):
    strips = width // 2 // strip
    pieces = pieces.reshape(place.xs, 2, strips, rows, strip)
    return jnp.transpose(pieces, (0, 3, 1, 2, 4)).reshape(place.xs * rows, width)


def on_device(
    token_ids,
    lengths,
    valid,
    false_neg,
    word_table,
    qkv_weight,
    out_weight,
    up_weight,
    down_weight,
    word_master,
    qkv_master,
    out_master,
    up_master,
    down_master,
    word_moments,
    qkv_moments,
    out_moments,
    up_moments,
    down_moments,
    small_rows,
    small_moments,
):
    place = Place()
    pairs_here = token_ids.shape[0]
    total_pairs = pairs_here * place.count
    seq_count = 2 * pairs_here
    seq_len = token_ids.shape[2]
    width = word_table.shape[1]
    head_dim = width // HEADS
    flat_ids = token_ids.reshape(-1)
    tokens = flat_ids.shape[0]
    lengths_flat = lengths.reshape(-1)

    shard_rows = word_master.shape[0]
    table_rows = word_table.shape[0]
    per_owner = table_rows // shard_rows
    room = max(16, tokens // place.blk)
    shard = flat_ids // shard_rows
    same_id = flat_ids[:, None] == flat_ids[None, :]
    before = jnp.arange(tokens)[:, None] < jnp.arange(tokens)[None, :]
    first = ~jnp.any(same_id & before, 0)
    smaller = (
        (shard[:, None] == shard[None, :])
        & (flat_ids[None, :] < flat_ids[:, None])
        & first[None, :]
    )
    rank = jnp.sum(smaller.astype(jnp.int32), 1)
    slots = place.blk * room

    def slot_ids_of(round_number):
        at = rank - round_number * room
        slot = jnp.where((at >= 0) & (at < room), shard * room + at, slots)
        hit = slot[None, :] == jnp.arange(slots)[:, None]
        return jnp.max(jnp.where(hit, flat_ids[None, :], -1), 1)

    def lookup_slots(round_number):
        at = rank - round_number * room
        owner = shard // per_owner
        relative = ((owner ^ place.g) * per_owner + shard % per_owner) * room + at
        return jnp.where((at >= 0) & (at < room), relative, slots)

    def gradient_slots(round_number):
        at = rank - round_number * room
        relative = (shard ^ place.b) * room + at
        return jnp.where((at >= 0) & (at < room), relative, slots)

    def fetch(grp_ids, round_number):
        span = per_owner * room
        asked = [lax.dynamic_slice_in_dim(ids, place.g * span, span) for ids in grp_ids]
        local = jnp.concatenate(asked) - place.g * table_rows
        found = word_table.at[jnp.clip(local, 0, table_rows - 1)].get(mode="clip")
        parts = [found[k * span : (k + 1) * span] for k in range(place.grp)]
        rows = [parts[0]] + [place.send(parts[k], k) for k in range(1, place.grp)]
        return jnp.concatenate(rows)

    def pack(values, length):
        return jnp.concatenate([values, jnp.zeros((length - values.shape[0],), values.dtype)])

    slot_ids = slot_ids_of(0)
    early = jnp.concatenate(
        [slot_ids, false_neg.reshape(-1), valid, jnp.max(rank)[None]]
    )
    early = pack(early, -(-early.shape[0] // 1024) * 1024).reshape(-1, 128)
    grp_early = [early] + [place.send(early, k) for k in range(1, place.grp)]
    grp_ids = [item.reshape(-1)[:slots] for item in grp_early]
    looked_up = fetch(grp_ids, 0)
    early_all = jnp.stack(in_order(grp_early, place.g))
    early_all = gather_stage(place, early_all, place.y_masks, place.y)
    early_all = gather_stage(place, early_all, place.z_masks, place.z)
    early_all = early_all.reshape(place.count, -1)
    ids_all = early_all[:, :slots]
    at = slots
    false_neg_all = early_all[:, at : at + pairs_here * total_pairs].reshape(
        total_pairs, total_pairs
    )
    at += pairs_here * total_pairs
    valid_all = early_all[:, at : at + pairs_here].reshape(-1)
    at += pairs_here
    rounds = jnp.max(early_all[:, at]) // room + 1

    def look_up_all():
        whole = lax.all_gather(word_table, "grp", axis=0, tiled=True)
        return jnp.arange(tokens, dtype=jnp.int32), whole[flat_ids]

    slot, found = lax.cond(
        rounds > 1, look_up_all, lambda: (lookup_slots(0).astype(jnp.int32), looked_up)
    )
    (
        unit1,
        inverse1,
        normed_low,
        projected,
        probs,
        attended,
        unit2,
        inverse2,
        middle_low,
        activated_low,
        slope,
        unit3,
        inverse3,
        pooled,
        own_embed,
    ) = forward(
        lengths_flat,
        slot[:, None],
        found,
        small_rows,
        (qkv_weight, out_weight, up_weight, down_weight),
        seq_len,
        head_dim,
    )

    gathered = gather_far_first(place, own_embed).reshape(total_pairs, 2, width)
    queries, documents = gathered[:, 0], gathered[:, 1]
    diagonal = jnp.arange(total_pairs)[:, None] == jnp.arange(total_pairs)[None, :]
    allowed = (valid_all[None, :] > 0) & ((false_neg_all == 0) | diagonal)
    scores = contract_cols(queries, documents) / logit_divisor_constant
    query_lse, query_probs = masked_softmax(scores, allowed)
    doc_lse, doc_probs = masked_softmax(scores.T, allowed)
    diag = jnp.sum(jnp.where(diagonal, scores, 0.0), -1)
    valid_floats = valid_all.astype(jnp.float32)
    pair_count = jnp.maximum(jnp.sum(valid_floats), 1.0)
    loss_total = jnp.sum(valid_floats * (query_lse + doc_lse - 2.0 * diag)) / 2.0
    row_weight = valid_floats / (2.0 * pair_count)
    identity_mask = diagonal.astype(jnp.float32)
    score_grad = (
        row_weight[:, None] * (query_probs - identity_mask)
        + (row_weight[:, None] * (doc_probs - identity_mask)).T
    )
    row_start = (place.b * place.grp + place.g) * pairs_here
    query_grad_rows = lax.dynamic_slice_in_dim(score_grad, row_start, pairs_here, 0)
    doc_grad_rows = lax.dynamic_slice_in_dim(score_grad, row_start, pairs_here, 1).T
    embed_grad = (
        jnp.stack(
            [
                jnp.dot(
                    query_grad_rows, documents.astype(jnp.float32), precision=finest_arithmetic
                ),
                jnp.dot(doc_grad_rows, queries.astype(jnp.float32), precision=finest_arithmetic),
            ],
            1,
        )
        / logit_divisor_constant
    )

    lowered_grad, lifted_low, second, feed_sums = feed_back(
        lengths_flat,
        embed_grad,
        (unit2, inverse2, slope, unit3, inverse3, pooled),
        small_rows,
        (up_weight, down_weight),
        seq_len,
    )
    group_one, _ = reduce_group(
        place, [(activated_low, lowered_grad), (middle_low, lifted_low)], None
    )
    second, group_one = lax.optimization_barrier((second, group_one))
    group_one = reduce_group_rest(place, group_one, 0)
    branch_grad, projected_grad, own_rows, position_grad, attention_sums = attention_back(
        gradient_slots(0),
        second,
        (projected, probs, unit1, inverse1),
        small_rows,
        (qkv_weight, out_weight),
        seq_len,
        head_dim,
        slots,
    )

    grid_ids = lax.dynamic_slice_in_dim(
        ids_all.reshape(place.blk, place.grp, place.blk, room), place.b, 1, 2
    )[:, :, 0]

    rows = own_rows.reshape(place.blk, room, width)
    arrived = [rows[0]] + [place.send(rows[k], k * place.grp) for k in range(1, place.blk)]
    halves = [jnp.concatenate(arrived[: place.far]), jnp.concatenate(arrived[place.far :])]
    over_x = [
        jnp.concatenate([halves[0], halves[1]])
        if mask == 0
        else jnp.concatenate([place.send(half, mask) for half in halves])
        for mask in place.x_masks
    ]
    over_core = [place.send(item, 1) for item in over_x]
    sources = [item for pair in zip(over_x, over_core) for item in pair]
    ids = jnp.stack(in_order([grid_ids[i] for i in range(place.blk)], place.b), 1)
    local = ids - place.b * shard_rows
    inside = ids >= 0
    counts = jnp.sum(inside.astype(jnp.int32), -1).reshape(-1)
    local = jnp.where(inside, local, shard_rows).reshape(-1)
    word_rows, word_squares = word_sum(
        place.g, counts, local, sources, shard_rows, place.blk, room
    )
    word_squares = jnp.sum(word_squares)

    def all_rows(carry):
        token_grads = attention_back(
            jnp.arange(tokens, dtype=jnp.int32) + carry[0],
            second,
            (projected, probs, unit1, inverse1),
            small_rows,
            (qkv_weight, out_weight),
            seq_len,
            head_dim,
            slots,
        )[2]
        every_id = lax.all_gather(flat_ids + carry[0], "blk", axis=0, tiled=True) - place.b * shard_rows
        every_row = lax.all_gather(token_grads, "blk", axis=0, tiled=True)
        inside = (every_id >= 0) & (every_id < shard_rows)
        total = (
            jnp.zeros((shard_rows, width), jnp.float32)
            .at[jnp.where(inside, every_id, shard_rows)]
            .add(every_row.astype(jnp.float32), mode="drop")
        )
        total = lax.psum(total, "grp")
        return (carry[0] + 1, total, jnp.sum(total * total))

    _, word_rows, word_squares = lax.while_loop(
        lambda carry: (carry[0] < 1) & (rounds > 1),
        all_rows,
        (jnp.int32(0), word_rows, word_squares),
    )

    small_grad = jnp.concatenate([position_grad, attention_sums[:4], feed_sums[:10]], 0)
    small_flat = small_grad.reshape(-1, strip)
    small_piece = -(-small_flat.shape[0] // (16 * place.count)) * 16
    small_padded = jnp.concatenate(
        [
            small_flat,
            jnp.zeros((small_piece * place.count - small_flat.shape[0], strip), jnp.float32),
        ]
    )
    small_parts = small_padded.reshape(place.blk, place.xs, 2, small_piece, strip)
    group_two, fine = reduce_group(
        place, [(normed_low, projected_grad), (attended, branch_grad)], small_parts
    )
    group_two = reduce_group_rest(place, group_two, fine)
    cut = group_two.shape[0] - small_piece
    small_own = group_two[cut:]
    matrix_own = jnp.concatenate([group_one, group_two[:cut]]).astype(jnp.bfloat16)
    gathered_grads = gather_stage(place, matrix_own, place.x_masks, place.x)
    gathered_grads = gather_stage(place, gathered_grads, place.core_masks, place.core)
    gathered_grads = jnp.swapaxes(gathered_grads, 0, 1)
    masters = (down_master, up_master, qkv_master, out_master)
    shards, at = [], 0
    for master in masters:
        rows, columns = master.shape[0] // place.xs, master.shape[1]
        length = rows * (columns // 2 // strip)
        shards.append(
            whole_rows(place, gathered_grads[:, :, at : at + length], rows, columns).astype(
                jnp.float32
            )
        )
        at += length

    matrix_floats = matrix_own.astype(jnp.float32)
    squares = (
        jnp.sum(matrix_floats * matrix_floats)
        + jnp.sum(small_own * small_own)
        + word_squares / place.grp
    )
    late = jnp.concatenate([small_own, jnp.full((8, strip), squares)])
    late = gather_far_first(place, late).reshape(place.count, -1, strip)
    small_total = late[:, :small_piece].reshape(-1, strip)[: small_flat.shape[0]]
    small_total = small_total.reshape(small_grad.shape)
    grad_norm = jnp.sqrt(jnp.sum(late[:, small_piece, 0]))
    factor = clip_bound / jnp.maximum(grad_norm, clip_bound)
    down_shard, up_shard, qkv_shard, out_shard = shards
    grads = (word_rows, qkv_shard, out_shard, up_shard, down_shard, small_total)
    parameters = (word_master, qkv_master, out_master, up_master, down_master, small_rows)
    moments = (word_moments, qkv_moments, out_moments, up_moments, down_moments, small_moments)
    results = []
    for grad, moment, master, rate in zip(grads, moments, parameters, rate_table):
        results.extend(adam_update(grad * factor, moment, master, rate))
    return (loss_total, pair_count, grad_norm, *results)


def solution(mesh):
    in_specs = (
        P(both, None, None),
        P(both, None),
        P(both),
        P(both, None),
        P("grp", None),
        P(),
        P(),
        P(),
        P(),
        P("blk", None),
        P("blk", None),
        P("blk", None),
        P("blk", None),
        P("blk", None),
        P(None, "blk", None),
        P(None, "blk", None),
        P(None, "blk", None),
        P(None, "blk", None),
        P(None, "blk", None),
        P(),
        P(),
    )
    out_specs = (P(), P(), P()) + (P("blk", None),) * 15 + (P(), P(), P())
    return jax.shard_map(
        on_device, mesh=mesh, in_specs=in_specs, out_specs=out_specs, check_vma=False
    )
```

time: 754 us -> 555 us (0.74)
  matrix products: 171 us -> 0.76 us
  Pallas kernels: 0 us -> 156 us
  local copies, waits for them, and re-layouts: 155 us -> 46.9 us
  other arithmetic: 188 us -> 84.1 us
  waiting for transfers between devices: 126 us -> 162 us
  between operations: 13.2 us -> 25.9 us
  starting transfers between devices: 81.9 us -> 73 us
  loops' own time: 9.1 us -> 0.24 us
    pallas_call x0 -> x6, Pallas kernels: none -> 156 us  [the longest x1 44 us: forward(): pl.pallas_call(functools.partial(forward_kernel, seq_len=seq_len, seqs=se...]
    dot_general x20 -> x0, matrix products: 130 us -> none  [the longest x8 37.6 us: contract_rows(): lax.dot_general(left, right, (((0,), (0,)), ((), ())), preferred_element_...]
    dot_general x5 -> x1, matrix products: 38.1 us -> 0.24 us  [contract_cols(): lax.dot_general(left, right, (((1,), (1,)), ((), ())), preferred_element_...]
    ppermute x57 -> x59, waiting for transfers between devices: 126 us -> 162 us  [send(): return lax.ppermute(value, both, pairs)]
    scatter-add x1 -> x0, other arithmetic: 32.8 us -> none  [word_rows_of(): held.at[jnp.where(inside, local, shard_rows)]]
    reduce_sum x18 -> x1, other arithmetic: 30.7 us -> 1.3 us  [on_device(): word_squares = jnp.sum(word_squares)]
    unnamed x316 -> x77, local copies, waits for them, and re-layouts: 41.1 us -> 15.2 us
    convert_element_type x18 -> x12, other arithmetic: 24.3 us -> 1.11 us  [the longest x6 0.75 us: from_sent(): value = value.astype(jnp.float32)]
  transfers between devices with their start and end apart: 57 -> 59, of which waited for: 27 -> 33; matrix products, arithmetic and copies ran while one was open for 25% -> 14% of each run, Pallas kernels for 0% -> 5%
where the time goes in v2:
time: 555 us; the launch traced here: 549 us
  waiting for transfers between devices  162 us (29%)
  Pallas kernels  156 us (28%)
  other arithmetic  84.1 us (15%)
  starting transfers between devices  73 us (13%)
  local copies, waits for them, and re-layouts  46.9 us (8%)
  between operations  25.9 us (5%)
    ppermute x59, waiting for transfers between devices, send(): return lax.ppermute(value, both, pairs)  162 us
    ppermute x59, starting transfers between devices, send(): return lax.ppermute(value, both, pairs)  73 us
    pallas_call x1, Pallas kernels, forward(): pl.pallas_call(functools.partial(forward_kernel, seq_len=seq_len, seqs=se...  44 us
    sub x6, other arithmetic, adam_update(): master - rate * (first_hat / (jnp.sqrt(second_hat) + epsilon) + decay_wei...  39.2 us
    pallas_call x2, Pallas kernels, weight_grads(): pl.pallas_call(functools.partial(weight_grad_kernel, jobs=jobs, xs=place....  34.8 us
    pallas_call x1, Pallas kernels, attention_back(): pl.pallas_call(functools.partial(attention_back_kernel, seq_len=seq_len,...  30.7 us
    pallas_call x1, Pallas kernels, word_sum(): pl.pallas_call(functools.partial(word_sum_kernel, grp=grp, blk=blk, room=...  25.9 us
    pallas_call x1, Pallas kernels, feed_back(): pl.pallas_call(functools.partial(feed_back_kernel, seq_len=seq_len, seqs=...  20.5 us
  transfers between devices with their start and end apart: 59, of which 33 were waited for; matrix products, arithmetic and copies ran while one was open for 14% of the time, Pallas kernels for 5%

profile of v2, /device:TPU:0, one launch (start us, length us, event | category | flops | bytes accessed | tf_op | source)
XLA Modules:
  0.0 549.0 jit_solution(12595002236852919049)
XLA Ops:
  23.3 10.3 %gather_fusion.1 = bf16[1024,768]{1,0:T(8,128)(2,1)S(1)} fusion(bf16[7680,768]{1,0:T(8,128)(2,1)} %param.29, s32[1024]{0:T(1024)S(1)} %broadcast_clamp_fusion), kind=kCustom, calls=%fused_computation.1 | custom fusion | bytes 3149824 | tf_op jit(solution)/shard_map/gather | solution.py:914
  33.7 3.7 collective-permute-start.4
  46.1 4.5 collective-permute-done.9
  50.6 6.8 %collective-permute-done.8 = bf16[256,768]{1,0:T(8,128)(2,1)S(1)} collective-permute-done((bf16[256,768]{1,0:T(8,128)(2,1)S(1)}, bf16[256,768]{1,0:T(8,128)(2,1)S(1)}, u32[]{:S(2)}, u32[]{:S(2)}) %collective-permute-start.8) | collective-permute-done | bytes 393248 | tf_op jit(solution)/shard_map/ppermute | solution.py:724
  61.1 44.0 %encoder_forward.1 = (f32[1024,768]{1,0:T(8,128)}, f32[1024,1]{1,0:T(8,128)}, bf16[1024,768]{1,0:T(8,128)(2,1)}, bf16[1024,2304]{1,0:T(8,128)(2,1)}, bf16[8,6,25...) custom-call(s32[8]{0:T(128)} %reshape.973.lengths_ref, ...), custom_call_target="tpu_custom_call" | custom-call | flops 20000000000 | bytes 50000000 | tf_op jit(solution)/shard_map/encoder_forward/pallas_call | solution.py:252
  105.2 3.7 collective-permute-start.10
  110.9 2.7 collective-permute-done.11
  130.3 20.5 %feed_back.1 = (bf16[1024,768]{1,0:T(8,128)(2,1)}, bf16[1024,3072]{1,0:T(8,128)(2,1)}, f32[1024,768]{1,0:T(8,128)}, f32[16,768]{1,0:T(8,128)}) custom-call(s32[8]{0:T(128)} %reshape.973.lengths_ref, f32[4,2,768]{2,1,0:T(2,128)} %maximum_multiply_fusion.embed_grad_ref, f32[4,2,768]{2,1,0:T(2,128)} %get-tuple-element.250.pooled_ref, ...), custom_call_target="tpu_custom_call" | custom-call | flops 10000000000 | bytes 40000000 | tf_op jit(solution)/shard_map/feed_back/pallas_call | solution.py:343
  150.8 22.0 %weight_grads.2 = (bf16[8,2,384,384]{3,2,1,0:T(8,128)(2,1)}, f32[8,2,384,384]{3,2,1,0:T(8,128)}) custom-call(s32[1]{0:T(128)} %bitcast.37.core_ref, bf16[1024,3072]{1,0:T(8,128)(2,1)} %get-tuple-element.257.refs_0_, bf16[1024,768]{1,0:T(8,128)(2,1)} %get-tuple-element.258.refs_1_, bf16[1024,768]{1,0:T(8,128)(2,1)} %get-tuple-element.259.refs_2_, ...), custom_call_target="tpu_custom_call" | custom-call | flops 9663676416 | bytes 16000000 | tf_op jit(solution)/shard_map/weight_grads/pallas_call | solution.py:593
  175.1 6.0 %collective-permute-done.17 = bf16[8,2,384,384]{3,2,1,0:T(8,128)(2,1)} collective-permute-done((bf16[8,2,384,384]{3,2,1,0:T(8,128)(2,1)}, bf16[8,2,384,384]{3,2,1,0:T(8,128)(2,1)}, u32[]{:S(2)}, u32[]{:S(2)}) %collective-permute-start.17) | collective-permute-done | bytes 4718624 | tf_op jit(solution)/shard_map/ppermute | solution.py:724
  181.1 9.9 %convert_add_fusion = f32[8,2,384,384]{3,2,1,0:T(8,128)} fusion(f32[8,2,384,384]{3,2,1,0:T(8,128)} %get-tuple-element.261, bf16[8,2,384,384]{3,2,1,0:T(8,128)(2,1)} %collective-permute-done.17), kind=kLoop, calls=%fused_computation.36 | loop fusion | flops 4718592 | bytes 23592960 | tf_op jit(solution)/shard_map/add | solution.py:824
  191.1 30.7 %attention_back.4 = (bf16[1024,768]{1,0:T(8,128)(2,1)}, bf16[1024,2304]{1,0:T(8,128)(2,1)}, bf16[1024,768]{1,0:T(8,128)(2,1)}, f32[128,768]{1,0:T(8,128)}, f32[8,768]{1,0:T(8,128)}) custom-call(s32[4,1,256]{2,1,0:T(1,128)} %and_select_fusion.slots_ref, f32[1024,768]{1,0:T(8,128)} %get-tuple-element.549.second_ref, ...), custom_call_target="tpu_custom_call" | custom-call | flops 10000000000 | bytes 30000000 | tf_op jit(solution)/shard_map/attention_back/pallas_call | solution.py:484
  223.7 12.8 %weight_grads.3 = (bf16[8,2,192,384]{3,2,1,0:T(8,128)(2,1)}, f32[8,2,192,384]{3,2,1,0:T(8,128)}) custom-call(s32[1]{0:T(128)} %bitcast.37.core_ref, bf16[1024,768]{1,0:T(8,128)(2,1)} %get-tuple-element.249.refs_0_, bf16[1024,2304]{1,0:T(8,128)(2,1)} %get-tuple-element.268.refs_1_, bf16[1024,768]{1,0:T(8,128)(2,1)} %get-tuple-element.269.refs_2_, ...), custom_call_target="tpu_custom_call" | custom-call | flops 4831838208 | bytes 16000000 | tf_op jit(solution)/shard_map/weight_grads/pallas_call | solution.py:593
  238.7 4.4 fusion.96
  246.6 29.3 %collective-permute-done.39 = bf16[128,768]{1,0:T(8,128)(2,1)S(1)} collective-permute-done((bf16[128,768]{1,0:T(8,128)(2,1)S(1)}, bf16[128,768]{1,0:T(8,128)(2,1)S(1)}, u32[]{:S(2)}, u32[]{:S(2)}) %collective-permute-start.39) | collective-permute-done | bytes 196640 | tf_op jit(solution)/shard_map/ppermute | solution.py:724
  279.2 8.1 %collective-permute-done.41 = bf16[128,768]{1,0:T(8,128)(2,1)S(1)} collective-permute-done((bf16[128,768]{1,0:T(8,128)(2,1)S(1)}, bf16[128,768]{1,0:T(8,128)(2,1)S(1)}, u32[]{:S(2)}, u32[]{:S(2)}) %collective-permute-start.41) | collective-permute-done | bytes 196640 | tf_op jit(solution)/shard_map/ppermute | solution.py:724
  288.0 10.5 %collective-permute-start.44 = (bf16[128,768]{1,0:T(8,128)(2,1)S(1)}, bf16[128,768]{1,0:T(8,128)(2,1)S(1)}, u32[]{:S(2)}, u32[]{:S(2)}) collective-permute-start(bf16[128,768]{1,0:T(8,128)(2,1)S(1)} %get-tuple-element.364), channel_id=1, source_target_pairs={{0,24},{1,25},{2,26},{3,27},{4,28},{5,29},{6,30},{7,31},{8,16},{9,... | collective-permute-start | bytes 589832 | tf_op jit(solution)/shard_map/ppermute | solution.py:724
  305.1 5.9 %collective-permute-done.45 = bf16[128,768]{1,0:T(8,128)(2,1)S(1)} collective-permute-done((bf16[128,768]{1,0:T(8,128)(2,1)S(1)}, bf16[128,768]{1,0:T(8,128)(2,1)S(1)}, u32[]{:S(2)}, u32[]{:S(2)}) %collective-permute-start.45) | collective-permute-done | bytes 196640 | tf_op jit(solution)/shard_map/ppermute | solution.py:724
  314.7 17.5 %collective-permute-done.47 = bf16[512,768]{1,0:T(8,128)(2,1)S(1)} collective-permute-done((bf16[512,768]{1,0:T(8,128)(2,1)S(1)}, bf16[512,768]{1,0:T(8,128)(2,1)S(1)}, u32[]{:S(2)}, u32[]{:S(2)}) %collective-permute-start.47) | collective-permute-done | bytes 786464 | tf_op jit(solution)/shard_map/ppermute | solution.py:724
  334.0 15.0 %collective-permute-done.48 = bf16[512,768]{1,0:T(8,128)(2,1)S(1)} collective-permute-done((bf16[512,768]{1,0:T(8,128)(2,1)S(1)}, bf16[512,768]{1,0:T(8,128)(2,1)S(1)}, u32[]{:S(2)}, u32[]{:S(2)}) %collective-permute-start.48) | collective-permute-done | bytes 786464 | tf_op jit(solution)/shard_map/ppermute | solution.py:724
  349.2 12.1 %collective-permute-done.30 = bf16[4,192,384]{2,1,0:T(8,128)(2,1)S(1)} collective-permute-done((bf16[4,192,384]{2,1,0:T(8,128)(2,1)S(1)}, bf16[4,192,384]{2,1,0:T(8,128)(2,1)S(1)}, u32[]{:S(2)}, u32[]{:S(2)}) %collective-permute-start.30) | collective-permute-done | bytes 589856 | tf_op jit(solution)/shard_map/ppermute | solution.py:724
  361.5 5.1 collective-permute-start.33
  371.8 3.6 collective-permute-start.28
  375.4 7.6 %collective-permute-done.32 = bf16[192,384]{1,0:T(8,128)(2,1)S(1)} collective-permute-done((bf16[192,384]{1,0:T(8,128)(2,1)S(1)}, bf16[192,384]{1,0:T(8,128)(2,1)S(1)}, u32[]{:S(2)}, u32[]{:S(2)}) %collective-permute-start.32) | collective-permute-done | bytes 147488 | tf_op jit(solution)/shard_map/ppermute | solution.py:724
  385.3 4.8 collective-permute-start.26
  397.1 25.9 %word_sum.1 = (f32[3840,768]{1,0:T(8,128)}, f32[1,768]{1,0:T(1,128)}) custom-call(s32[1]{0:T(128)} %bitcast.83.place_ref, s32[32]{0:T(128)} %reshape.983.count_ref, s32[4096]{0:T(1024)} %get-tuple-element.434.id_ref, bf16[1024,768]{1,0:T(8,128)(2,1)} %constant_dynamic-update-slice_fusion.refs_0_, bf16[1024,768]{1,0:T(8,128)(2,1)} %collective-permute-done.46.refs_1_, ...), custom_call_target="tpu_custom_call" | custom-call | flops 10000000 | bytes 40000000 | tf_op jit(solution)/shard_map/word_sum/pallas_call | solution.py:682
  427.2 7.4 %collective-permute-done.35 = bf16[4,96,384]{2,1,0:T(8,128)(2,1)S(1)} collective-permute-done((bf16[4,96,384]{2,1,0:T(8,128)(2,1)S(1)}, bf16[4,96,384]{2,1,0:T(8,128)(2,1)S(1)}, u32[]{:S(2)}, u32[]{:S(2)}) %collective-permute-start.35) | collective-permute-done | bytes 294944 | tf_op jit(solution)/shard_map/ppermute | solution.py:724
  449.6 2.9 collective-permute-done.23
  457.7 2.8 collective-permute-start.50
  474.0 2.9 collective-permute-done.55
  479.2 3.9 collective-permute-done.57
  486.9 30.1 %multiply_subtract_fusion = (f32[3840,768]{1,0:T(8,128)}, f32[3840,768]{1,0:T(8,128)}, f32[3840,768]{1,0:T(8,128)}) fusion(f32[3840,768]{1,0:T(8,128)} %param.34, f32[3840,768]{1,0:T(8,128)} %get-tuple-element.281, f32[]{:T(128)S(6)} %div.191, f32[2,3840,768]{2,1,0:T(8,128)} %param.39), kind=kLoop, calls=%fused_computation.35 | loop fusion | flops 44236800 | bytes 82575360 | tf_op jit(solution)/shard_map/sub | solution.py:43
  (352 shorter events, 146.0 us)
Async XLA Ops:
  21.4 12.2 %collective-permute-start.3 = (s32[4,16,128]{2,1,0:T(8,128)S(1)}, s32[4,16,128]{2,1,0:T(8,128)S(1)}, u32[]{:S(2)}, u32[]{:S(2)}) collective-permute-start(s32[4,16,128]{2,1,0:T(8,128)S(1)} %pad_add_fusion.2), channel_id=1, source_target_pairs={{0,4},{1,5},{2,6},{3,7},{4,0},{5,1},{6,2},{7,3},{8,12},{9,13},{10,... | collective-permute-start | bytes 98312 | tf_op jit(solution)/shard_map/ppermute | solution.py:724
  39.0 11.6 %collective-permute-start.9 = (bf16[256,768]{1,0:T(8,128)(2,1)}, bf16[256,768]{1,0:T(8,128)(2,1)S(1)}, u32[]{:S(2)}, u32[]{:S(2)}) collective-permute-start(bf16[256,768]{1,0:T(8,128)(2,1)} %get-tuple-element.373), channel_id=1, source_target_pairs={{0,3},{1,2},{2,1},{3,0},{4,7},{5,6},{6,5},{7,4},{8,11},{9,10},{10,... | collective-permute-start | bytes 1179656 | tf_op jit(solution)/shard_map/ppermute | solution.py:724
  39.0 18.4 %collective-permute-start.8 = (bf16[256,768]{1,0:T(8,128)(2,1)S(1)}, bf16[256,768]{1,0:T(8,128)(2,1)S(1)}, u32[]{:S(2)}, u32[]{:S(2)}) collective-permute-start(bf16[256,768]{1,0:T(8,128)(2,1)S(1)} %get-tuple-element.371), channel_id=1, source_target_pairs={{0,2},{1,3},{2,0},{3,1},{4,6},{5,7},{6,4},{7,5},{8,10},{9,11},{10,... | collective-permute-start | bytes 1179656 | tf_op jit(solution)/shard_map/ppermute | solution.py:724
  40.3 17.0 %collective-permute-start.7 = (bf16[256,768]{1,0:T(8,128)(2,1)S(1)}, bf16[256,768]{1,0:T(8,128)(2,1)S(1)}, u32[]{:S(2)}, u32[]{:S(2)}) collective-permute-start(bf16[256,768]{1,0:T(8,128)(2,1)S(1)} %get-tuple-element.372), channel_id=1, source_target_pairs={{0,1},{1,0},{2,3},{3,2},{4,5},{5,4},{6,7},{7,6},{8,9},{9,8},{10,11... | collective-permute-start | bytes 1179656 | tf_op jit(solution)/shard_map/ppermute | solution.py:724
  238.5 128.6 %collective-permute-start.18 = (bf16[8,2,224,384]{3,2,1,0:T(8,128)(2,1)S(1)}, bf16[8,2,224,384]{3,2,1,0:T(8,128)(2,1)S(1)}, u32[]{:S(2)}, u32[]{:S(2)}) collective-permute-start(bf16[8,2,224,384]{3,2,1,0:T(8,128)(2,1)S(1)} %pad_maximum_fusion), channel_id=1, source_target_pairs={{0,1},{1,0},{2,3},{3,2},{4,5},{5,4},{6,7},{7,6},{8,9},{9,8},{10,11... | collective-permute-start | bytes 8257544 | tf_op jit(solution)/shard_map/ppermute | solution.py:724
  243.3 68.6 %collective-permute-start.29 = (bf16[4,2,192,384]{3,2,0,1:T(8,128)(2,1)S(1)}, bf16[4,2,192,384]{3,2,0,1:T(8,128)(2,1)S(1)}, u32[]{:S(2)}, u32[]{:S(2)}) collective-permute-start(bf16[4,2,192,384]{3,2,0,1:T(8,128)(2,1)S(1)} %fusion.21), channel_id=1, source_target_pairs={{0,4},{1,5},{2,6},{3,7},{4,0},{5,1},{6,2},{7,3},{8,12},{9,13},{10,... | collective-permute-start | bytes 3538952 | tf_op jit(solution)/shard_map/ppermute | solution.py:724
  245.3 30.5 %collective-permute-start.39 = (bf16[128,768]{1,0:T(8,128)(2,1)S(1)}, bf16[128,768]{1,0:T(8,128)(2,1)S(1)}, u32[]{:S(2)}, u32[]{:S(2)}) collective-permute-start(bf16[128,768]{1,0:T(8,128)(2,1)S(1)} %get-tuple-element.369), channel_id=1, source_target_pairs={{0,4},{1,5},{2,6},{3,7},{4,0},{5,1},{6,2},{7,3},{8,12},{9,13},{10,... | collective-permute-start | bytes 589832 | tf_op jit(solution)/shard_map/ppermute | solution.py:724
  246.4 67.9 %collective-permute-start.24 = (bf16[4,2,192,384]{3,2,0,1:T(8,128)(2,1)S(1)}, bf16[4,2,192,384]{3,2,0,1:T(8,128)(2,1)S(1)}, u32[]{:S(2)}, u32[]{:S(2)}) collective-permute-start(bf16[4,2,192,384]{3,2,0,1:T(8,128)(2,1)S(1)} %fusion.20), channel_id=1, source_target_pairs={{0,2},{1,3},{2,0},{3,1},{4,6},{5,7},{6,4},{7,5},{8,10},{9,11},{10,... | collective-permute-start | bytes 3538952 | tf_op jit(solution)/shard_map/ppermute | solution.py:724
  246.4 30.1 %collective-permute-start.40 = (bf16[128,768]{1,0:T(8,128)(2,1)S(1)}, bf16[128,768]{1,0:T(8,128)(2,1)S(1)}, u32[]{:S(2)}, u32[]{:S(2)}) collective-permute-start(bf16[128,768]{1,0:T(8,128)(2,1)S(1)} %get-tuple-element.368), channel_id=1, source_target_pairs={{0,8},{1,9},{2,10},{3,11},{4,12},{5,13},{6,14},{7,15},{8,0},{9,1},... | collective-permute-start | bytes 589832 | tf_op jit(solution)/shard_map/ppermute | solution.py:724
  275.8 11.5 %collective-permute-start.41 = (bf16[128,768]{1,0:T(8,128)(2,1)S(1)}, bf16[128,768]{1,0:T(8,128)(2,1)S(1)}, u32[]{:S(2)}, u32[]{:S(2)}) collective-permute-start(bf16[128,768]{1,0:T(8,128)(2,1)S(1)} %get-tuple-element.367), channel_id=1, source_target_pairs={{0,12},{1,13},{2,14},{3,15},{4,8},{5,9},{6,10},{7,11},{8,4},{9,5},... | collective-permute-start | bytes 589832 | tf_op jit(solution)/shard_map/ppermute | solution.py:724
  276.5 11.5 %collective-permute-start.42 = (bf16[128,768]{1,0:T(8,128)(2,1)S(1)}, bf16[128,768]{1,0:T(8,128)(2,1)S(1)}, u32[]{:S(2)}, u32[]{:S(2)}) collective-permute-start(bf16[128,768]{1,0:T(8,128)(2,1)S(1)} %get-tuple-element.366), channel_id=1, source_target_pairs={{0,16},{1,17},{2,18},{3,19},{4,20},{5,21},{6,22},{7,23},{8,24},{9,... | collective-permute-start | bytes 589832 | tf_op jit(solution)/shard_map/ppermute | solution.py:724
  287.3 14.2 %collective-permute-start.43 = (bf16[128,768]{1,0:T(8,128)(2,1)S(1)}, bf16[128,768]{1,0:T(8,128)(2,1)S(1)}, u32[]{:S(2)}, u32[]{:S(2)}) collective-permute-start(bf16[128,768]{1,0:T(8,128)(2,1)S(1)} %get-tuple-element.365), channel_id=1, source_target_pairs={{0,20},{1,21},{2,22},{3,23},{4,16},{5,17},{6,18},{7,19},{8,28},{9,... | collective-permute-start | bytes 589832 | tf_op jit(solution)/shard_map/ppermute | solution.py:724
  288.0 16.3 %collective-permute-start.44 = (bf16[128,768]{1,0:T(8,128)(2,1)S(1)}, bf16[128,768]{1,0:T(8,128)(2,1)S(1)}, u32[]{:S(2)}, u32[]{:S(2)}) collective-permute-start(bf16[128,768]{1,0:T(8,128)(2,1)S(1)} %get-tuple-element.364), channel_id=1, source_target_pairs={{0,24},{1,25},{2,26},{3,27},{4,28},{5,29},{6,30},{7,31},{8,16},{9,... | collective-permute-start | bytes 589832 | tf_op jit(solution)/shard_map/ppermute | solution.py:724
  301.5 9.5 %collective-permute-start.45 = (bf16[128,768]{1,0:T(8,128)(2,1)S(1)}, bf16[128,768]{1,0:T(8,128)(2,1)S(1)}, u32[]{:S(2)}, u32[]{:S(2)}) collective-permute-start(bf16[128,768]{1,0:T(8,128)(2,1)S(1)} %get-tuple-element.363), channel_id=1, source_target_pairs={{0,28},{1,29},{2,30},{3,31},{4,24},{5,25},{6,26},{7,27},{8,20},{9,... | collective-permute-start | bytes 589832 | tf_op jit(solution)/shard_map/ppermute | solution.py:724
  311.7 84.3 %collective-permute-start.46 = (bf16[1024,768]{1,0:T(8,128)(2,1)}, bf16[1024,768]{1,0:T(8,128)(2,1)}, u32[]{:S(2)}, u32[]{:S(2)}) collective-permute-start(bf16[1024,768]{1,0:T(8,128)(2,1)} %constant_dynamic-update-slice_fusion.refs_0_), channel_id=1, source_target_pairs={{0,1},{1,0},{2,3},{3,2},{4,5},{5,4},{6,7},{7,6},{8,9},{9,8},{10,11... | collective-permute-start | bytes 4718600 | tf_op jit(solution)/shard_map/ppermute | solution.py:724
  311.8 20.4 %collective-permute-start.47 = (bf16[512,768]{1,0:T(8,128)(2,1)S(1)}, bf16[512,768]{1,0:T(8,128)(2,1)S(1)}, u32[]{:S(2)}, u32[]{:S(2)}) collective-permute-start(bf16[512,768]{1,0:T(8,128)(2,1)S(1)} %pad_maximum_fusion.5), channel_id=1, source_target_pairs={{0,2},{1,3},{2,0},{3,1},{4,6},{5,7},{6,4},{7,5},{8,10},{9,11},{10,... | collective-permute-start | bytes 2359304 | tf_op jit(solution)/shard_map/ppermute | solution.py:724
  311.9 37.1 %collective-permute-start.48 = (bf16[512,768]{1,0:T(8,128)(2,1)S(1)}, bf16[512,768]{1,0:T(8,128)(2,1)S(1)}, u32[]{:S(2)}, u32[]{:S(2)}) collective-permute-start(bf16[512,768]{1,0:T(8,128)(2,1)S(1)} %pad_maximum_fusion.6), channel_id=1, source_target_pairs={{0,2},{1,3},{2,0},{3,1},{4,6},{5,7},{6,4},{7,5},{8,10},{9,11},{10,... | collective-permute-start | bytes 2359304 | tf_op jit(solution)/shard_map/ppermute | solution.py:724
  314.3 47.0 %collective-permute-start.30 = (bf16[4,192,384]{2,1,0:T(8,128)(2,1)S(1)}, bf16[4,192,384]{2,1,0:T(8,128)(2,1)S(1)}, u32[]{:S(2)}, u32[]{:S(2)}) collective-permute-start(bf16[4,192,384]{2,1,0:T(8,128)(2,1)S(1)} %fusion.24), channel_id=1, source_target_pairs={{0,2},{1,3},{2,0},{3,1},{4,6},{5,7},{6,4},{7,5},{8,10},{9,11},{10,... | collective-permute-start | bytes 1769480 | tf_op jit(solution)/shard_map/ppermute | solution.py:724
  332.2 34.4 %collective-permute-start.25 = (bf16[4,192,384]{2,1,0:T(8,128)(2,1)S(1)}, bf16[4,192,384]{2,1,0:T(8,128)(2,1)S(1)}, u32[]{:S(2)}, u32[]{:S(2)}) collective-permute-start(bf16[4,192,384]{2,1,0:T(8,128)(2,1)S(1)} %fusion.23), channel_id=1, source_target_pairs={{0,4},{1,5},{2,6},{3,7},{4,0},{5,1},{6,2},{7,3},{8,12},{9,13},{10,... | collective-permute-start | bytes 1769480 | tf_op jit(solution)/shard_map/ppermute | solution.py:724
  349.1 46.9 %collective-permute-start.49 = (bf16[1024,768]{1,0:T(8,128)(2,1)S(1)}, bf16[1024,768]{1,0:T(8,128)(2,1)S(1)}, u32[]{:S(2)}, u32[]{:S(2)}) collective-permute-start(bf16[1024,768]{1,0:T(8,128)(2,1)S(1)} %constant_dynamic-update-slice_fusion.8.refs_2_), channel_id=1, source_target_pairs={{0,1},{1,0},{2,3},{3,2},{4,5},{5,4},{6,7},{7,6},{8,9},{9,8},{10,11... | collective-permute-start | bytes 4718600 | tf_op jit(solution)/shard_map/ppermute | solution.py:724
  361.5 10.3 %collective-permute-start.33 = (bf16[192,384]{1,0:T(8,128)(2,1)S(1)}, bf16[192,384]{1,0:T(8,128)(2,1)S(1)}, u32[]{:S(2)}, u32[]{:S(2)}) collective-permute-start(bf16[192,384]{1,0:T(8,128)(2,1)S(1)} %get-tuple-element.380), channel_id=1, source_target_pairs={{0,24},{1,25},{2,26},{3,27},{4,28},{5,29},{6,30},{7,31},{8,16},{9,... | collective-permute-start | bytes 442376 | tf_op jit(solution)/shard_map/ppermute | solution.py:724
  366.5 16.5 %collective-permute-start.32 = (bf16[192,384]{1,0:T(8,128)(2,1)S(1)}, bf16[192,384]{1,0:T(8,128)(2,1)S(1)}, u32[]{:S(2)}, u32[]{:S(2)}) collective-permute-start(bf16[192,384]{1,0:T(8,128)(2,1)S(1)} %get-tuple-element.381), channel_id=1, source_target_pairs={{0,16},{1,17},{2,18},{3,19},{4,20},{5,21},{6,22},{7,23},{8,24},{9,... | collective-permute-start | bytes 442376 | tf_op jit(solution)/shard_map/ppermute | solution.py:724
  367.1 16.8 %collective-permute-start.31 = (bf16[192,384]{1,0:T(8,128)(2,1)S(1)}, bf16[192,384]{1,0:T(8,128)(2,1)S(1)}, u32[]{:S(2)}, u32[]{:S(2)}) collective-permute-start(bf16[192,384]{1,0:T(8,128)(2,1)S(1)} %get-tuple-element.379), channel_id=1, source_target_pairs={{0,8},{1,9},{2,10},{3,11},{4,12},{5,13},{6,14},{7,15},{8,0},{9,1},... | collective-permute-start | bytes 442376 | tf_op jit(solution)/shard_map/ppermute | solution.py:724
  371.8 13.6 %collective-permute-start.28 = (bf16[192,384]{1,0:T(8,128)(2,1)S(1)}, bf16[192,384]{1,0:T(8,128)(2,1)S(1)}, u32[]{:S(2)}, u32[]{:S(2)}) collective-permute-start(bf16[192,384]{1,0:T(8,128)(2,1)S(1)} %get-tuple-element.377), channel_id=1, source_target_pairs={{0,24},{1,25},{2,26},{3,27},{4,28},{5,29},{6,30},{7,31},{8,16},{9,... | collective-permute-start | bytes 442376 | tf_op jit(solution)/shard_map/ppermute | solution.py:724
  383.0 9.5 %collective-permute-start.27 = (bf16[192,384]{1,0:T(8,128)(2,1)S(1)}, bf16[192,384]{1,0:T(8,128)(2,1)S(1)}, u32[]{:S(2)}, u32[]{:S(2)}) collective-permute-start(bf16[192,384]{1,0:T(8,128)(2,1)S(1)} %get-tuple-element.378), channel_id=1, source_target_pairs={{0,16},{1,17},{2,18},{3,19},{4,20},{5,21},{6,22},{7,23},{8,24},{9,... | collective-permute-start | bytes 442376 | tf_op jit(solution)/shard_map/ppermute | solution.py:724
  383.9 40.4 %collective-permute-start.34 = (bf16[4,2,96,384]{3,2,0,1:T(8,128)(2,1)}, bf16[4,2,96,384]{3,2,0,1:T(8,128)(2,1)}, u32[]{:S(2)}, u32[]{:S(2)}) collective-permute-start(bf16[4,2,96,384]{3,2,0,1:T(8,128)(2,1)} %fusion.25), channel_id=1, source_target_pairs={{0,2},{1,3},{2,0},{3,1},{4,6},{5,7},{6,4},{7,5},{8,10},{9,11},{10,... | collective-permute-start | bytes 1769480 | tf_op jit(solution)/shard_map/ppermute | solution.py:724
  385.3 9.9 %collective-permute-start.26 = (bf16[192,384]{1,0:T(8,128)(2,1)S(1)}, bf16[192,384]{1,0:T(8,128)(2,1)S(1)}, u32[]{:S(2)}, u32[]{:S(2)}) collective-permute-start(bf16[192,384]{1,0:T(8,128)(2,1)S(1)} %get-tuple-element.376), channel_id=1, source_target_pairs={{0,8},{1,9},{2,10},{3,11},{4,12},{5,13},{6,14},{7,15},{8,0},{9,1},... | collective-permute-start | bytes 442376 | tf_op jit(solution)/shard_map/ppermute | solution.py:724
  392.5 33.5 %collective-permute-start.19 = (bf16[4,2,128,384]{3,2,1,0:T(8,128)(2,1)}, bf16[4,2,128,384]{3,2,1,0:T(8,128)(2,1)S(1)}, u32[]{:S(2)}, u32[]{:S(2)}) collective-permute-start(bf16[4,2,128,384]{3,2,1,0:T(8,128)(2,1)} %pad_maximum_fusion.4), channel_id=1, source_target_pairs={{0,4},{1,5},{2,6},{3,7},{4,0},{5,1},{6,2},{7,3},{8,12},{9,13},{10,... | collective-permute-start | bytes 2359304 | tf_op jit(solution)/shard_map/ppermute | solution.py:724
  426.6 18.0 %collective-permute-start.20 = (bf16[4,128,384]{2,1,0:T(8,128)(2,1)S(1)}, bf16[4,128,384]{2,1,0:T(8,128)(2,1)S(1)}, u32[]{:S(2)}, u32[]{:S(2)}) collective-permute-start(bf16[4,128,384]{2,1,0:T(8,128)(2,1)S(1)} %pad_maximum_fusion.11), channel_id=1, source_target_pairs={{0,2},{1,3},{2,0},{3,1},{4,6},{5,7},{6,4},{7,5},{8,10},{9,11},{10,... | collective-permute-start | bytes 1179656 | tf_op jit(solution)/shard_map/ppermute | solution.py:724
  467.9 9.0 %collective-permute-start.55 = (f32[4,24,384]{2,1,0:T(8,128)S(1)}, f32[4,24,384]{2,1,0:T(8,128)S(1)}, u32[]{:S(2)}, u32[]{:S(2)}) collective-permute-start(f32[4,24,384]{2,1,0:T(8,128)S(1)} %pad_maximum_fusion.13), channel_id=1, source_target_pairs={{0,2},{1,3},{2,0},{3,1},{4,6},{5,7},{6,4},{7,5},{8,10},{9,11},{10,... | collective-permute-start | bytes 442376 | tf_op jit(solution)/shard_map/ppermute | solution.py:724
  469.0 14.1 %collective-permute-start.57 = (bf16[576,384]{1,0:T(8,128)(2,1)S(1)}, bf16[576,384]{1,0:T(8,128)(2,1)}, u32[]{:S(2)}, u32[]{:S(2)}) collective-permute-start(bf16[576,384]{1,0:T(8,128)(2,1)S(1)} %get-tuple-element.344), channel_id=1, source_target_pairs={{0,2},{1,3},{2,0},{3,1},{4,6},{5,7},{6,4},{7,5},{8,10},{9,11},{10,... | collective-permute-start | bytes 1327112 | tf_op jit(solution)/shard_map/ppermute | solution.py:724
  485.2 34.1 %collective-permute-start.58 = (bf16[2,576,384]{2,1,0:T(8,128)(2,1)}, bf16[2,576,384]{2,1,0:T(8,128)(2,1)}, u32[]{:S(2)}, u32[]{:S(2)}) collective-permute-start(bf16[2,576,384]{2,1,0:T(8,128)(2,1)} %pad_maximum_fusion.3), channel_id=1, source_target_pairs={{0,1},{1,0},{2,3},{3,2},{4,5},{5,4},{6,7},{7,6},{8,9},{9,8},{10,11... | collective-permute-start | bytes 2654216 | tf_op jit(solution)/shard_map/ppermute | solution.py:724
  (59 other events, 351.5 us)

commit v3 on v2

--- a/solution.py
+++ b/solution.py
@@ -401,7 +401,8 @@
     out_ref,
     branch_ref,
     projected_grad_ref,
-    rows_ref,
+    mine_ref,
+    theirs_ref,
     positions_ref,
     sums_ref,
     total_ref,
@@ -467,7 +468,9 @@
 
     @pl.when(step == pl.num_programs(0) - 1)
     def _():
-        rows_ref[...] = total_ref[...].astype(low)
+        half = total_ref.shape[0] // 2
+        mine_ref[...] = total_ref[:half]
+        theirs_ref[...] = total_ref[half:].astype(low)
 
 
 def attention_back(slot, second, kept, small_rows, weights, seq_len, head_dim, slots):
@@ -488,7 +491,8 @@
         out_shape=[
             jax.ShapeDtypeStruct((tokens, width), low),
             jax.ShapeDtypeStruct((tokens, 3 * width), low),
-            jax.ShapeDtypeStruct((slots, width), low),
+            jax.ShapeDtypeStruct((slots // 2, width), jnp.float32),
+            jax.ShapeDtypeStruct((slots // 2, width), low),
             jax.ShapeDtypeStruct((seq_len, width), jnp.float32),
             jax.ShapeDtypeStruct((8, width), jnp.float32),
         ],
@@ -507,7 +511,8 @@
         out_specs=[
             rows_block(rows, width),
             rows_block(rows, 3 * width),
-            fixed((slots, width)),
+            fixed((slots // 2, width)),
+            fixed((slots // 2, width)),
             fixed((seq_len, width)),
             fixed((8, width)),
         ],
@@ -613,7 +618,7 @@
     )(place.core.reshape(1).astype(jnp.int32), *operands)
 
 
-def word_sum_kernel(place_ref, count_ref, id_ref, *refs, grp, blk, room, span):
+def word_sum_kernel(place_ref, count_ref, id_ref, *refs, grp, chunks, room, span):
     sources = refs[:grp]
     out_ref, squares_ref, total_ref, rows_ref, chunk_ref, in_sems, out_sem = refs[grp:]
     batch = 8
@@ -633,8 +638,8 @@
         copy.wait()
 
     def one_source(n, _):
-        slot = (n // blk) ^ place_ref[0]
-        start = (n % blk) * room
+        slot = (n // chunks) ^ place_ref[0]
+        start = (n % chunks) * room
         count = count_ref[n]
 
         def widen(i, _):
@@ -658,7 +663,7 @@
         lax.fori_loop(0, (count + batch - 1) // batch, add, 0)
         return 0
 
-    lax.fori_loop(0, grp * blk, one_source, 0)
+    lax.fori_loop(0, grp * chunks, one_source, 0)
     shard_rows = out_ref.shape[0]
 
     def finish(i, squares):
@@ -675,12 +680,12 @@
     pltpu.make_async_copy(total_ref.at[pl.ds(0, shard_rows)], out_ref, out_sem).wait()
 
 
-def word_sum(grp_index, counts, ids, sources, shard_rows, blk, room):
+def word_sum(grp_index, counts, ids, sources, shard_rows, chunks, room):
     grp, width = len(sources), sources[0].shape[1]
     span = next(size for size in (128, 64, 32, 16, 8) if shard_rows % size == 0)
     anywhere = pl.BlockSpec(memory_space=pl.ANY)
     return pl.pallas_call(
-        functools.partial(word_sum_kernel, grp=grp, blk=blk, room=room, span=span),
+        functools.partial(word_sum_kernel, grp=grp, chunks=chunks, room=room, span=span),
         out_shape=[
             jax.ShapeDtypeStruct((shard_rows, width), jnp.float32),
             jax.ShapeDtypeStruct((1, width), jnp.float32),
@@ -706,6 +711,95 @@
     )(grp_index.reshape(1), counts, ids, *sources)
 
 
+def adam_kernel(factor_ref, grad_ref, master_ref, moments_ref, first_ref, second_ref, new_ref, *, rate):
+    results = adam_update(
+        grad_ref[...] * factor_ref[0], (moments_ref[0], moments_ref[1]), master_ref[...], rate
+    )
+    first_ref[...], second_ref[...], new_ref[...] = results
+
+
+def adam_rows(factor, grad, master, moments, rate):
+    rows, width = master.shape
+    span = next(size for size in (256, 240, 192, 128, 96, 64, 32, 16, 8) if rows % size == 0)
+    block = rows_block(span, width)
+    return pl.pallas_call(
+        functools.partial(adam_kernel, rate=rate),
+        out_shape=[jax.ShapeDtypeStruct((rows, width), jnp.float32)] * 3,
+        grid=(rows // span,),
+        in_specs=[
+            pl.BlockSpec(memory_space=pltpu.SMEM),
+            block,
+            block,
+            pl.BlockSpec((2, span, width), lambda i: (0, i, 0)),
+        ],
+        out_specs=[block] * 3,
+        compiler_params=pltpu.CompilerParams(vmem_limit_bytes=VMEM_ALLOWED),
+        cost_estimate=pl.CostEstimate(
+            flops=20 * rows * width, bytes_accessed=28 * rows * width, transcendentals=0
+        ),
+        name="adam_rows",
+    )(factor, grad, master, moments)
+
+
+def adam_matrices_kernel(place_ref, factor_ref, *refs, grp, shapes, rates):
+    count = len(shapes)
+    pieces, rest = (refs[:grp], refs[grp : 2 * grp]), refs[2 * grp :]
+    small_ref, rest = rest[0], rest[1:]
+    masters, rest = rest[: count + 1], rest[count + 1 :]
+    moments, rest = rest[: count + 1], rest[count + 1 :]
+    outs, scratch = rest[: 3 * count + 3], rest[3 * count + 3 :]
+    factor = factor_ref[0]
+    base = 0
+    for n, (rows, width) in enumerate(shapes):
+        strips = width // 2 // strip
+        piece = rows // (grp // 2)
+        group = pieces[n // 2]
+        base = 0 if n % 2 == 0 else base
+        for k in range(grp):
+            source = place_ref[0] ^ k
+            x, core = source // 2, source % 2
+            for s in range(strips):
+                part = group[k][base + s * piece : base + (s + 1) * piece, :]
+                to_row = pl.multiple_of(x * piece, 16)
+                to_column = pl.multiple_of((core * strips + s) * strip, 128)
+                scratch[n][pl.ds(to_row, piece), pl.ds(to_column, strip)] = part.astype(
+                    jnp.float32
+                )
+        base += strips * piece
+    for n in range(count + 1):
+        grad = small_ref[...] if n == count else scratch[n][...]
+        results = adam_update(
+            grad * factor, (moments[n][0], moments[n][1]), masters[n][...], rates[n]
+        )
+        for m in range(3):
+            outs[3 * n + m][...] = results[m]
+
+
+def adam_matrices(grp_index, factor, pieces_one, pieces_two, small, masters, moments, rates):
+    shapes = [item.shape for item in masters]
+    count = len(shapes) - 1
+    operands = [*pieces_one, *pieces_two, small, *masters, *moments]
+    return pl.pallas_call(
+        functools.partial(
+            adam_matrices_kernel, grp=len(pieces_one), shapes=shapes[:count], rates=rates
+        ),
+        out_shape=[jax.ShapeDtypeStruct(s, jnp.float32) for s in shapes for _ in range(3)],
+        grid_spec=pltpu.PrefetchScalarGridSpec(
+            num_scalar_prefetch=1,
+            grid=(1,),
+            in_specs=[pl.BlockSpec(memory_space=pltpu.SMEM)]
+            + [whole_block(item.shape) for item in operands],
+            out_specs=[whole_block(s) for s in shapes for _ in range(3)],
+            scratch_shapes=[pltpu.VMEM(s, jnp.float32) for s in shapes[:count]],
+        ),
+        compiler_params=pltpu.CompilerParams(vmem_limit_bytes=VMEM_ALLOWED),
+        cost_estimate=pl.CostEstimate(
+            flops=10**8, bytes_accessed=30 * 10**6, transcendentals=0
+        ),
+        name="adam_matrices",
+    )(grp_index.reshape(1), factor, *operands)
+
+
 class Place:
     def __init__(self):
         self.blk, self.grp = lax.axis_size("blk"), lax.axis_size("grp")
@@ -719,6 +813,14 @@
         self.y_masks = [0, self.grp]
         self.z_masks = [2 * self.grp * i for i in range(self.far)]
 
+    def send_swapped(self, value, far_mask):
+        pairs = []
+        for i in range(self.count):
+            core, x, y = i % 2, i // 2 % self.xs, i // self.grp % 2
+            z = i // (2 * self.grp) ^ far_mask
+            pairs.append((i, ((z * 2 + core) * self.xs + x) * 2 + y))
+        return lax.ppermute(value, both, pairs)
+
     def send(self, value, mask):
         pairs = [(i, i ^ mask) for i in range(self.count)]
         return lax.ppermute(value, both, pairs)
@@ -768,30 +870,53 @@
     return jnp.concatenate([value[..., : rows - fine, :], tail], -2)
 
 
-def reduce_stage(place, value, masks, index, fine):
-    terms = [lax.dynamic_index_in_dim(value, index, 0, keepdims=False).astype(jnp.float32)]
-    for k in range(1, len(masks)):
-        part = lax.dynamic_index_in_dim(value, index ^ k, 0, keepdims=False)
-        terms.append(from_sent(place.send(to_send(part, fine), masks[k]), fine))
+def stage_parts(value, masks, index, fine):
+    keep = lax.dynamic_index_in_dim(value, index, 0, keepdims=False)
+    parts = [
+        to_send(lax.dynamic_index_in_dim(value, index ^ k, 0, keepdims=False), fine)
+        for k in range(1, len(masks))
+    ]
+    return keep, parts
+
+
+def stage_sum(keep, arrived, fine):
+    terms = [keep.astype(jnp.float32)] + [from_sent(item, fine) for item in arrived]
     while len(terms) > 1:
         terms = [terms[i] + terms[i + 1] for i in range(0, len(terms), 2)]
     return terms[0]
 
 
-def reduce_rest(place, value, x_first, fine):
-    rows = value.shape[2]
-    value = value.reshape(place.far, 2, place.xs, rows, value.shape[3])
-    if x_first:
-        value = jnp.moveaxis(value, 2, 0)
-        value = reduce_stage(place, value, place.x_masks, place.x, fine)
-        value = jnp.moveaxis(value, 1, 0)
-        value = reduce_stage(place, value, place.y_masks, place.y, fine)
-    else:
-        value = jnp.moveaxis(value, 1, 0)
-        value = reduce_stage(place, value, place.y_masks, place.y, fine)
-        value = jnp.moveaxis(value, 1, 0)
-        value = reduce_stage(place, value, place.x_masks, place.x, fine)
-    return reduce_stage(place, value, place.z_masks, place.z, fine)
+class Reduction:
+    def __init__(self, place, value, x_first, fine=0):
+        rows, columns = value.shape[2:]
+        value = value.reshape(place.far, 2, place.xs, rows, columns)
+        x_stage = (place.x_masks, place.x)
+        y_stage = (place.y_masks, place.y)
+        self.place, self.fine = place, fine
+        if x_first:
+            self.stages = [(*x_stage, 2), (*y_stage, 1)]
+        else:
+            self.stages = [(*y_stage, 1), (*x_stage, 1)]
+        self.stages.append((place.z_masks, place.z, 0))
+        self.value = value
+
+    def prepare(self):
+        self.masks, index, axis = self.stages.pop(0)
+        self.keep, self.parts = stage_parts(
+            jnp.moveaxis(self.value, axis, 0), self.masks, index, self.fine
+        )
+
+    def send(self):
+        self.arrived = [
+            self.place.send(part, mask) for part, mask in zip(self.parts, self.masks[1:])
+        ]
+
+    def add(self):
+        self.value = stage_sum(self.keep, self.arrived, self.fine)
+
+
+def tie(*items):
+    return lax.optimization_barrier(items)
 
 
 def half_gradient(place, left, right, core):
@@ -806,32 +931,27 @@
     )
 
 
-def reduce_group(place, pairs, extra):
+def group_products(place, pairs):
     if all(a.shape[1] % (16 * place.blk * place.xs) == 0 for a, _ in pairs):
-        theirs, mine = weight_grads(place, pairs)
-    else:
-        mine = [half_gradient(place, a, b, place.core) for a, b in pairs]
-        theirs = [half_gradient(place, a, b, 1 - place.core) for a, b in pairs]
-        mine, theirs = jnp.concatenate(mine, 2), jnp.concatenate(theirs, 2)
-    fine = 0
-    if extra is not None:
-        fine = extra.shape[3]
-        own = lax.dynamic_index_in_dim(extra, place.core, 2, keepdims=False)
-        mine = jnp.concatenate([mine.astype(jnp.float32), own], 2)
-        other = lax.dynamic_index_in_dim(extra, 1 - place.core, 2, keepdims=False)
-        theirs = jnp.concatenate([theirs, to_send(other, fine)], 2)
-    arrived = from_sent(place.send(theirs, 1), fine)
-    return mine.astype(jnp.float32) + arrived, fine
-
-
-def reduce_group_rest(place, value, fine):
-    cut = value.shape[2] // 32 * 16
-    return jnp.concatenate(
-        [
-            reduce_rest(place, value[:, :, :cut], True, 0),
-            reduce_rest(place, value[:, :, cut:], False, fine),
-        ]
-    )
+        return weight_grads(place, pairs)
+    mine = [half_gradient(place, a, b, place.core) for a, b in pairs]
+    theirs = [half_gradient(place, a, b, 1 - place.core) for a, b in pairs]
+    return jnp.concatenate(theirs, 2), jnp.concatenate(mine, 2).astype(jnp.float32)
+
+
+def merge_ids(left, right, length):
+    hits = []
+    for own, other in ((left, right), (right, left)):
+        repeated = jnp.any(other[..., :, None] == own[..., None, :], -1)
+        lower = (
+            (other >= 0)[..., None, :]
+            & ~repeated[..., None, :]
+            & (other[..., None, :] < own[..., :, None])
+        )
+        rank = jnp.arange(own.shape[-1]) + jnp.sum(lower.astype(jnp.int32), -1)
+        hit = rank[..., None, :] == jnp.arange(length)[:, None]
+        hits.append(jnp.max(jnp.where(hit, own[..., None, :], -1), -1))
+    return jnp.maximum(*hits)
 
 
 def whole_rows(place, pieces, rows, width):
@@ -890,48 +1010,42 @@
     rank = jnp.sum(smaller.astype(jnp.int32), 1)
     slots = place.blk * room
 
-    def slot_ids_of(round_number):
-        at = rank - round_number * room
-        slot = jnp.where((at >= 0) & (at < room), shard * room + at, slots)
-        hit = slot[None, :] == jnp.arange(slots)[:, None]
-        return jnp.max(jnp.where(hit, flat_ids[None, :], -1), 1)
-
-    def lookup_slots(round_number):
-        at = rank - round_number * room
-        owner = shard // per_owner
-        relative = ((owner ^ place.g) * per_owner + shard % per_owner) * room + at
-        return jnp.where((at >= 0) & (at < room), relative, slots)
-
-    def gradient_slots(round_number):
-        at = rank - round_number * room
-        relative = (shard ^ place.b) * room + at
-        return jnp.where((at >= 0) & (at < room), relative, slots)
-
-    def fetch(grp_ids, round_number):
+    owner = shard // per_owner
+    relative = ((owner ^ place.g) * per_owner + shard % per_owner) * room + rank
+    lookup_slots = jnp.where(rank < room, relative, slots)
+
+    def fetch(grp_ids):
         span = per_owner * room
         asked = [lax.dynamic_slice_in_dim(ids, place.g * span, span) for ids in grp_ids]
         local = jnp.concatenate(asked) - place.g * table_rows
         found = word_table.at[jnp.clip(local, 0, table_rows - 1)].get(mode="clip")
+        found, sibling = tie(found, grp_ids[1])
         parts = [found[k * span : (k + 1) * span] for k in range(place.grp)]
         rows = [parts[0]] + [place.send(parts[k], k) for k in range(1, place.grp)]
-        return jnp.concatenate(rows)
+        return jnp.concatenate(rows), sibling
 
     def pack(values, length):
         return jnp.concatenate([values, jnp.zeros((length - values.shape[0],), values.dtype)])
 
-    slot_ids = slot_ids_of(0)
+    slot = jnp.where(rank < room, shard * room + rank, slots)
+    hit = slot[None, :] == jnp.arange(slots)[:, None]
+    slot_ids = jnp.max(jnp.where(hit, flat_ids[None, :], -1), 1)
     early = jnp.concatenate(
-        [slot_ids, false_neg.reshape(-1), valid, jnp.max(rank)[None]]
+        [
+            slot_ids,
+            false_neg.reshape(-1),
+            valid,
+            (jnp.max(rank) >= room).astype(jnp.int32)[None],
+        ]
     )
     early = pack(early, -(-early.shape[0] // 1024) * 1024).reshape(-1, 128)
     grp_early = [early] + [place.send(early, k) for k in range(1, place.grp)]
-    grp_ids = [item.reshape(-1)[:slots] for item in grp_early]
-    looked_up = fetch(grp_ids, 0)
+    looked_up, sibling = fetch([item.reshape(-1)[:slots] for item in grp_early])
     early_all = jnp.stack(in_order(grp_early, place.g))
     early_all = gather_stage(place, early_all, place.y_masks, place.y)
     early_all = gather_stage(place, early_all, place.z_masks, place.z)
     early_all = early_all.reshape(place.count, -1)
-    ids_all = early_all[:, :slots]
+    ids_all = early_all[:, :slots].reshape(place.blk, place.xs, 2, place.blk, room)
     at = slots
     false_neg_all = early_all[:, at : at + pairs_here * total_pairs].reshape(
         total_pairs, total_pairs
@@ -939,14 +1053,36 @@
     at += pairs_here * total_pairs
     valid_all = early_all[:, at : at + pairs_here].reshape(-1)
     at += pairs_here
-    rounds = jnp.max(early_all[:, at]) // room + 1
+    crowded = jnp.max(early_all[:, at]) > 0
+
+    chip_room = max(16, tokens * 3 // 2 // place.blk // 16 * 16)
+    chip_slots = place.blk * chip_room
+    known = jnp.any(sibling[:, None] == flat_ids[None, :], 1)
+    extra = (
+        (sibling[None, :] >= 0)
+        & ~known[None, :]
+        & (sibling[None, :] // shard_rows == shard[:, None])
+        & (sibling[None, :] < flat_ids[:, None])
+    )
+    chip_rank = rank + jnp.sum(extra.astype(jnp.int32), 1)
+    shard_y, shard_z = shard % 2, shard // 2
+    order = jnp.where(shard_y == place.core, 0, place.far) + (shard_z ^ place.z)
+    gradient_slot = jnp.where(
+        chip_rank < chip_room, order * chip_room + chip_rank, chip_slots
+    )
+    weights = (qkv_weight, out_weight, up_weight, down_weight)
+
+    def encode(slot, found):
+        return forward(
+            lengths_flat, slot[:, None], found, small_rows, weights, seq_len, head_dim
+        )
 
     def look_up_all():
         whole = lax.all_gather(word_table, "grp", axis=0, tiled=True)
         return jnp.arange(tokens, dtype=jnp.int32), whole[flat_ids]
 
     slot, found = lax.cond(
-        rounds > 1, look_up_all, lambda: (lookup_slots(0).astype(jnp.int32), looked_up)
+        crowded, look_up_all, lambda: (lookup_slots.astype(jnp.int32), looked_up)
     )
     (
         unit1,
@@ -964,17 +1100,15 @@
         inverse3,
         pooled,
         own_embed,
-    ) = forward(
-        lengths_flat,
-        slot[:, None],
-        found,
-        small_rows,
-        (qkv_weight, out_weight, up_weight, down_weight),
-        seq_len,
-        head_dim,
-    )
-
-    gathered = gather_far_first(place, own_embed).reshape(total_pairs, 2, width)
+    ) = encode(slot, found)
+
+    chip_crowded = (jnp.max(rank) >= room) | (jnp.max(chip_rank) >= chip_room)
+    embed_rows = jnp.concatenate(
+        [own_embed.reshape(-1, width), jnp.full((8, width), chip_crowded, low)]
+    )
+    gathered = gather_far_first(place, embed_rows).reshape(place.count, -1, width)
+    rows_crowded = jnp.max(gathered[:, -1, 0].astype(jnp.float32)) > 0.5
+    gathered = gathered[:, : 2 * pairs_here].reshape(total_pairs, 2, width)
     queries, documents = gathered[:, 0], gathered[:, 1]
     diagonal = jnp.arange(total_pairs)[:, None] == jnp.arange(total_pairs)[None, :]
     allowed = (valid_all[None, :] > 0) & ((false_neg_all == 0) | diagonal)
@@ -1015,50 +1149,98 @@
         (up_weight, down_weight),
         seq_len,
     )
-    group_one, _ = reduce_group(
-        place, [(activated_low, lowered_grad), (middle_low, lifted_low)], None
-    )
-    second, group_one = lax.optimization_barrier((second, group_one))
-    group_one = reduce_group_rest(place, group_one, 0)
-    branch_grad, projected_grad, own_rows, position_grad, attention_sums = attention_back(
-        gradient_slots(0),
+    theirs_down, mine_down = group_products(place, [(activated_low, lowered_grad)])
+    lifted_low, theirs_down, mine_down = tie(lifted_low, theirs_down, mine_down)
+    core_down = place.send(theirs_down, 1)
+    theirs_up, mine_up = group_products(place, [(middle_low, lifted_low)])
+    down = Reduction(place, mine_down + core_down.astype(jnp.float32), False)
+    down.prepare()
+    theirs_up, mine_up, down.parts = tie(theirs_up, mine_up, down.parts)
+    down.send()
+    core_up = place.send(theirs_up, 1)
+    up = Reduction(place, mine_up + core_up.astype(jnp.float32), True)
+    up.prepare()
+    second, up.parts = tie(second, up.parts)
+    up.send()
+    branch_grad, projected_grad, mine_rows, theirs_rows, position_grad, attention_sums = attention_back(
+        gradient_slot,
         second,
         (projected, probs, unit1, inverse1),
         small_rows,
         (qkv_weight, out_weight),
         seq_len,
         head_dim,
-        slots,
-    )
-
-    grid_ids = lax.dynamic_slice_in_dim(
-        ids_all.reshape(place.blk, place.grp, place.blk, room), place.b, 1, 2
-    )[:, :, 0]
-
-    rows = own_rows.reshape(place.blk, room, width)
-    arrived = [rows[0]] + [place.send(rows[k], k * place.grp) for k in range(1, place.blk)]
-    halves = [jnp.concatenate(arrived[: place.far]), jnp.concatenate(arrived[place.far :])]
-    over_x = [
-        jnp.concatenate([halves[0], halves[1]])
-        if mask == 0
-        else jnp.concatenate([place.send(half, mask) for half in halves])
-        for mask in place.x_masks
-    ]
-    over_core = [place.send(item, 1) for item in over_x]
-    sources = [item for pair in zip(over_x, over_core) for item in pair]
-    ids = jnp.stack(in_order([grid_ids[i] for i in range(place.blk)], place.b), 1)
+        chip_slots,
+    )
+
+    theirs_rows, down.arrived, up.arrived = tie(theirs_rows, down.arrived, up.arrived)
+    rows = mine_rows + place.send(theirs_rows, 1).astype(jnp.float32)
+    rows = rows.astype(low).reshape(place.far, chip_room, width)
+    arrived = [place.send_swapped(rows[k], k) for k in range(place.far)]
+    down.add()
+    down.prepare()
+    up.add()
+    up.prepare()
+    projected_grad, branch_grad, down.parts, up.parts = tie(
+        projected_grad, branch_grad, down.parts, up.parts
+    )
+    down.send()
+    theirs_two, mine_two = group_products(
+        place, [(normed_low, projected_grad), (attended, branch_grad)]
+    )
+    arrived, down.arrived, up.parts, theirs_two, mine_two = tie(
+        arrived, down.arrived, up.parts, theirs_two, mine_two
+    )
+    core_two = place.send(theirs_two, 1)
+    up.send()
+    arrived = jnp.concatenate(arrived)
+    over_x = [arrived] + [place.send(arrived, mask) for mask in place.x_masks[1:]]
+
+    small_grad = jnp.concatenate([position_grad, attention_sums[:4], feed_sums[:10]], 0)
+    small_flat = small_grad.reshape(-1, strip)
+    small_piece = -(-small_flat.shape[0] // (16 * place.count)) * 16
+    small_padded = jnp.concatenate(
+        [
+            small_flat,
+            jnp.zeros((small_piece * place.count - small_flat.shape[0], strip), jnp.float32),
+        ]
+    )
+    small_parts = small_padded.reshape(place.blk, place.xs, 2, small_piece, strip)
+    fine = small_piece
+    small_mine = lax.dynamic_index_in_dim(small_parts, place.core, 2, keepdims=False)
+    small_theirs = lax.dynamic_index_in_dim(small_parts, 1 - place.core, 2, keepdims=False)
+    small_theirs = place.send(to_send(small_theirs, fine), 1)
+    value_two = jnp.concatenate(
+        [mine_two + core_two.astype(jnp.float32), small_mine + from_sent(small_theirs, fine)], 2
+    )
+    two = Reduction(place, value_two, False, fine)
+    two.prepare()
+    over_x, up.arrived, two.parts = tie(over_x, up.arrived, two.parts)
+    two.send()
+    down.add()
+    up.add()
+    one = Reduction(place, jnp.zeros((place.blk, place.xs, 16, strip), low), False)
+    one.stages = one.stages[-1:]
+    one.value = jnp.concatenate([down.value, up.value], 1)
+    one.prepare()
+    over_x, one.parts = tie(over_x, one.parts)
+    one.send()
+    sources = [item for value in over_x for item in (value, place.send(value, 1))]
+    ids = lax.dynamic_index_in_dim(ids_all, place.b, 3, keepdims=False)
+    ids = merge_ids(ids[:, :, 0], ids[:, :, 1], chip_room)
+    ids = ids.reshape(place.far, 2, place.xs, chip_room)
+    ids = jnp.stack(in_order([ids[i] for i in range(place.far)], place.z))
+    ids = jnp.transpose(ids, (2, 1, 0, 3))
     local = ids - place.b * shard_rows
     inside = ids >= 0
     counts = jnp.sum(inside.astype(jnp.int32), -1).reshape(-1)
     local = jnp.where(inside, local, shard_rows).reshape(-1)
-    word_rows, word_squares = word_sum(
-        place.g, counts, local, sources, shard_rows, place.blk, room
-    )
-    word_squares = jnp.sum(word_squares)
-
-    def all_rows(carry):
-        token_grads = attention_back(
-            jnp.arange(tokens, dtype=jnp.int32) + carry[0],
+    def few_rows():
+        return word_sum(place.g, counts, local, sources, shard_rows, place.far, chip_room)
+
+    def all_rows():
+        token_halves = attention_back(
+            jnp.arange(tokens, dtype=jnp.int32),
             second,
             (projected, probs, unit1, inverse1),
             small_rows,
@@ -1066,8 +1248,9 @@
             seq_len,
             head_dim,
             slots,
-        )[2]
-        every_id = lax.all_gather(flat_ids + carry[0], "blk", axis=0, tiled=True) - place.b * shard_rows
+        )[2:4]
+        token_grads = jnp.concatenate([token_halves[0].astype(low), token_halves[1]])
+        every_id = lax.all_gather(flat_ids, "blk", axis=0, tiled=True) - place.b * shard_rows
         every_row = lax.all_gather(token_grads, "blk", axis=0, tiled=True)
         inside = (every_id >= 0) & (every_id < shard_rows)
         total = (
@@ -1076,65 +1259,74 @@
             .add(every_row.astype(jnp.float32), mode="drop")
         )
         total = lax.psum(total, "grp")
-        return (carry[0] + 1, total, jnp.sum(total * total))
-
-    _, word_rows, word_squares = lax.while_loop(
-        lambda carry: (carry[0] < 1) & (rounds > 1),
-        all_rows,
-        (jnp.int32(0), word_rows, word_squares),
-    )
-
-    small_grad = jnp.concatenate([position_grad, attention_sums[:4], feed_sums[:10]], 0)
-    small_flat = small_grad.reshape(-1, strip)
-    small_piece = -(-small_flat.shape[0] // (16 * place.count)) * 16
-    small_padded = jnp.concatenate(
-        [
-            small_flat,
-            jnp.zeros((small_piece * place.count - small_flat.shape[0], strip), jnp.float32),
-        ]
-    )
-    small_parts = small_padded.reshape(place.blk, place.xs, 2, small_piece, strip)
-    group_two, fine = reduce_group(
-        place, [(normed_low, projected_grad), (attended, branch_grad)], small_parts
-    )
-    group_two = reduce_group_rest(place, group_two, fine)
-    cut = group_two.shape[0] - small_piece
-    small_own = group_two[cut:]
-    matrix_own = jnp.concatenate([group_one, group_two[:cut]]).astype(jnp.bfloat16)
-    gathered_grads = gather_stage(place, matrix_own, place.x_masks, place.x)
-    gathered_grads = gather_stage(place, gathered_grads, place.core_masks, place.core)
-    gathered_grads = jnp.swapaxes(gathered_grads, 0, 1)
-    masters = (down_master, up_master, qkv_master, out_master)
-    shards, at = [], 0
-    for master in masters:
-        rows, columns = master.shape[0] // place.xs, master.shape[1]
-        length = rows * (columns // 2 // strip)
-        shards.append(
-            whole_rows(place, gathered_grads[:, :, at : at + length], rows, columns).astype(
-                jnp.float32
-            )
-        )
-        at += length
-
-    matrix_floats = matrix_own.astype(jnp.float32)
-    squares = (
-        jnp.sum(matrix_floats * matrix_floats)
-        + jnp.sum(small_own * small_own)
-        + word_squares / place.grp
-    )
-    late = jnp.concatenate([small_own, jnp.full((8, strip), squares)])
-    late = gather_far_first(place, late).reshape(place.count, -1, strip)
+        return total, jnp.sum(total * total, 0, keepdims=True)
+
+    word_rows, word_squares = lax.cond(rows_crowded, all_rows, few_rows)
+    word_rows, word_squares, two.arrived, one.arrived = tie(
+        word_rows, word_squares, two.arrived, one.arrived
+    )
+    two.add()
+    two.prepare()
+    two.send()
+    one.add()
+    two.add()
+    two.prepare()
+    one.value, two.parts = tie(one.value, two.parts)
+    two.send()
+    piece_one = one.value.astype(low)
+    one_x = [piece_one] + [place.send(piece_one, mask) for mask in place.x_masks[1:]]
+    two.add()
+    cut = two.value.shape[0] - small_piece
+    piece_two, small_own = two.value[:cut].astype(low), two.value[cut:]
+    squares = jnp.sum(small_own * small_own, 0, keepdims=True)
+    for item in (piece_one, piece_two):
+        item = item.astype(jnp.float32)
+        squares = squares + jnp.sum(item * item, 0, keepdims=True)
+    squares = squares + jnp.sum(word_squares.reshape(-1, 1, strip), 0) / place.grp
+    late = jnp.concatenate([small_own, jnp.broadcast_to(squares, (8, strip))])
+    late, one_x = tie(late, one_x)
+    late = gather_stage(place, late, place.z_masks, place.z)
+    two_x = [piece_two] + [place.send(piece_two, mask) for mask in place.x_masks[1:]]
+    late, two_x = tie(late, two_x)
+    middle = [a + b for a in place.y_masks for b in place.x_masks]
+    late = gather_stage(place, late, middle, place.y * place.xs + place.x)
+    pieces_one = [item for value in one_x for item in (value, place.send(value, 1))]
+    late, pieces_one = tie(late, pieces_one)
+    late = gather_stage(place, late, place.core_masks, place.core)
+    pieces_two = [item for value in two_x for item in (value, place.send(value, 1))]
+    late = late.reshape((2, 2, place.xs, place.far) + late.shape[3:])
+    late = jnp.transpose(late, (3, 1, 2, 0, 4, 5)).reshape(place.count, -1, strip)
     small_total = late[:, :small_piece].reshape(-1, strip)[: small_flat.shape[0]]
     small_total = small_total.reshape(small_grad.shape)
-    grad_norm = jnp.sqrt(jnp.sum(late[:, small_piece, 0]))
-    factor = clip_bound / jnp.maximum(grad_norm, clip_bound)
-    down_shard, up_shard, qkv_shard, out_shard = shards
-    grads = (word_rows, qkv_shard, out_shard, up_shard, down_shard, small_total)
-    parameters = (word_master, qkv_master, out_master, up_master, down_master, small_rows)
-    moments = (word_moments, qkv_moments, out_moments, up_moments, down_moments, small_moments)
-    results = []
-    for grad, moment, master, rate in zip(grads, moments, parameters, rate_table):
-        results.extend(adam_update(grad * factor, moment, master, rate))
+    grad_norm = jnp.sqrt(jnp.sum(late[:, small_piece]))
+    factor = (clip_bound / jnp.maximum(grad_norm, clip_bound)).reshape(1)
+    word_results = adam_rows(factor, word_rows, word_master, word_moments, rate_table[0])
+    masters = (down_master, up_master, qkv_master, out_master, small_rows)
+    moments = (down_moments, up_moments, qkv_moments, out_moments, small_moments)
+    rates = tuple(rate_table[i] for i in (4, 3, 1, 2, 5))
+    if all(item.shape[0] % (16 * place.xs) == 0 for item in masters[:4]):
+        results = adam_matrices(
+            place.g, factor, pieces_one, pieces_two, small_total, masters, moments, rates
+        )
+    else:
+        ordered = [
+            jnp.concatenate(pair)
+            for pair in zip(in_order(pieces_one, place.g), in_order(pieces_two, place.g))
+        ]
+        ordered = jnp.stack(ordered).reshape((place.xs, 2) + ordered[0].shape)
+        grads, at = [], 0
+        for master in masters[:4]:
+            rows, columns = master.shape[0] // place.xs, master.shape[1]
+            length = rows * (columns // 2 // strip)
+            part = ordered[:, :, at : at + length]
+            grads.append(whole_rows(place, part, rows, columns).astype(jnp.float32))
+            at += length
+        grads.append(small_total)
+        results = []
+        for grad, moment, master, rate in zip(grads, moments, masters, rates):
+            results.extend(adam_update(grad * factor[0], moment, master, rate))
+    down, up, qkv, out, small = (results[3 * n : 3 * n + 3] for n in range(5))
+    results = [*word_results, *qkv, *out, *up, *down, *small]
     return (loss_total, pair_count, grad_norm, *results)
 
 

time: 555 us -> 464 us (0.84)
  waiting for transfers between devices: 162 us -> 85 us
  Pallas kernels: 156 us -> 200 us
  other arithmetic: 84.1 us -> 45 us
  starting transfers between devices: 73 us -> 60.1 us
  local copies, waits for them, and re-layouts: 46.9 us -> 41 us
    ppermute x59 -> x50, waiting for transfers between devices: 162 us -> 80.8 us  [send(): return lax.ppermute(value, both, pairs)]
    pallas_call x1 -> x3, Pallas kernels: 25.9 us -> 65.1 us  [the longest x1 32.6 us: adam_rows(): pl.pallas_call(functools.partial(adam_kernel, rate=rate), out_shape=[jax....]
    sub x6 -> x0, other arithmetic: 39.2 us -> none  [adam_update(): master - rate * (first_hat / (jnp.sqrt(second_hat) + epsilon) + decay_wei...]
    ppermute x59 -> x50, starting transfers between devices: 73 us -> 55 us  [send(): return lax.ppermute(value, both, pairs)]
    another operation x18 -> x15, other arithmetic: 6.61 us -> 0.51 us  [gather_stage(): return jnp.stack(in_order(pieces, index))]
    slice x8 -> x5, local copies, waits for them, and re-layouts: 6.11 us -> 0.11 us  [the longest x1 0.08 us: on_device(): arrived = [place.send_swapped(rows[k], k) for k in range(place.far)]]
    add x10 -> x14, other arithmetic: 13 us -> 10.8 us  [the longest x7 5.17 us: stage_sum(): terms = [terms[i] + terms[i + 1] for i in range(0, len(terms), 2)]]
    unnamed x77 -> x93, local copies, waits for them, and re-layouts: 15.2 us -> 14.2 us
  transfers between devices with their start and end apart: 59 -> 54, of which waited for: 33 -> 25; matrix products, arithmetic and copies ran while one was open for 14% -> 9% of each run, Pallas kernels for 5% -> 25%
where the time goes in v3:
time: 464 us; the launch traced here: 457 us
  Pallas kernels  200 us (43%)
  waiting for transfers between devices  85 us (18%)
  starting transfers between devices  60.1 us (13%)
  other arithmetic  45 us (10%)
  local copies, waits for them, and re-layouts  41 us (9%)
  between operations  23.9 us (5%)
    ppermute x50, waiting for transfers between devices, send(): return lax.ppermute(value, both, pairs)  80.8 us
    ppermute x50, starting transfers between devices, send(): return lax.ppermute(value, both, pairs)  55 us
    pallas_call x1, Pallas kernels, forward(): pl.pallas_call(functools.partial(forward_kernel, seq_len=seq_len, seqs=se...  43.8 us
    pallas_call x3, Pallas kernels, weight_grads(): pl.pallas_call(functools.partial(weight_grad_kernel, jobs=jobs, xs=place....  35.8 us
    pallas_call x1, Pallas kernels, attention_back(): pl.pallas_call(functools.partial(attention_back_kernel, seq_len=seq_len,...  35 us
    pallas_call x1, Pallas kernels, adam_rows(): pl.pallas_call(functools.partial(adam_kernel, rate=rate), out_shape=[jax....  32.6 us
    pallas_call x1, Pallas kernels, feed_back(): pl.pallas_call(functools.partial(feed_back_kernel, seq_len=seq_len, seqs=...  20.8 us
    pallas_call x1, Pallas kernels, word_sum(): pl.pallas_call(functools.partial(word_sum_kernel, grp=grp, chunks=chunks,...  20.4 us
  transfers between devices with their start and end apart: 54, of which 25 were waited for; matrix products, arithmetic and copies ran while one was open for 9% of the time, Pallas kernels for 25%

profile of v3, /device:TPU:0, one launch (start us, length us, event | category | flops | bytes accessed | tf_op | source)
XLA Modules:
  0.0 456.6 jit_solution(16646753078588275412)
XLA Ops:
  15.4 2.4 collective-permute-start
  21.7 10.3 %gather_fusion.1 = bf16[1024,768]{1,0:T(8,128)(2,1)S(1)} fusion(bf16[7680,768]{1,0:T(8,128)(2,1)} %param.29, s32[1024]{0:T(1024)S(1)} %broadcast_clamp_fusion), kind=kCustom, calls=%fused_computation.1 | custom fusion | bytes 3149824 | tf_op jit(solution)/shard_map/gather | solution.py:1021
  37.5 3.7 collective-permute-start.4
  44.4 3.3 collective-permute-done.5
  49.3 4.9 %collective-permute-done.8 = bf16[256,768]{1,0:T(8,128)(2,1)S(1)} collective-permute-done((bf16[256,768]{1,0:T(8,128)(2,1)S(1)}, bf16[256,768]{1,0:T(8,128)(2,1)S(1)}, u32[]{:S(2)}, u32[]{:S(2)}) %collective-permute-start.8) | collective-permute-done | bytes 393248 | tf_op jit(solution)/shard_map/ppermute | solution.py:826
  57.9 43.8 %encoder_forward.1 = (f32[1024,768]{1,0:T(8,128)}, f32[1024,1]{1,0:T(8,128)}, bf16[1024,768]{1,0:T(8,128)(2,1)}, bf16[1024,2304]{1,0:T(8,128)(2,1)}, bf16[8,6,25...) custom-call(s32[8]{0:T(128)} %reshape.612.lengths_ref, ...), custom_call_target="tpu_custom_call" | custom-call | flops 20000000000 | bytes 50000000 | tf_op jit(solution)/shard_map/encoder_forward/pallas_call | solution.py:252
  102.5 3.7 collective-permute-start.10
  108.2 2.7 collective-permute-done.11
  111.5 2.6 collective-permute-start.13
  126.4 20.8 %feed_back.1 = (bf16[1024,768]{1,0:T(8,128)(2,1)}, bf16[1024,3072]{1,0:T(8,128)(2,1)}, f32[1024,768]{1,0:T(8,128)}, f32[16,768]{1,0:T(8,128)}) custom-call(s32[8]{0:T(128)} %reshape.612.lengths_ref, f32[4,2,768]{2,1,0:T(2,128)} %maximum_multiply_fusion.embed_grad_ref, f32[4,2,768]{2,1,0:T(2,128)} %get-tuple-element.293.pooled_ref, ...), custom_call_target="tpu_custom_call" | custom-call | flops 10000000000 | bytes 40000000 | tf_op jit(solution)/shard_map/feed_back/pallas_call | solution.py:343
  147.2 11.3 %weight_grads.3 = (bf16[8,2,192,384]{3,2,1,0:T(8,128)(2,1)}, f32[8,2,192,384]{3,2,1,0:T(8,128)}) custom-call(s32[1]{0:T(128)} %bitcast.42.core_ref, bf16[1024,3072]{1,0:T(8,128)(2,1)} %get-tuple-element.302.refs_0_, bf16[1024,768]{1,0:T(8,128)(2,1)} %get-tuple-element.303.refs_1_), custom_call_target="tpu_custom_call" | custom-call | flops 4831838208 | bytes 16000000 | tf_op jit(solution)/shard_map/weight_grads/pallas_call | solution.py:598
  158.6 11.7 %weight_grads.4 = (bf16[8,2,192,384]{3,2,1,0:T(8,128)(2,1)}, f32[8,2,192,384]{3,2,1,0:T(8,128)}) custom-call(s32[1]{0:T(128)} %bitcast.42.core_ref, bf16[1024,768]{1,0:T(8,128)(2,1)} %get-tuple-element.300.refs_0_, bf16[1024,3072]{1,0:T(8,128)(2,1)} %get-tuple-element.306.refs_1_), custom_call_target="tpu_custom_call" | custom-call | flops 4831838208 | bytes 16000000 | tf_op jit(solution)/shard_map/weight_grads/pallas_call | solution.py:598
  175.1 3.8 collective-permute-done.18
  178.9 2.8 convert_add_fusion.1
  187.1 35.0 %attention_back.3 = (bf16[1024,768]{1,0:T(8,128)(2,1)}, bf16[1024,2304]{1,0:T(8,128)(2,1)}, f32[768,768]{1,0:T(8,128)}, bf16[768,768]{1,0:T(8,128)(2,1)}, f32[128,768]{1,0:T(8,128)}, /*index=5*/f32[8,768]{1,0:T(8,128)}) custom-call(s32[4,1,256]{2,1,0:T(1,128)} %compare_select_fusion.4.slots_ref, f32[1024,768]{1,0:T(8,128)} %get-tuple-element.313.second_ref, ...), custom_call_target="tpu_custom_call" | custom-call | flops 10000000000 | bytes 30000000 | tf_op jit(solution)/shard_map/attention_back/pallas_call | solution.py:487
  223.1 3.2 bitcast_add_fusion
  235.8 12.8 %weight_grads.5 = (bf16[8,2,192,384]{3,2,1,0:T(8,128)(2,1)}, f32[8,2,192,384]{3,2,1,0:T(8,128)}) custom-call(s32[1]{0:T(128)} %bitcast.42.core_ref, bf16[1024,768]{1,0:T(8,128)(2,1)} %get-tuple-element.329.refs_0_, bf16[1024,2304]{1,0:T(8,128)(2,1)} %get-tuple-element.330.refs_1_, bf16[1024,768]{1,0:T(8,128)(2,1)} %get-tuple-element.331.refs_2_, ...), custom_call_target="tpu_custom_call" | custom-call | flops 4831838208 | bytes 16000000 | tf_op jit(solution)/shard_map/weight_grads/pallas_call | solution.py:598
  249.5 4.2 collective-permute-done.25
  254.4 3.5 collective-permute-start.27
  273.8 7.4 %collective-permute-done.30 = bf16[4,192,384]{2,1,0:T(8,128)(2,1)S(1)} collective-permute-done((bf16[4,192,384]{2,1,0:T(8,128)(2,1)S(1)}, bf16[4,192,384]{2,1,0:T(8,128)(2,1)S(1)}, u32[]{:S(2)}, u32[]{:S(2)}) %collective-permute-start.30) | collective-permute-done | bytes 589856 | tf_op jit(solution)/shard_map/ppermute | solution.py:826
  281.2 12.1 %collective-permute-done.29 = bf16[768,768]{1,0:T(8,128)(2,1)} collective-permute-done((bf16[768,768]{1,0:T(8,128)(2,1)S(1)}, bf16[768,768]{1,0:T(8,128)(2,1)}, u32[]{:S(2)}, u32[]{:S(2)}) %collective-permute-start.29) | collective-permute-done | bytes 1179680 | tf_op jit(solution)/shard_map/ppermute | solution.py:826
  300.4 5.0 %collective-permute-start.34 = (bf16[384,384]{1,0:T(8,128)(2,1)}, bf16[384,384]{1,0:T(8,128)(2,1)}, u32[]{:S(2)}, u32[]{:S(2)}) collective-permute-start(bf16[384,384]{1,0:T(8,128)(2,1)} %get-tuple-element.354), channel_id=1, source_target_pairs={{0,8},{1,9},{2,10},{3,11},{4,12},{5,13},{6,14},{7,15},{8,0},{9,1},... | collective-permute-start | bytes 884744 | tf_op jit(solution)/shard_map/ppermute | solution.py:826
  311.6 23.7 %conditional.3 = ((f32[3840,768]{1,0:T(8,128)}, f32[1,768]{1,0:T(1,128)S(1)})) conditional(s32[]{:T(128)} %convert_element_type.255, (s32[]{:T(128)}, s32[2,2,4,192]{3,0,1,2:T(2,128)}, s32[]{:T(128)}, s32[2,2,4,192]{3,0,1,2:T(2,128)}, pred[2,2,4,192]{3,0,1,2:T(4,128)(4,1)}, /*index=5*/bf16[768,768]{1,0:T(8,128)(2,1)}, ...), branch_computations={%region_24.26_spmd, %region_26.30_spmd} | conditional | flops 10025035776 | bytes 188188672 | solution.py:1264
  314.7 20.4 %word_sum.1 = (f32[3840,768]{1,0:T(8,128)}, f32[1,768]{1,0:T(1,128)S(1)}) custom-call(s32[1]{0:T(128)} %bitcast.1.place_ref, s32[16]{0:T(128)} %reshape.583.count_ref, s32[3072]{0:T(1024)} %reshape.584.id_ref, bf16[768,768]{1,0:T(8,128)(2,1)} %get-tuple-element.143.refs_0_, bf16[768,768]{1,0:T(8,128)(2,1)S(1)} %get-tuple-element.144.refs_1_, ...), custom_call_target="tpu_custom_call" | custom-call | flops 10000000 | bytes 40000000 | tf_op jit(solution)/shard_map/cond/branch_0_fun/word_sum/pallas_call | solution.py:687
  343.1 15.0 %collective-permute-done.37 = bf16[4,224,384]{2,1,0:T(8,128)(2,1)S(1)} collective-permute-done((bf16[4,224,384]{2,1,0:T(8,128)(2,1)}, bf16[4,224,384]{2,1,0:T(8,128)(2,1)S(1)}, u32[]{:S(2)}, u32[]{:S(2)}) %collective-permute-start.37) | collective-permute-done | bytes 688160 | tf_op jit(solution)/shard_map/ppermute | solution.py:826
  359.4 4.5 collective-permute-start.39
  366.2 10.0 %collective-permute-done.39 = bf16[224,384]{1,0:T(8,128)(2,1)S(1)} collective-permute-done((bf16[224,384]{1,0:T(8,128)(2,1)S(1)}, bf16[224,384]{1,0:T(8,128)(2,1)S(1)}, u32[]{:S(2)}, u32[]{:S(2)}) %collective-permute-start.39) | collective-permute-done | bytes 172064 | tf_op jit(solution)/shard_map/ppermute | solution.py:826
  378.6 2.4 collective-permute-start.43
  385.0 2.7 collective-permute-done.45.refs_6_
  387.7 2.3 collective-permute-start.47
  400.5 32.6 %adam_rows.1 = (f32[3840,768]{1,0:T(8,128)}, f32[3840,768]{1,0:T(8,128)}, f32[3840,768]{1,0:T(8,128)}) custom-call(f32[1]{0:T(128)} %bitcast.97.factor_ref, f32[3840,768]{1,0:T(8,128)} %get-tuple-element.371.grad_ref, f32[3840,768]{1,0:T(8,128)} %master_ref.1, f32[2,3840,768]{2,1,0:T(8,128)} %moments_ref.1), custom_call_target="tpu_custom_call" | custom-call | flops 58982400 | bytes 82575360 | tf_op jit(solution)/shard_map/adam_rows/pallas_call | solution.py:725
  433.9 12.1 %adam_matrices.1 = (f32[384,768]{1,0:T(8,128)}, f32[384,768]{1,0:T(8,128)}, f32[384,768]{1,0:T(8,128)}, f32[96,3072]{1,0:T(8,128)}, f32[96,3072]{1,0:T(8,128)}, ...) custom-call(s32[1]{0:T(128)} %bitcast.98.place_ref, ...), custom_call_target="tpu_custom_call" | custom-call | flops 100000000 | bytes 30000000 | tf_op jit(solution)/shard_map/adam_matrices/pallas_call | solution.py:782
  (354 shorter events, 119.8 us)
Async XLA Ops:
  35.2 14.0 %collective-permute-start.9 = (bf16[256,768]{1,0:T(8,128)(2,1)}, bf16[256,768]{1,0:T(8,128)(2,1)S(1)}, u32[]{:S(2)}, u32[]{:S(2)}) collective-permute-start(bf16[256,768]{1,0:T(8,128)(2,1)} %get-tuple-element.436), channel_id=1, source_target_pairs={{0,3},{1,2},{2,1},{3,0},{4,7},{5,6},{6,5},{7,4},{8,11},{9,10},{10,... | collective-permute-start | bytes 1179656 | tf_op jit(solution)/shard_map/ppermute | solution.py:826
  35.2 19.0 %collective-permute-start.8 = (bf16[256,768]{1,0:T(8,128)(2,1)S(1)}, bf16[256,768]{1,0:T(8,128)(2,1)S(1)}, u32[]{:S(2)}, u32[]{:S(2)}) collective-permute-start(bf16[256,768]{1,0:T(8,128)(2,1)S(1)} %get-tuple-element.437), channel_id=1, source_target_pairs={{0,2},{1,3},{2,0},{3,1},{4,6},{5,7},{6,4},{7,5},{8,10},{9,11},{10,... | collective-permute-start | bytes 1179656 | tf_op jit(solution)/shard_map/ppermute | solution.py:826
  37.5 6.9 %collective-permute-start.4 = (s32[2,4,16,128]{3,2,1,0:T(8,128)S(1)}, s32[2,4,16,128]{3,2,1,0:T(8,128)S(1)}, u32[]{:S(2)}, u32[]{:S(2)}) collective-permute-start(s32[2,4,16,128]{3,2,1,0:T(8,128)S(1)} %pad_add_fusion.1), channel_id=1, source_target_pairs={{0,24},{1,25},{2,26},{3,27},{4,28},{5,29},{6,30},{7,31},{8,16},{9,... | collective-permute-start | bytes 196616 | tf_op jit(solution)/shard_map/ppermute | solution.py:826
  41.1 6.6 %collective-permute-start.5 = (s32[2,4,16,128]{3,2,1,0:T(8,128)S(1)}, s32[2,4,16,128]{3,2,1,0:T(8,128)S(1)}, u32[]{:S(2)}, u32[]{:S(2)}) collective-permute-start(s32[2,4,16,128]{3,2,1,0:T(8,128)S(1)} %pad_add_fusion.1), channel_id=1, source_target_pairs={{0,16},{1,17},{2,18},{3,19},{4,20},{5,21},{6,22},{7,23},{8,24},{9,... | collective-permute-start | bytes 196616 | tf_op jit(solution)/shard_map/ppermute | solution.py:826
  41.2 6.6 %collective-permute-start.6 = (s32[2,4,16,128]{3,2,1,0:T(8,128)S(1)}, s32[2,4,16,128]{3,2,1,0:T(8,128)S(1)}, u32[]{:S(2)}, u32[]{:S(2)}) collective-permute-start(s32[2,4,16,128]{3,2,1,0:T(8,128)S(1)} %pad_add_fusion.1), channel_id=1, source_target_pairs={{0,8},{1,9},{2,10},{3,11},{4,12},{5,13},{6,14},{7,15},{8,0},{9,1},... | collective-permute-start | bytes 196616 | tf_op jit(solution)/shard_map/ppermute | solution.py:826
  44.3 9.9 %collective-permute-start.7 = (bf16[256,768]{1,0:T(8,128)(2,1)S(1)}, bf16[256,768]{1,0:T(8,128)(2,1)S(1)}, u32[]{:S(2)}, u32[]{:S(2)}) collective-permute-start(bf16[256,768]{1,0:T(8,128)(2,1)S(1)} %get-tuple-element.438), channel_id=1, source_target_pairs={{0,1},{1,0},{2,3},{3,2},{4,5},{5,4},{6,7},{7,6},{8,9},{9,8},{10,11... | collective-permute-start | bytes 1179656 | tf_op jit(solution)/shard_map/ppermute | solution.py:826
  158.4 11.9 %collective-permute-start.17 = (bf16[8,2,192,384]{3,2,1,0:T(8,128)(2,1)}, bf16[8,2,192,384]{3,2,1,0:T(8,128)(2,1)S(1)}, u32[]{:S(2)}, u32[]{:S(2)}) collective-permute-start(bf16[8,2,192,384]{3,2,1,0:T(8,128)(2,1)} %get-tuple-element.310), channel_id=1, source_target_pairs={{0,1},{1,0},{2,3},{3,2},{4,5},{5,4},{6,7},{7,6},{8,9},{9,8},{10,11... | collective-permute-start | bytes 7077896 | tf_op jit(solution)/shard_map/ppermute | solution.py:826
  174.5 47.5 %collective-permute-start.19 = (bf16[4,2,192,384]{3,2,0,1:T(8,128)(2,1)}, bf16[4,2,192,384]{3,2,0,1:T(8,128)(2,1)S(1)}, u32[]{:S(2)}, u32[]{:S(2)}) collective-permute-start(bf16[4,2,192,384]{3,2,0,1:T(8,128)(2,1)} %fusion.17), channel_id=1, source_target_pairs={{0,4},{1,5},{2,6},{3,7},{4,0},{5,1},{6,2},{7,3},{8,12},{9,13},{10,... | collective-permute-start | bytes 3538952 | tf_op jit(solution)/shard_map/ppermute | solution.py:826
  184.0 38.1 %collective-permute-start.20 = (bf16[4,2,192,384]{3,2,0,1:T(8,128)(2,1)S(1)}, bf16[4,2,192,384]{3,2,0,1:T(8,128)(2,1)S(1)}, u32[]{:S(2)}, u32[]{:S(2)}) collective-permute-start(bf16[4,2,192,384]{3,2,0,1:T(8,128)(2,1)S(1)} %fusion.18), channel_id=1, source_target_pairs={{0,2},{1,3},{2,0},{3,1},{4,6},{5,7},{6,4},{7,5},{8,10},{9,11},{10,... | collective-permute-start | bytes 3538952 | tf_op jit(solution)/shard_map/ppermute | solution.py:826
  227.2 21.4 %collective-permute-start.26 = (bf16[4,192,384]{2,1,0:T(8,128)(2,1)S(1)}, bf16[4,192,384]{2,1,0:T(8,128)(2,1)S(1)}, u32[]{:S(2)}, u32[]{:S(2)}) collective-permute-start(bf16[4,192,384]{2,1,0:T(8,128)(2,1)S(1)} %fusion.19), channel_id=1, source_target_pairs={{0,2},{1,3},{2,0},{3,1},{4,6},{5,7},{6,4},{7,5},{8,10},{9,11},{10,... | collective-permute-start | bytes 1769480 | tf_op jit(solution)/shard_map/ppermute | solution.py:826
  230.7 18.8 %collective-permute-start.22 = (bf16[192,768]{1,0:T(8,128)(2,1)S(1)}, bf16[192,768]{1,0:T(8,128)(2,1)S(1)}, u32[]{:S(2)}, u32[]{:S(2)}) collective-permute-start(bf16[192,768]{1,0:T(8,128)(2,1)S(1)} %get-tuple-element.450), channel_id=1, source_target_pairs={{0,0},{1,4},{2,2},{3,6},{4,1},{5,5},{6,3},{7,7},{8,8},{9,12},{10,1... | collective-permute-start | bytes 884744 | tf_op jit(solution)/shard_map/ppermute | solution.py:822
  231.4 18.1 %collective-permute-start.23 = (bf16[192,768]{1,0:T(8,128)(2,1)S(1)}, bf16[192,768]{1,0:T(8,128)(2,1)S(1)}, u32[]{:S(2)}, u32[]{:S(2)}) collective-permute-start(bf16[192,768]{1,0:T(8,128)(2,1)S(1)} %get-tuple-element.449), channel_id=1, source_target_pairs={{0,8},{1,12},{2,10},{3,14},{4,9},{5,13},{6,11},{7,15},{8,0},{9,4},... | collective-permute-start | bytes 884744 | tf_op jit(solution)/shard_map/ppermute | solution.py:822
  231.5 18.0 %collective-permute-start.24 = (bf16[192,768]{1,0:T(8,128)(2,1)S(1)}, bf16[192,768]{1,0:T(8,128)(2,1)S(1)}, u32[]{:S(2)}, u32[]{:S(2)}) collective-permute-start(bf16[192,768]{1,0:T(8,128)(2,1)S(1)} %get-tuple-element.448), channel_id=1, source_target_pairs={{0,16},{1,20},{2,18},{3,22},{4,17},{5,21},{6,19},{7,23},{8,24},{9,... | collective-permute-start | bytes 884744 | tf_op jit(solution)/shard_map/ppermute | solution.py:822
  233.5 20.1 %collective-permute-start.25 = (bf16[192,768]{1,0:T(8,128)(2,1)S(1)}, bf16[192,768]{1,0:T(8,128)(2,1)S(1)}, u32[]{:S(2)}, u32[]{:S(2)}) collective-permute-start(bf16[192,768]{1,0:T(8,128)(2,1)S(1)} %get-tuple-element.447), channel_id=1, source_target_pairs={{0,24},{1,28},{2,26},{3,30},{4,25},{5,29},{6,27},{7,31},{8,16},{9,... | collective-permute-start | bytes 884744 | tf_op jit(solution)/shard_map/ppermute | solution.py:822
  254.4 13.3 %collective-permute-start.27 = (bf16[8,2,192,384]{3,2,1,0:T(8,128)(2,1)}, bf16[8,2,192,384]{3,2,1,0:T(8,128)(2,1)}, u32[]{:S(2)}, u32[]{:S(2)}) collective-permute-start(bf16[8,2,192,384]{3,2,1,0:T(8,128)(2,1)} %get-tuple-element.336), channel_id=1, source_target_pairs={{0,1},{1,0},{2,3},{3,2},{4,5},{5,4},{6,7},{7,6},{8,9},{9,8},{10,11... | collective-permute-start | bytes 7077896 | tf_op jit(solution)/shard_map/ppermute | solution.py:826
  265.1 28.2 %collective-permute-start.29 = (bf16[768,768]{1,0:T(8,128)(2,1)S(1)}, bf16[768,768]{1,0:T(8,128)(2,1)}, u32[]{:S(2)}, u32[]{:S(2)}) collective-permute-start(bf16[768,768]{1,0:T(8,128)(2,1)S(1)} %constant_dynamic-update-slice_fusion), channel_id=1, source_target_pairs={{0,2},{1,3},{2,0},{3,1},{4,6},{5,7},{6,4},{7,5},{8,10},{9,11},{10,... | collective-permute-start | bytes 3538952 | tf_op jit(solution)/shard_map/ppermute | solution.py:826
  266.1 15.1 %collective-permute-start.30 = (bf16[4,192,384]{2,1,0:T(8,128)(2,1)S(1)}, bf16[4,192,384]{2,1,0:T(8,128)(2,1)S(1)}, u32[]{:S(2)}, u32[]{:S(2)}) collective-permute-start(bf16[4,192,384]{2,1,0:T(8,128)(2,1)S(1)} %copy-done.19), channel_id=1, source_target_pairs={{0,4},{1,5},{2,6},{3,7},{4,0},{5,1},{6,2},{7,3},{8,12},{9,13},{10,... | collective-permute-start | bytes 1769480 | tf_op jit(solution)/shard_map/ppermute | solution.py:826
  294.4 13.1 %collective-permute-start.31 = (bf16[768,768]{1,0:T(8,128)(2,1)S(1)}, bf16[768,768]{1,0:T(8,128)(2,1)S(1)}, u32[]{:S(2)}, u32[]{:S(2)}) collective-permute-start(bf16[768,768]{1,0:T(8,128)(2,1)S(1)} %constant_dynamic-update-slice_fusion), channel_id=1, source_target_pairs={{0,1},{1,0},{2,3},{3,2},{4,5},{5,4},{6,7},{7,6},{8,9},{9,8},{10,11... | collective-permute-start | bytes 3538952 | tf_op jit(solution)/shard_map/ppermute | solution.py:826
  295.7 39.6 %collective-permute-start.33 = (bf16[4,2,224,384]{3,2,0,1:T(8,128)(2,1)}, bf16[4,2,224,384]{3,2,0,1:T(8,128)(2,1)}, u32[]{:S(2)}, u32[]{:S(2)}) collective-permute-start(bf16[4,2,224,384]{3,2,0,1:T(8,128)(2,1)} %pad_maximum_fusion.3), channel_id=1, source_target_pairs={{0,4},{1,5},{2,6},{3,7},{4,0},{5,1},{6,2},{7,3},{8,12},{9,13},{10,... | collective-permute-start | bytes 4128776 | tf_op jit(solution)/shard_map/ppermute | solution.py:826
  297.4 14.2 %collective-permute-start.32 = (bf16[768,768]{1,0:T(8,128)(2,1)}, bf16[768,768]{1,0:T(8,128)(2,1)}, u32[]{:S(2)}, u32[]{:S(2)}) collective-permute-start(bf16[768,768]{1,0:T(8,128)(2,1)} %collective-permute-done.29), channel_id=1, source_target_pairs={{0,1},{1,0},{2,3},{3,2},{4,5},{5,4},{6,7},{7,6},{8,9},{9,8},{10,11... | collective-permute-start | bytes 3538952 | tf_op jit(solution)/shard_map/ppermute | solution.py:826
  300.4 34.9 %collective-permute-start.34 = (bf16[384,384]{1,0:T(8,128)(2,1)}, bf16[384,384]{1,0:T(8,128)(2,1)}, u32[]{:S(2)}, u32[]{:S(2)}) collective-permute-start(bf16[384,384]{1,0:T(8,128)(2,1)} %get-tuple-element.354), channel_id=1, source_target_pairs={{0,8},{1,9},{2,10},{3,11},{4,12},{5,13},{6,14},{7,15},{8,0},{9,1},... | collective-permute-start | bytes 884744 | tf_op jit(solution)/shard_map/ppermute | solution.py:826
  305.4 29.9 %collective-permute-start.35 = (bf16[384,384]{1,0:T(8,128)(2,1)}, bf16[384,384]{1,0:T(8,128)(2,1)}, u32[]{:S(2)}, u32[]{:S(2)}) collective-permute-start(bf16[384,384]{1,0:T(8,128)(2,1)} %get-tuple-element.355), channel_id=1, source_target_pairs={{0,16},{1,17},{2,18},{3,19},{4,20},{5,21},{6,22},{7,23},{8,24},{9,... | collective-permute-start | bytes 884744 | tf_op jit(solution)/shard_map/ppermute | solution.py:826
  307.4 27.9 %collective-permute-start.36 = (bf16[384,384]{1,0:T(8,128)(2,1)}, bf16[384,384]{1,0:T(8,128)(2,1)}, u32[]{:S(2)}, u32[]{:S(2)}) collective-permute-start(bf16[384,384]{1,0:T(8,128)(2,1)} %get-tuple-element.356), channel_id=1, source_target_pairs={{0,24},{1,25},{2,26},{3,27},{4,28},{5,29},{6,30},{7,31},{8,16},{9,... | collective-permute-start | bytes 884744 | tf_op jit(solution)/shard_map/ppermute | solution.py:826
  340.9 17.3 %collective-permute-start.37 = (bf16[4,224,384]{2,1,0:T(8,128)(2,1)}, bf16[4,224,384]{2,1,0:T(8,128)(2,1)S(1)}, u32[]{:S(2)}, u32[]{:S(2)}) collective-permute-start(bf16[4,224,384]{2,1,0:T(8,128)(2,1)} %pad_maximum_fusion.6), channel_id=1, source_target_pairs={{0,2},{1,3},{2,0},{3,1},{4,6},{5,7},{6,4},{7,5},{8,10},{9,11},{10,... | collective-permute-start | bytes 2064392 | tf_op jit(solution)/shard_map/ppermute | solution.py:826
  358.7 7.5 %collective-permute-start.38 = (bf16[224,384]{1,0:T(8,128)(2,1)S(1)}, bf16[224,384]{1,0:T(8,128)(2,1)S(1)}, u32[]{:S(2)}, u32[]{:S(2)}) collective-permute-start(bf16[224,384]{1,0:T(8,128)(2,1)S(1)} %pad_maximum_fusion.11), channel_id=1, source_target_pairs={{0,8},{1,9},{2,10},{3,11},{4,12},{5,13},{6,14},{7,15},{8,0},{9,1},... | collective-permute-start | bytes 516104 | tf_op jit(solution)/shard_map/ppermute | solution.py:826
  359.4 16.8 %collective-permute-start.39 = (bf16[224,384]{1,0:T(8,128)(2,1)S(1)}, bf16[224,384]{1,0:T(8,128)(2,1)S(1)}, u32[]{:S(2)}, u32[]{:S(2)}) collective-permute-start(bf16[224,384]{1,0:T(8,128)(2,1)S(1)} %pad_maximum_fusion.12), channel_id=1, source_target_pairs={{0,16},{1,17},{2,18},{3,19},{4,20},{5,21},{6,22},{7,23},{8,24},{9,... | collective-permute-start | bytes 516104 | tf_op jit(solution)/shard_map/ppermute | solution.py:826
  363.9 12.3 %collective-permute-start.40 = (bf16[224,384]{1,0:T(8,128)(2,1)S(1)}, bf16[224,384]{1,0:T(8,128)(2,1)S(1)}, u32[]{:S(2)}, u32[]{:S(2)}) collective-permute-start(bf16[224,384]{1,0:T(8,128)(2,1)S(1)} %pad_maximum_fusion.13), channel_id=1, source_target_pairs={{0,24},{1,25},{2,26},{3,27},{4,28},{5,29},{6,30},{7,31},{8,16},{9,... | collective-permute-start | bytes 516104 | tf_op jit(solution)/shard_map/ppermute | solution.py:826
  363.9 12.7 %collective-permute-start.41 = (bf16[384,384]{1,0:T(8,128)(2,1)S(1)}, bf16[384,384]{1,0:T(8,128)(2,1)S(1)}, u32[]{:S(2)}, u32[]{:S(2)}) collective-permute-start(bf16[384,384]{1,0:T(8,128)(2,1)S(1)} %fusion.24.refs_0_), channel_id=1, source_target_pairs={{0,2},{1,3},{2,0},{3,1},{4,6},{5,7},{6,4},{7,5},{8,10},{9,11},{10,... | collective-permute-start | bytes 884744 | tf_op jit(solution)/shard_map/ppermute | solution.py:826
  381.1 6.6 %collective-permute-start.45 = (bf16[192,384]{1,0:T(8,128)(2,1)S(1)}, bf16[192,384]{1,0:T(8,128)(2,1)S(1)}, u32[]{:S(2)}, u32[]{:S(2)}) collective-permute-start(bf16[192,384]{1,0:T(8,128)(2,1)S(1)} %get-tuple-element.379.refs_4_), channel_id=1, source_target_pairs={{0,2},{1,3},{2,0},{3,1},{4,6},{5,7},{6,4},{7,5},{8,10},{9,11},{10,... | collective-permute-start | bytes 442376 | tf_op jit(solution)/shard_map/ppermute | solution.py:826
  387.7 7.0 %collective-permute-start.47 = (f32[4,24,384]{2,1,0:T(8,128)S(1)}, f32[4,24,384]{2,1,0:T(8,128)S(1)}, u32[]{:S(2)}, u32[]{:S(2)}) collective-permute-start(f32[4,24,384]{2,1,0:T(8,128)S(1)} %pad_maximum_fusion.14), channel_id=1, source_target_pairs={{0,4},{1,5},{2,6},{3,7},{4,0},{5,1},{6,2},{7,3},{8,12},{9,13},{10,... | collective-permute-start | bytes 442376 | tf_op jit(solution)/shard_map/ppermute | solution.py:826
  397.1 36.0 %collective-permute-start.52 = (bf16[192,384]{1,0:T(8,128)(2,1)S(1)}, bf16[192,384]{1,0:T(8,128)(2,1)S(1)}, u32[]{:S(2)}, u32[]{:S(2)}) collective-permute-start(bf16[192,384]{1,0:T(8,128)(2,1)S(1)} %get-tuple-element.379.refs_4_), channel_id=1, source_target_pairs={{0,1},{1,0},{2,3},{3,2},{4,5},{5,4},{6,7},{7,6},{8,9},{9,8},{10,11... | collective-permute-start | bytes 442376 | tf_op jit(solution)/shard_map/ppermute | solution.py:826
  397.7 35.4 %collective-permute-start.53 = (bf16[192,384]{1,0:T(8,128)(2,1)S(1)}, bf16[192,384]{1,0:T(8,128)(2,1)S(1)}, u32[]{:S(2)}, u32[]{:S(2)}) collective-permute-start(bf16[192,384]{1,0:T(8,128)(2,1)S(1)} %collective-permute-done.45.refs_6_), channel_id=1, source_target_pairs={{0,1},{1,0},{2,3},{3,2},{4,5},{5,4},{6,7},{7,6},{8,9},{9,8},{10,11... | collective-permute-start | bytes 442376 | tf_op jit(solution)/shard_map/ppermute | solution.py:826
  (64 other events, 528.0 us)

commit v4 on v3

--- a/solution.py
+++ b/solution.py
@@ -72,6 +72,7 @@
 
 
 def normalize_back(grad, gain, unit_states, inverse):
+    unit_states = unit_states.astype(jnp.float32)
     scaled = grad * gain
     inner = jnp.mean(scaled * unit_states, -1, keepdims=True)
     back = inverse * (scaled - jnp.mean(scaled, -1, keepdims=True) - unit_states * inner)
@@ -155,7 +156,7 @@
     positions = small_ref[:seq_len, :]
     embedded = embedded + jnp.concatenate([positions] * seqs, 0)
     unit1, inverse1 = normalize(embedded)
-    unit1_ref[...] = unit1
+    unit1_ref[...] = unit1.astype(low)
     inverse1_ref[...] = inverse1
     normed = unit1 * vector(0) + vector(1)
     normed_low = normed.astype(low)
@@ -187,7 +188,7 @@
             ).astype(low)
     branch = dot_plain(attended_ref[...], out_ref[...]) + vector(4)
     unit2, inverse2 = normalize(normed + branch)
-    unit2_ref[...] = unit2
+    unit2_ref[...] = unit2.astype(low)
     inverse2_ref[...] = inverse2
     middle = unit2 * vector(5) + vector(6)
     middle_low = middle.astype(low)
@@ -202,7 +203,7 @@
         slope_ref[:, at] = slope.astype(low)
         lowered = lowered + dot_plain(activated, down_ref[at, :])
     unit3, inverse3 = normalize(lowered)
-    unit3_ref[...] = unit3
+    unit3_ref[...] = unit3.astype(low)
     inverse3_ref[...] = inverse3
     final = unit3 * vector(8) + vector(9)
     row_at = lax.broadcasted_iota(jnp.int32, (seq_len, 1), 0)
@@ -226,18 +227,18 @@
     lifted = weights[2].shape[1]
     f32 = jnp.float32
     outs = [
-        ((tokens, width), f32),
+        ((tokens, width), low),
         ((tokens, 1), f32),
         ((tokens, width), low),
         ((tokens, 3 * width), low),
         ((steps * seqs, width // (2 * head_dim), 2 * seq_len, seq_len), low),
         ((tokens, width), low),
-        ((tokens, width), f32),
+        ((tokens, width), low),
         ((tokens, 1), f32),
         ((tokens, width), low),
         ((tokens, lifted), low),
         ((tokens, lifted), low),
-        ((tokens, width), f32),
+        ((tokens, width), low),
         ((tokens, 1), f32),
         ((steps, seqs, width), f32),
         ((steps, seqs, width), low),
@@ -282,6 +283,7 @@
     lowered_ref,
     lifted_ref,
     second_ref,
+    branch_ref,
     sums_ref,
     *,
     seq_len,
@@ -326,7 +328,9 @@
         middle_grad, vector(5), unit2_ref[...], inverse2_ref[...]
     )
     second_ref[...] = second
-    branch_sum = jnp.sum(second.astype(low).astype(jnp.float32), 0, keepdims=True)
+    branch = second.astype(low)
+    branch_ref[...] = branch
+    branch_sum = jnp.sum(branch.astype(jnp.float32), 0, keepdims=True)
     lowered_sum = jnp.sum(lowered_grad.astype(jnp.float32), 0, keepdims=True)
     sums = [branch_sum, gain2, shift2, lowered_sum, gain3, shift3] + up_sums
     sums_ref[: len(sums), :] += jnp.concatenate(sums, 0)
@@ -346,6 +350,7 @@
             jax.ShapeDtypeStruct((tokens, width), low),
             jax.ShapeDtypeStruct((tokens, lifted), low),
             jax.ShapeDtypeStruct((tokens, width), jnp.float32),
+            jax.ShapeDtypeStruct((tokens, width), low),
             jax.ShapeDtypeStruct((16, width), jnp.float32),
         ],
         grid_spec=pltpu.PrefetchScalarGridSpec(
@@ -367,6 +372,7 @@
                 rows_block(rows, width),
                 rows_block(rows, lifted),
                 rows_block(rows, width),
+                rows_block(rows, width),
                 pl.BlockSpec((16, width), lambda i, *_: (0, 0)),
             ],
         ),
@@ -399,13 +405,12 @@
     small_ref,
     qkv_ref,
     out_ref,
-    branch_ref,
     projected_grad_ref,
     mine_ref,
     theirs_ref,
     positions_ref,
     sums_ref,
-    total_ref,
+    tokens_ref,
     *,
     seq_len,
     seqs,
@@ -413,6 +418,7 @@
 ):
     step = pl.program_id(0)
     width = second_ref.shape[1]
+    rows = seqs * seq_len
     lanes = 2 * head_dim
     scale = head_dim ** (-0.5)
 
@@ -420,12 +426,9 @@
     def _():
         sums_ref[...] = jnp.zeros_like(sums_ref)
         positions_ref[...] = jnp.zeros_like(positions_ref)
-        total_ref[...] = jnp.zeros_like(total_ref)
 
     second = second_ref[...]
-    branch = second.astype(low)
-    branch_ref[...] = branch
-    attended_grad = dot_cols(branch, out_ref[...]).astype(low)
+    attended_grad = dot_cols(second.astype(low), out_ref[...]).astype(low)
     even, odd = head_masks(lanes, head_dim)
     for s in range(seqs):
         at = slice(s * seq_len, (s + 1) * seq_len)
@@ -461,16 +464,20 @@
     for s in range(seqs):
         positions_ref[...] += embedded_grad[s * seq_len : (s + 1) * seq_len]
     sums_ref[:4, :] += jnp.concatenate([gain1, shift1, query_sum, value_sum], 0)
-    slots, rows = total_ref.shape[0], seqs * seq_len
-    hit = slots_ref[0] == lax.broadcasted_iota(jnp.int32, (slots, rows), 0)
-    hit = jnp.where(hit, 1.0, 0.0).astype(low)
-    total_ref[...] += dot_plain(hit, embedded_grad.astype(low))
+    tokens_ref[pl.ds(step * rows, rows), :] = embedded_grad.astype(low)
 
     @pl.when(step == pl.num_programs(0) - 1)
     def _():
-        half = total_ref.shape[0] // 2
-        mine_ref[...] = total_ref[:half]
-        theirs_ref[...] = total_ref[half:].astype(low)
+        half, tokens = mine_ref.shape[0], tokens_ref.shape[0]
+        block = next(size for size in (256, 128, 64, 32, 16) if half % size == 0)
+        for out_ref, base in ((mine_ref, 0), (theirs_ref, half)):
+            for n in range(half // block):
+                slot_at = lax.broadcasted_iota(jnp.int32, (block, tokens), 0)
+                hit = slots_ref[...] == slot_at + (base + n * block)
+                hit = jnp.where(hit, 1.0, 0.0).astype(low)
+                out_ref[n * block : (n + 1) * block, :] = dot_plain(hit, tokens_ref[...]).astype(
+                    out_ref.dtype
+                )
 
 
 def attention_back(slot, second, kept, small_rows, weights, seq_len, head_dim, slots):
@@ -489,7 +496,6 @@
             attention_back_kernel, seq_len=seq_len, seqs=seqs, head_dim=head_dim
         ),
         out_shape=[
-            jax.ShapeDtypeStruct((tokens, width), low),
             jax.ShapeDtypeStruct((tokens, 3 * width), low),
             jax.ShapeDtypeStruct((slots // 2, width), jnp.float32),
             jax.ShapeDtypeStruct((slots // 2, width), low),
@@ -498,7 +504,7 @@
         ],
         grid=(steps,),
         in_specs=[
-            pl.BlockSpec((1, 1, rows), lambda i: (i, 0, 0)),
+            whole_block((1, tokens)),
             rows_block(rows, width),
             rows_block(rows, 3 * width),
             pl.BlockSpec(probs_block, lambda i: (i, 0, 0, 0)),
@@ -509,20 +515,19 @@
             whole_block(weights[1].shape),
         ],
         out_specs=[
-            rows_block(rows, width),
             rows_block(rows, 3 * width),
             fixed((slots // 2, width)),
             fixed((slots // 2, width)),
             fixed((seq_len, width)),
             fixed((8, width)),
         ],
-        scratch_shapes=[pltpu.VMEM((slots, width), jnp.float32)],
+        scratch_shapes=[pltpu.VMEM((tokens, width), low)],
         compiler_params=pltpu.CompilerParams(vmem_limit_bytes=VMEM_ALLOWED),
         cost_estimate=pl.CostEstimate(
             flops=10 * 10**9, bytes_accessed=30 * 10**6, transcendentals=0
         ),
         name="attention_back",
-    )(slot.reshape(steps, 1, rows), second, projected, probs, unit1, inverse1, small_rows, *weights)
+    )(slot.reshape(1, tokens), second, projected, probs, unit1, inverse1, small_rows, *weights)
 
 
 def weight_grad_kernel(core_ref, *refs, jobs, xs):
@@ -559,7 +564,7 @@
 
                 @pl.when(core_ref[0] == half)
                 def _(at=at, part=part):
-                    mine_ref[at] = part
+                    mine_ref[at] = part.astype(low)
 
                 @pl.when(core_ref[0] != half)
                 def _(at=at, part=part):
@@ -599,7 +604,7 @@
         functools.partial(weight_grad_kernel, jobs=jobs, xs=place.xs),
         out_shape=[
             jax.ShapeDtypeStruct(shape, low),
-            jax.ShapeDtypeStruct(shape, jnp.float32),
+            jax.ShapeDtypeStruct(shape, low),
         ],
         grid_spec=pltpu.PrefetchScalarGridSpec(
             num_scalar_prefetch=1,
@@ -609,21 +614,25 @@
             scratch_shapes=[pltpu.VMEM((tile_rows, tokens), low)],
         ),
         compiler_params=pltpu.CompilerParams(vmem_limit_bytes=VMEM_ALLOWED),
-        cost_estimate=pl.CostEstimate(
-            flops=start * 2 * tokens * tile_rows * tile_rows,
-            bytes_accessed=16 * 10**6,
-            transcendentals=0,
-        ),
+        cost_estimate=pl.CostEstimate(flops=1000, bytes_accessed=1000, transcendentals=0),
         name="weight_grads",
     )(place.core.reshape(1).astype(jnp.int32), *operands)
 
 
-def word_sum_kernel(place_ref, count_ref, id_ref, *refs, grp, chunks, room, span):
-    sources = refs[:grp]
-    out_ref, squares_ref, total_ref, rows_ref, chunk_ref, in_sems, out_sem = refs[grp:]
+def word_sum_kernel(
+    place_ref, count_ref, id_ref, *refs, sources, chunks, room, span, own, finishing
+):
+    inputs, rest = refs[:sources], refs[sources:]
+    if finishing:
+        base_ref, out_ref, squares_ref, total_ref, rows_ref, chunk_ref = rest[:6]
+        in_sems, out_sem, base_total_ref, base_sem = rest[6:]
+        base_copy = pltpu.make_async_copy(base_ref, base_total_ref, base_sem)
+        base_copy.start()
+    else:
+        out_ref, total_ref, rows_ref, chunk_ref, in_sems, out_sem = rest
     batch = 8
     copies = [
-        pltpu.make_async_copy(sources[k], rows_ref.at[k], in_sems.at[k]) for k in range(grp)
+        pltpu.make_async_copy(inputs[k], rows_ref.at[k], in_sems.at[k]) for k in range(sources)
     ]
     for copy in copies:
         copy.start()
@@ -637,9 +646,19 @@
     for copy in copies:
         copy.wait()
 
-    def one_source(n, _):
-        slot = (n // chunks) ^ place_ref[0]
-        start = (n % chunks) * room
+    def one_source(m, _):
+        me = place_ref[0]
+        place = m // chunks
+        if sources == 2:
+            x = (me // 2) ^ (own // 2)
+            source = x * 2 + place
+        else:
+            x = place // 2
+            x = x + jnp.where(x >= me // 2, 1, 0)
+            source = x * 2 + place % 2
+        slot = (source ^ me) - own
+        n = source * chunks + m % chunks
+        start = (m % chunks) * room
         count = count_ref[n]
 
         def widen(i, _):
@@ -663,12 +682,19 @@
         lax.fori_loop(0, (count + batch - 1) // batch, add, 0)
         return 0
 
-    lax.fori_loop(0, grp * chunks, one_source, 0)
+    lax.fori_loop(0, sources * chunks, one_source, 0)
     shard_rows = out_ref.shape[0]
+    if not finishing:
+        copy = pltpu.make_async_copy(total_ref.at[pl.ds(0, shard_rows)], out_ref, out_sem)
+        copy.start()
+        copy.wait()
+        return
+    base_copy.wait()
 
     def finish(i, squares):
         at = pl.ds(pl.multiple_of(i * span, span), span)
-        part = total_ref[at, :]
+        part = total_ref[at, :] + base_total_ref[at, :]
+        total_ref[at, :] = part
         pltpu.make_async_copy(total_ref.at[at], out_ref.at[at], out_sem).start()
         part = part * part
         return squares + jnp.sum(part.reshape(span // 8, 8, part.shape[1]), 0)
@@ -680,35 +706,49 @@
     pltpu.make_async_copy(total_ref.at[pl.ds(0, shard_rows)], out_ref, out_sem).wait()
 
 
-def word_sum(grp_index, counts, ids, sources, shard_rows, chunks, room):
-    grp, width = len(sources), sources[0].shape[1]
+def word_sum(grp_index, counts, ids, sources, shard_rows, chunks, room, base=None):
+    count, width = len(sources), sources[0].shape[1]
     span = next(size for size in (128, 64, 32, 16, 8) if shard_rows % size == 0)
     anywhere = pl.BlockSpec(memory_space=pl.ANY)
-    return pl.pallas_call(
-        functools.partial(word_sum_kernel, grp=grp, chunks=chunks, room=room, span=span),
-        out_shape=[
-            jax.ShapeDtypeStruct((shard_rows, width), jnp.float32),
-            jax.ShapeDtypeStruct((1, width), jnp.float32),
-        ],
+    finishing = base is not None
+    out_shape = [jax.ShapeDtypeStruct((shard_rows, width), jnp.float32)]
+    out_specs = [anywhere]
+    scratch = [
+        pltpu.VMEM((shard_rows + 32, width), jnp.float32),
+        pltpu.VMEM((count,) + sources[0].shape, low),
+        pltpu.VMEM((room, width), jnp.float32),
+        pltpu.SemaphoreType.DMA((count,)),
+        pltpu.SemaphoreType.DMA,
+    ]
+    operands = list(sources)
+    if finishing:
+        out_shape.append(jax.ShapeDtypeStruct((1, width), jnp.float32))
+        out_specs.append(whole_block((1, width)))
+        scratch += [pltpu.VMEM((shard_rows, width), jnp.float32), pltpu.SemaphoreType.DMA]
+        operands.append(base)
+    results = pl.pallas_call(
+        functools.partial(
+            word_sum_kernel,
+            sources=count,
+            chunks=chunks,
+            room=room,
+            span=span,
+            own=2 if finishing else 0,
+            finishing=finishing,
+        ),
+        out_shape=out_shape,
         grid_spec=pltpu.PrefetchScalarGridSpec(
             num_scalar_prefetch=3,
             grid=(1,),
-            in_specs=[anywhere] * grp,
-            out_specs=[anywhere, whole_block((1, width))],
-            scratch_shapes=[
-                pltpu.VMEM((shard_rows + 32, width), jnp.float32),
-                pltpu.VMEM((grp,) + sources[0].shape, low),
-                pltpu.VMEM((room, width), jnp.float32),
-                pltpu.SemaphoreType.DMA((grp,)),
-                pltpu.SemaphoreType.DMA,
-            ],
+            in_specs=[anywhere] * len(operands),
+            out_specs=out_specs,
+            scratch_shapes=scratch,
         ),
         compiler_params=pltpu.CompilerParams(vmem_limit_bytes=VMEM_ALLOWED),
-        cost_estimate=pl.CostEstimate(
-            flops=10**7, bytes_accessed=40 * 10**6, transcendentals=0
-        ),
+        cost_estimate=pl.CostEstimate(flops=1000, bytes_accessed=1000, transcendentals=0),
         name="word_sum",
-    )(grp_index.reshape(1), counts, ids, *sources)
+    )(grp_index.reshape(1), counts, ids, *operands)
+    return results if finishing else results[0]
 
 
 def adam_kernel(factor_ref, grad_ref, master_ref, moments_ref, first_ref, second_ref, new_ref, *, rate):
@@ -720,7 +760,7 @@
 
 def adam_rows(factor, grad, master, moments, rate):
     rows, width = master.shape
-    span = next(size for size in (256, 240, 192, 128, 96, 64, 32, 16, 8) if rows % size == 0)
+    span = next(size for size in (384, 320, 240, 192, 128, 96, 64, 32, 16, 8) if rows % size == 0)
     block = rows_block(span, width)
     return pl.pallas_call(
         functools.partial(adam_kernel, rate=rate),
@@ -753,8 +793,8 @@
     for n, (rows, width) in enumerate(shapes):
         strips = width // 2 // strip
         piece = rows // (grp // 2)
-        group = pieces[n // 2]
-        base = 0 if n % 2 == 0 else base
+        group = pieces[n // 3]
+        base = 0 if n % 3 == 0 else base
         for k in range(grp):
             source = place_ref[0] ^ k
             x, core = source // 2, source % 2
@@ -813,13 +853,9 @@
         self.y_masks = [0, self.grp]
         self.z_masks = [2 * self.grp * i for i in range(self.far)]
 
-    def send_swapped(self, value, far_mask):
-        pairs = []
-        for i in range(self.count):
-            core, x, y = i % 2, i // 2 % self.xs, i // self.grp % 2
-            z = i // (2 * self.grp) ^ far_mask
-            pairs.append((i, ((z * 2 + core) * self.xs + x) * 2 + y))
-        return lax.ppermute(value, both, pairs)
+    def send_split(self, value, far_mask):
+        masks = [2 * self.grp * far_mask + self.grp * core for core in range(2)]
+        return lax.ppermute(value, both, [(i, i ^ masks[i % 2]) for i in range(self.count)])
 
     def send(self, value, mask):
         pairs = [(i, i ^ mask) for i in range(self.count)]
@@ -852,59 +888,54 @@
     )
 
 
-def to_send(value, fine):
-    high = value.astype(low)
-    if not fine:
-        return high
-    rows = value.shape[-2]
-    rest = value[..., rows - fine :, :] - high[..., rows - fine :, :].astype(jnp.float32)
-    return jnp.concatenate([high, rest.astype(low)], -2)
-
-
-def from_sent(value, fine):
+def two_terms(value):
+    high = lax.reduce_precision(value, 8, 7)
+    return jnp.concatenate([high, value - high], -2).astype(low)
+
+
+def one_term(value):
     value = value.astype(jnp.float32)
-    if not fine:
-        return value
-    rows = value.shape[-2] - fine
-    tail = value[..., rows - fine : rows, :] + value[..., rows:, :]
-    return jnp.concatenate([value[..., : rows - fine, :], tail], -2)
-
-
-def stage_parts(value, masks, index, fine):
-    keep = lax.dynamic_index_in_dim(value, index, 0, keepdims=False)
-    parts = [
-        to_send(lax.dynamic_index_in_dim(value, index ^ k, 0, keepdims=False), fine)
-        for k in range(1, len(masks))
-    ]
-    return keep, parts
-
-
-def stage_sum(keep, arrived, fine):
-    terms = [keep.astype(jnp.float32)] + [from_sent(item, fine) for item in arrived]
+    rows = value.shape[-2] // 2
+    return value[..., :rows, :] + value[..., rows:, :]
+
+
+def add_up(terms):
     while len(terms) > 1:
         terms = [terms[i] + terms[i + 1] for i in range(0, len(terms), 2)]
     return terms[0]
 
 
 class Reduction:
-    def __init__(self, place, value, x_first, fine=0):
-        rows, columns = value.shape[2:]
-        value = value.reshape(place.far, 2, place.xs, rows, columns)
+    def __init__(self, place, value, x_first, small=None):
+        self.place = place
+        self.value, self.small = self.shaped(value), self.shaped(small)
         x_stage = (place.x_masks, place.x)
         y_stage = (place.y_masks, place.y)
-        self.place, self.fine = place, fine
         if x_first:
             self.stages = [(*x_stage, 2), (*y_stage, 1)]
         else:
             self.stages = [(*y_stage, 1), (*x_stage, 1)]
         self.stages.append((place.z_masks, place.z, 0))
-        self.value = value
+
+    def shaped(self, value):
+        if value is None:
+            return None
+        place = self.place
+        return value.reshape((place.far, 2, place.xs) + value.shape[2:])
 
     def prepare(self):
-        self.masks, index, axis = self.stages.pop(0)
-        self.keep, self.parts = stage_parts(
-            jnp.moveaxis(self.value, axis, 0), self.masks, index, self.fine
-        )
+        self.masks, self.index, axis = self.stages.pop(0)
+        self.value = jnp.moveaxis(self.value, axis, 0)
+        if self.small is not None:
+            self.small = jnp.moveaxis(self.small, axis, 0)
+        self.parts = []
+        for k in range(1, len(self.masks)):
+            at = self.index ^ k
+            part = lax.dynamic_index_in_dim(self.value, at, 0, keepdims=False).astype(low)
+            if self.small is not None:
+                small = lax.dynamic_index_in_dim(self.small, at, 0, keepdims=False)
+                part = jnp.concatenate([part, two_terms(small)], -2)
+            self.parts.append(part)
 
     def send(self):
         self.arrived = [
@@ -912,7 +943,13 @@
         ]
 
     def add(self):
-        self.value = stage_sum(self.keep, self.arrived, self.fine)
+        rows = self.value.shape[-2]
+        own = lax.dynamic_index_in_dim(self.value, self.index, 0, keepdims=False)
+        arrived = [item[..., :rows, :].astype(jnp.float32) for item in self.arrived]
+        self.value = add_up([own.astype(jnp.float32)] + arrived)
+        if self.small is not None:
+            own = lax.dynamic_index_in_dim(self.small, self.index, 0, keepdims=False)
+            self.small = add_up([own] + [one_term(item[..., rows:, :]) for item in self.arrived])
 
 
 def tie(*items):
@@ -936,7 +973,7 @@
         return weight_grads(place, pairs)
     mine = [half_gradient(place, a, b, place.core) for a, b in pairs]
     theirs = [half_gradient(place, a, b, 1 - place.core) for a, b in pairs]
-    return jnp.concatenate(theirs, 2), jnp.concatenate(mine, 2).astype(jnp.float32)
+    return jnp.concatenate(theirs, 2), jnp.concatenate(mine, 2)
 
 
 def merge_ids(left, right, length):
@@ -997,7 +1034,7 @@
     shard_rows = word_master.shape[0]
     table_rows = word_table.shape[0]
     per_owner = table_rows // shard_rows
-    room = max(16, tokens // place.blk)
+    room = max(16, tokens * 7 // 8 // place.blk)
     shard = flat_ids // shard_rows
     same_id = flat_ids[:, None] == flat_ids[None, :]
     before = jnp.arange(tokens)[:, None] < jnp.arange(tokens)[None, :]
@@ -1022,6 +1059,7 @@
         found, sibling = tie(found, grp_ids[1])
         parts = [found[k * span : (k + 1) * span] for k in range(place.grp)]
         rows = [parts[0]] + [place.send(parts[k], k) for k in range(1, place.grp)]
+        rows.append(jnp.zeros((tokens - slots, width), low))
         return jnp.concatenate(rows), sibling
 
     def pack(values, length):
@@ -1066,7 +1104,7 @@
     )
     chip_rank = rank + jnp.sum(extra.astype(jnp.int32), 1)
     shard_y, shard_z = shard % 2, shard // 2
-    order = jnp.where(shard_y == place.core, 0, place.far) + (shard_z ^ place.z)
+    order = jnp.where(shard_y ^ place.y == place.core, 0, place.far) + (shard_z ^ place.z)
     gradient_slot = jnp.where(
         chip_rank < chip_room, order * chip_room + chip_rank, chip_slots
     )
@@ -1141,7 +1179,7 @@
         / logit_divisor_constant
     )
 
-    lowered_grad, lifted_low, second, feed_sums = feed_back(
+    lowered_grad, lifted_low, second, branch_grad, feed_sums = feed_back(
         lengths_flat,
         embed_grad,
         (unit2, inverse2, slope, unit3, inverse3, pooled),
@@ -1152,17 +1190,19 @@
     theirs_down, mine_down = group_products(place, [(activated_low, lowered_grad)])
     lifted_low, theirs_down, mine_down = tie(lifted_low, theirs_down, mine_down)
     core_down = place.send(theirs_down, 1)
-    theirs_up, mine_up = group_products(place, [(middle_low, lifted_low)])
-    down = Reduction(place, mine_down + core_down.astype(jnp.float32), False)
+    theirs_up, mine_up = group_products(
+        place, [(middle_low, lifted_low), (attended, branch_grad)]
+    )
+    down = Reduction(place, mine_down.astype(jnp.float32) + core_down.astype(jnp.float32), False)
     down.prepare()
     theirs_up, mine_up, down.parts = tie(theirs_up, mine_up, down.parts)
     down.send()
     core_up = place.send(theirs_up, 1)
-    up = Reduction(place, mine_up + core_up.astype(jnp.float32), True)
+    up = Reduction(place, mine_up.astype(jnp.float32) + core_up.astype(jnp.float32), True)
     up.prepare()
     second, up.parts = tie(second, up.parts)
     up.send()
-    branch_grad, projected_grad, mine_rows, theirs_rows, position_grad, attention_sums = attention_back(
+    projected_grad, mine_rows, theirs_rows, position_grad, attention_sums = attention_back(
         gradient_slot,
         second,
         (projected, probs, unit1, inverse1),
@@ -1173,29 +1213,19 @@
         chip_slots,
     )
 
-    theirs_rows, down.arrived, up.arrived = tie(theirs_rows, down.arrived, up.arrived)
-    rows = mine_rows + place.send(theirs_rows, 1).astype(jnp.float32)
-    rows = rows.astype(low).reshape(place.far, chip_room, width)
-    arrived = [place.send_swapped(rows[k], k) for k in range(place.far)]
-    down.add()
-    down.prepare()
-    up.add()
-    up.prepare()
-    projected_grad, branch_grad, down.parts, up.parts = tie(
-        projected_grad, branch_grad, down.parts, up.parts
-    )
-    down.send()
-    theirs_two, mine_two = group_products(
-        place, [(normed_low, projected_grad), (attended, branch_grad)]
-    )
-    arrived, down.arrived, up.parts, theirs_two, mine_two = tie(
-        arrived, down.arrived, up.parts, theirs_two, mine_two
-    )
-    core_two = place.send(theirs_two, 1)
-    up.send()
-    arrived = jnp.concatenate(arrived)
-    over_x = [arrived] + [place.send(arrived, mask) for mask in place.x_masks[1:]]
-
+    theirs_rows, position_grad, down.arrived, up.arrived = tie(
+        theirs_rows, position_grad, down.arrived, up.arrived
+    )
+    ids = lax.dynamic_index_in_dim(ids_all, place.b, 3, keepdims=False)
+    ids = merge_ids(ids[:, :, 0], ids[:, :, 1], chip_room)
+    ids = ids.reshape(place.far, 2, place.xs, chip_room)
+    ids = jnp.stack(in_order([ids[i] for i in range(place.far)], place.z))
+    ids = jnp.stack(in_order([ids[:, 0], ids[:, 1]], place.y), 1)
+    ids = jnp.transpose(ids, (2, 1, 0, 3))
+    local = ids - place.b * shard_rows
+    inside = ids >= 0
+    counts = jnp.sum(inside.astype(jnp.int32), -1).reshape(-1)
+    local = jnp.where(inside, local, shard_rows).reshape(-1)
     small_grad = jnp.concatenate([position_grad, attention_sums[:4], feed_sums[:10]], 0)
     small_flat = small_grad.reshape(-1, strip)
     small_piece = -(-small_flat.shape[0] // (16 * place.count)) * 16
@@ -1206,37 +1236,61 @@
         ]
     )
     small_parts = small_padded.reshape(place.blk, place.xs, 2, small_piece, strip)
-    fine = small_piece
     small_mine = lax.dynamic_index_in_dim(small_parts, place.core, 2, keepdims=False)
     small_theirs = lax.dynamic_index_in_dim(small_parts, 1 - place.core, 2, keepdims=False)
-    small_theirs = place.send(to_send(small_theirs, fine), 1)
-    value_two = jnp.concatenate(
-        [mine_two + core_two.astype(jnp.float32), small_mine + from_sent(small_theirs, fine)], 2
-    )
-    two = Reduction(place, value_two, False, fine)
+    rows = mine_rows + place.send(theirs_rows, 1).astype(jnp.float32)
+    small_value = small_mine + one_term(place.send(two_terms(small_theirs), 1))
+    rows = rows.astype(low).reshape(place.far, chip_room, width)
+    down.add()
+    down.prepare()
+    up.add()
+    up.prepare()
+    first_rows = jnp.concatenate([rows[0, :, :strip], rows[0, :, strip:]])
+    rows, first_rows, small_value, projected_grad, down.parts, up.parts, counts, local = tie(
+        rows, first_rows, small_value, projected_grad, down.parts, up.parts, counts, local
+    )
+    arrived = [place.send_split(rows[k], k) for k in range(1, place.far)]
+    down.send()
+    up_shape = up.parts[0].shape
+    up_y = place.send(jnp.concatenate([up.parts[0].reshape(-1, strip), first_rows]), place.grp)
+    theirs_two, mine_two = group_products(place, [(normed_low, projected_grad)])
+    arrived, down.arrived, up_y, theirs_two, mine_two = tie(
+        arrived, down.arrived, up_y, theirs_two, mine_two
+    )
+    cut = up_y.shape[0] - first_rows.shape[0]
+    up.arrived = [up_y[:cut].reshape(up_shape)]
+    other_y = jnp.concatenate([up_y[cut : cut + chip_room], up_y[cut + chip_room :]], 1)
+    arrived = jnp.concatenate([jnp.where(place.core == 0, rows[0], other_y)] + arrived)
+    over_x = [arrived] + [place.send(arrived, mask) for mask in place.x_masks[1:]]
+    core_two = place.send(theirs_two, 1)
+    near = [arrived, place.send(arrived, 1)]
+    two = Reduction(
+        place, mine_two.astype(jnp.float32) + core_two.astype(jnp.float32), False, small_value
+    )
     two.prepare()
-    over_x, up.arrived, two.parts = tie(over_x, up.arrived, two.parts)
-    two.send()
     down.add()
     up.add()
     one = Reduction(place, jnp.zeros((place.blk, place.xs, 16, strip), low), False)
     one.stages = one.stages[-1:]
     one.value = jnp.concatenate([down.value, up.value], 1)
     one.prepare()
-    over_x, one.parts = tie(over_x, one.parts)
+    near, two.parts, one.parts = tie(near, two.parts, one.parts)
+    two.send()
     one.send()
-    sources = [item for value in over_x for item in (value, place.send(value, 1))]
-    ids = lax.dynamic_index_in_dim(ids_all, place.b, 3, keepdims=False)
-    ids = merge_ids(ids[:, :, 0], ids[:, :, 1], chip_room)
-    ids = ids.reshape(place.far, 2, place.xs, chip_room)
-    ids = jnp.stack(in_order([ids[i] for i in range(place.far)], place.z))
-    ids = jnp.transpose(ids, (2, 1, 0, 3))
-    local = ids - place.b * shard_rows
-    inside = ids >= 0
-    counts = jnp.sum(inside.astype(jnp.int32), -1).reshape(-1)
-    local = jnp.where(inside, local, shard_rows).reshape(-1)
+    own_total = word_sum(
+        place.g, counts, local, near, shard_rows, place.far, chip_room
+    )
+    own_total, two.arrived, over_x = tie(own_total, two.arrived, over_x)
+    others = [item for value in over_x[1:] for item in (value, place.send(value, 1))]
+    two.add()
+    two.prepare()
+    others, two.parts = tie(others, two.parts)
+    two.send()
+
     def few_rows():
-        return word_sum(place.g, counts, local, sources, shard_rows, place.far, chip_room)
+        return word_sum(
+            place.g, counts, local, others, shard_rows, place.far, chip_room, own_total
+        )
 
     def all_rows():
         token_halves = attention_back(
@@ -1247,8 +1301,8 @@
             (qkv_weight, out_weight),
             seq_len,
             head_dim,
-            slots,
-        )[2:4]
+            tokens,
+        )[1:3]
         token_grads = jnp.concatenate([token_halves[0].astype(low), token_halves[1]])
         every_id = lax.all_gather(flat_ids, "blk", axis=0, tiled=True) - place.b * shard_rows
         every_row = lax.all_gather(token_grads, "blk", axis=0, tiled=True)
@@ -1270,14 +1324,9 @@
     two.send()
     one.add()
     two.add()
-    two.prepare()
-    one.value, two.parts = tie(one.value, two.parts)
-    two.send()
     piece_one = one.value.astype(low)
     one_x = [piece_one] + [place.send(piece_one, mask) for mask in place.x_masks[1:]]
-    two.add()
-    cut = two.value.shape[0] - small_piece
-    piece_two, small_own = two.value[:cut].astype(low), two.value[cut:]
+    piece_two, small_own = two.value.astype(low), two.small
     squares = jnp.sum(small_own * small_own, 0, keepdims=True)
     for item in (piece_one, piece_two):
         item = item.astype(jnp.float32)
@@ -1290,9 +1339,9 @@
     late, two_x = tie(late, two_x)
     middle = [a + b for a in place.y_masks for b in place.x_masks]
     late = gather_stage(place, late, middle, place.y * place.xs + place.x)
+    late = gather_stage(place, late, place.core_masks, place.core)
+    late, one_x, two_x = tie(late, one_x, two_x)
     pieces_one = [item for value in one_x for item in (value, place.send(value, 1))]
-    late, pieces_one = tie(late, pieces_one)
-    late = gather_stage(place, late, place.core_masks, place.core)
     pieces_two = [item for value in two_x for item in (value, place.send(value, 1))]
     late = late.reshape((2, 2, place.xs, place.far) + late.shape[3:])
     late = jnp.transpose(late, (3, 1, 2, 0, 4, 5)).reshape(place.count, -1, strip)
@@ -1301,9 +1350,9 @@
     grad_norm = jnp.sqrt(jnp.sum(late[:, small_piece]))
     factor = (clip_bound / jnp.maximum(grad_norm, clip_bound)).reshape(1)
     word_results = adam_rows(factor, word_rows, word_master, word_moments, rate_table[0])
-    masters = (down_master, up_master, qkv_master, out_master, small_rows)
-    moments = (down_moments, up_moments, qkv_moments, out_moments, small_moments)
-    rates = tuple(rate_table[i] for i in (4, 3, 1, 2, 5))
+    masters = (down_master, up_master, out_master, qkv_master, small_rows)
+    moments = (down_moments, up_moments, out_moments, qkv_moments, small_moments)
+    rates = tuple(rate_table[i] for i in (4, 3, 2, 1, 5))
     if all(item.shape[0] % (16 * place.xs) == 0 for item in masters[:4]):
         results = adam_matrices(
             place.g, factor, pieces_one, pieces_two, small_total, masters, moments, rates
@@ -1325,7 +1374,7 @@
         results = []
         for grad, moment, master, rate in zip(grads, moments, masters, rates):
             results.extend(adam_update(grad * factor[0], moment, master, rate))
-    down, up, qkv, out, small = (results[3 * n : 3 * n + 3] for n in range(5))
+    down, up, out, qkv, small = (results[3 * n : 3 * n + 3] for n in range(5))
     results = [*word_results, *qkv, *out, *up, *down, *small]
     return (loss_total, pair_count, grad_norm, *results)
 

time: 464 us -> 444 us (0.957)
  waiting for transfers between devices: 85 us -> 68.6 us
    ppermute x50, waiting for transfers between devices: 80.8 us -> 58.4 us  [send(): return lax.ppermute(value, both, pairs)]
    pallas_call x1 -> x2, Pallas kernels: 20.4 us -> 30.5 us  [word_sum(): pl.pallas_call(functools.partial(word_sum_kernel, sources=count, chunks=c...]
    unnamed x93 -> x83, local copies, waits for them, and re-layouts: 14.2 us -> 23.1 us
    ppermute x4 -> x3, waiting for transfers between devices: 4.17 us -> 10.1 us  [send_split(): lax.ppermute(value, both, [(i, i ^ masks[i % 2]) for i in range(self.coun...]
    add x16 -> x12, other arithmetic: 10.8 us -> 11.6 us  [the longest x8 6.75 us: add_up(): terms = [terms[i] + terms[i + 1] for i in range(0, len(terms), 2)]]
  transfers between devices with their start and end apart: 54 -> 53, of which waited for: 25 -> 25; matrix products, arithmetic and copies ran while one was open for 9% -> 7% of each run, Pallas kernels for 25% -> 26%
where the time goes in v4:
time: 444 us; the launch traced here: 437 us
  Pallas kernels  201 us (45%)
  waiting for transfers between devices  68.6 us (15%)
  starting transfers between devices  56.7 us (13%)
  local copies, waits for them, and re-layouts  43.6 us (10%)
  other arithmetic  41.8 us (9%)
  between operations  23.6 us (5%)
    ppermute x50, waiting for transfers between devices, send(): return lax.ppermute(value, both, pairs)  58.4 us
    ppermute x50, starting transfers between devices, send(): return lax.ppermute(value, both, pairs)  52.3 us
    pallas_call x1, Pallas kernels, forward(): pl.pallas_call(functools.partial(forward_kernel, seq_len=seq_len, seqs=se...  43.5 us
    pallas_call x3, Pallas kernels, weight_grads(): pl.pallas_call(functools.partial(weight_grad_kernel, jobs=jobs, xs=place....  33.4 us
    pallas_call x1, Pallas kernels, attention_back(): pl.pallas_call(functools.partial(attention_back_kernel, seq_len=seq_len,...  32.8 us
    pallas_call x2, Pallas kernels, word_sum(): pl.pallas_call(functools.partial(word_sum_kernel, sources=count, chunks=c...  30.5 us
    pallas_call x1, Pallas kernels, adam_rows(): pl.pallas_call(functools.partial(adam_kernel, rate=rate), out_shape=[jax....  28.4 us
    unnamed x83, local copies, waits for them, and re-layouts  23.1 us
  transfers between devices with their start and end apart: 53, of which 25 were waited for; matrix products, arithmetic and copies ran while one was open for 7% of the time, Pallas kernels for 26%

profile of v4, /device:TPU:0, one launch (start us, length us, event | category | flops | bytes accessed | tf_op | source)
XLA Modules:
  0.0 436.9 jit_solution(16917654775019769602)
XLA Ops:
  15.3 2.4 collective-permute-start
  21.7 10.4 %gather_fusion.1 = bf16[896,768]{1,0:T(8,128)(2,1)S(1)} fusion(bf16[7680,768]{1,0:T(8,128)(2,1)} %param.29, s32[1024]{0:T(1024)S(1)} %pad_clamp_fusion), kind=kCustom, calls=%fused_computation.1 | custom fusion | bytes 2756096 | tf_op jit(solution)/shard_map/gather | solution.py:1058
  37.0 3.7 collective-permute-start.4
  43.7 2.9 collective-permute-done.5
  49.6 4.2 collective-permute-done.9
  56.6 43.5 %encoder_forward.1 = (bf16[1024,768]{1,0:T(8,128)(2,1)}, f32[1024,1]{1,0:T(8,128)}, bf16[1024,768]{1,0:T(8,128)(2,1)}, bf16[1024,2304]{1,0:T(8,128)(2,1)}, bf16[...) custom-call(s32[8]{0:T(128)} %reshape.568.lengths_ref, ...), custom_call_target="tpu_custom_call" | custom-call | flops 20000000000 | bytes 50000000 | tf_op jit(solution)/shard_map/encoder_forward/pallas_call | solution.py:253
  100.9 4.2 collective-permute-start.10
  107.1 2.6 collective-permute-done.11
  124.7 20.6 %feed_back.1 = (bf16[1024,768]{1,0:T(8,128)(2,1)}, bf16[1024,3072]{1,0:T(8,128)(2,1)}, f32[1024,768]{1,0:T(8,128)}, bf16[1024,768]{1,0:T(8,128)(2,1)}, f32[16,768]{1,0:T(8,128)}) custom-call(s32[8]{0:T(128)} %reshape.568.lengths_ref, f32[4,2,768]{2,1,0:T(2,128)} %maximum_multiply_fusion.embed_grad_ref, f32[4,2,768]{2,1,0:T(2,128)} %get-tuple-element.276.pooled_ref, ...), custom_call_target="tpu_custom_call" | custom-call | flops 10000000000 | bytes 40000000 | tf_op jit(solution)/shard_map/feed_back/pallas_call | solution.py:347
  145.3 10.5 %weight_grads.3 = (bf16[8,2,192,384]{3,2,1,0:T(8,128)(2,1)}, bf16[8,2,192,384]{3,2,1,0:T(8,128)(2,1)}) custom-call(s32[1]{0:T(128)} %bitcast.41.core_ref, bf16[1024,3072]{1,0:T(8,128)(2,1)} %get-tuple-element.285.refs_0_, bf16[1024,768]{1,0:T(8,128)(2,1)} %get-tuple-element.286.refs_1_), custom_call_target="tpu_custom_call" | custom-call | flops 1000 | bytes 1000 | tf_op jit(solution)/shard_map/weight_grads/pallas_call | solution.py:603
  155.9 13.9 %weight_grads.4 = (bf16[8,2,240,384]{3,2,1,0:T(8,128)(2,1)}, bf16[8,2,240,384]{3,2,1,0:T(8,128)(2,1)}) custom-call(s32[1]{0:T(128)} %bitcast.41.core_ref, bf16[1024,768]{1,0:T(8,128)(2,1)} %get-tuple-element.283.refs_0_, bf16[1024,3072]{1,0:T(8,128)(2,1)} %get-tuple-element.289.refs_1_, bf16[1024,768]{1,0:T(8,128)(2,1)} %get-tuple-element.290.refs_2_, ...), custom_call_target="tpu_custom_call" | custom-call | flops 1000 | bytes 1000 | tf_op jit(solution)/shard_map/weight_grads/pallas_call | solution.py:603
  170.4 2.4 copy-done.2
  179.8 2.4 convert_add_fusion
  182.2 2.6 copy-done
  187.5 32.8 %attention_back.3 = (bf16[1024,2304]{1,0:T(8,128)(2,1)}, f32[768,768]{1,0:T(8,128)}, bf16[768,768]{1,0:T(8,128)(2,1)}, f32[128,768]{1,0:T(8,128)}, f32[8,768]{1,0:T(8,128)}) custom-call(s32[1,1024]{1,0:T(1,128)} %compare_select_fusion.4.slots_ref, f32[1024,768]{1,0:T(8,128)} %get-tuple-element.298.second_ref, ...), custom_call_target="tpu_custom_call" | custom-call | flops 10000000000 | bytes 30000000 | tf_op jit(solution)/shard_map/attention_back/pallas_call | solution.py:494
  223.0 2.4 bitcast_add_fusion.1
  239.2 9.0 %weight_grads.5 = (bf16[8,2,144,384]{3,2,1,0:T(8,128)(2,1)}, bf16[8,2,144,384]{3,2,1,0:T(8,128)(2,1)}) custom-call(s32[1]{0:T(128)} %bitcast.41.core_ref, bf16[1024,768]{1,0:T(8,128)(2,1)} %get-tuple-element.322.refs_0_, bf16[1024,2304]{1,0:T(8,128)(2,1)} %get-tuple-element.323.refs_1_), custom_call_target="tpu_custom_call" | custom-call | flops 1000 | bytes 1000 | tf_op jit(solution)/shard_map/weight_grads/pallas_call | solution.py:603
  249.5 8.9 %collective-permute-done.24 = bf16[192,768]{1,0:T(8,128)(2,1)S(1)} collective-permute-done((bf16[192,768]{1,0:T(8,128)(2,1)S(1)}, bf16[192,768]{1,0:T(8,128)(2,1)S(1)}, u32[]{:S(2)}, u32[]{:S(2)}) %collective-permute-start.24) | collective-permute-done | bytes 294944 | tf_op jit(solution)/shard_map/ppermute | solution.py:858
  258.4 8.4 %collective-permute-done.27 = bf16[1344,384]{1,0:T(8,128)(2,1)S(1)} collective-permute-done((bf16[1344,384]{1,0:T(8,128)(2,1)S(1)}, bf16[1344,384]{1,0:T(8,128)(2,1)S(1)}, u32[]{:S(2)}, u32[]{:S(2)}) %collective-permute-start.27) | collective-permute-done | bytes 1032224 | tf_op jit(solution)/shard_map/ppermute | solution.py:862
  278.0 13.7 %word_sum.3 = f32[3840,768]{1,0:T(8,128)} custom-call(s32[1]{0:T(128)} %bitcast.71.place_ref, s32[16]{0:T(128)S(1)} %reshape.578.count_ref, s32[3072]{0:T(1024)S(1)} %reshape.579.id_ref, bf16[768,768]{1,0:T(8,128)(2,1)} %copy-done.8, bf16[768,768]{1,0:T(8,128)(2,1)} %copy-done.15), custom_call_target="tpu_custom_call" | custom-call | flops 1000 | bytes 1000 | tf_op jit(solution)/shard_map/word_sum/pallas_call | solution.py:729
  291.7 5.2 %collective-permute-done.31 = bf16[768,768]{1,0:T(8,128)(2,1)} collective-permute-done((bf16[768,768]{1,0:T(8,128)(2,1)S(1)}, bf16[768,768]{1,0:T(8,128)(2,1)}, u32[]{:S(2)}, u32[]{:S(2)}) %collective-permute-start.31) | collective-permute-done | bytes 1179680 | tf_op jit(solution)/shard_map/ppermute | solution.py:862
  297.0 6.1 %collective-permute-done.30 = bf16[4,2,176,384]{3,2,0,1:T(8,128)(2,1)} collective-permute-done((bf16[4,2,176,384]{3,2,0,1:T(8,128)(2,1)}, bf16[4,2,176,384]{3,2,0,1:T(8,128)(2,1)}, u32[]{:S(2)}, u32[]{:S(2)}) %collective-permute-start.30) | collective-permute-done | bytes 1081376 | tf_op jit(solution)/shard_map/ppermute | solution.py:862
  315.1 17.0 %conditional.3 = ((f32[3840,768]{1,0:T(8,128)}, f32[1,768]{1,0:T(1,128)S(1)})) conditional(s32[]{:T(128)} %convert_element_type.261, (s32[]{:T(128)}, s32[16]{0:T(128)S(1)}, s32[3072]{0:T(1024)S(1)}, bf16[768,768]{1,0:T(8,128)(2,1)}, bf16[768,768]{1,0:T(8,128)(2,1)}, /*index=5*/f32[3840,768]{1,0:T(8,128)}) %tuple.57, (s32[1024]{0:T(1024)S(1)}, ...), branch_computations={%region_25.26_spmd, %region_26.30_spmd} | conditional | flops 10025033728 | bytes 188189184 | solution.py:1318
  315.1 16.8 %word_sum.2 = (f32[3840,768]{1,0:T(8,128)}, f32[1,768]{1,0:T(1,128)S(1)}) custom-call(s32[1]{0:T(128)} %bitcast.1.place_ref, s32[16]{0:T(128)S(1)} %get-tuple-element.122.count_ref, s32[3072]{0:T(1024)S(1)} %get-tuple-element.123.id_ref, bf16[768,768]{1,0:T(8,128)(2,1)} %get-tuple-element.124.refs_0_, bf16[768,768]{1,0:T(8,128)(2,1)} %get-tuple-element.125.refs_1_, ...), custom_call_target="tpu_custom_call" | custom-call | flops 1000 | bytes 1000 | tf_op jit(solution)/shard_map/cond/branch_0_fun/word_sum/pallas_call | solution.py:729
  332.2 2.5 collective-permute-done.35
  338.8 3.5 collective-permute-start.39
  342.3 5.3 %collective-permute-start.38 = (bf16[176,384]{1,0:T(8,128)(2,1)S(1)}, bf16[176,384]{1,0:T(8,128)(2,1)S(1)}, u32[]{:S(2)}, u32[]{:S(2)}) collective-permute-start(bf16[176,384]{1,0:T(8,128)(2,1)S(1)} %pad_maximum_fusion.14), channel_id=1, source_target_pairs={{0,16},{1,17},{2,18},{3,19},{4,20},{5,21},{6,22},{7,23},{8,24},{9,... | collective-permute-start | bytes 405512 | tf_op jit(solution)/shard_map/ppermute | solution.py:862
  351.5 4.7 %collective-permute-done.38 = bf16[176,384]{1,0:T(8,128)(2,1)S(1)} collective-permute-done((bf16[176,384]{1,0:T(8,128)(2,1)S(1)}, bf16[176,384]{1,0:T(8,128)(2,1)S(1)}, u32[]{:S(2)}, u32[]{:S(2)}) %collective-permute-start.38) | collective-permute-done | bytes 135200 | tf_op jit(solution)/shard_map/ppermute | solution.py:862
  356.4 2.5 collective-permute-done.40.refs_2_
  372.4 2.6 collective-permute-done.45
  384.4 28.4 %adam_rows.1 = (f32[3840,768]{1,0:T(8,128)}, f32[3840,768]{1,0:T(8,128)}, f32[3840,768]{1,0:T(8,128)}) custom-call(f32[1]{0:T(128)} %bitcast.114.factor_ref, f32[3840,768]{1,0:T(8,128)} %get-tuple-element.359.grad_ref, f32[3840,768]{1,0:T(8,128)} %master_ref.1, f32[2,3840,768]{2,1,0:T(8,128)} %moments_ref.1), custom_call_target="tpu_custom_call" | custom-call | flops 58982400 | bytes 82575360 | tf_op jit(solution)/shard_map/adam_rows/pallas_call | solution.py:765
  414.3 12.1 %adam_matrices.1 = (f32[384,768]{1,0:T(8,128)}, f32[384,768]{1,0:T(8,128)}, f32[384,768]{1,0:T(8,128)}, f32[96,3072]{1,0:T(8,128)}, f32[96,3072]{1,0:T(8,128)}, ...) custom-call(s32[1]{0:T(128)} %bitcast.71.place_ref, ...), custom_call_target="tpu_custom_call" | custom-call | flops 100000000 | bytes 30000000 | tf_op jit(solution)/shard_map/adam_matrices/pallas_call | solution.py:822
  (342 shorter events, 122.0 us)
Async XLA Ops:
  35.1 12.9 %collective-permute-start.7 = (bf16[224,768]{1,0:T(8,128)(2,1)S(1)}, bf16[224,768]{1,0:T(8,128)(2,1)S(1)}, u32[]{:S(2)}, u32[]{:S(2)}) collective-permute-start(bf16[224,768]{1,0:T(8,128)(2,1)S(1)} %get-tuple-element.409), channel_id=1, source_target_pairs={{0,1},{1,0},{2,3},{3,2},{4,5},{5,4},{6,7},{7,6},{8,9},{9,8},{10,11... | collective-permute-start | bytes 1032200 | tf_op jit(solution)/shard_map/ppermute | solution.py:862
  35.1 13.7 %collective-permute-start.8 = (bf16[224,768]{1,0:T(8,128)(2,1)S(1)}, bf16[224,768]{1,0:T(8,128)(2,1)S(1)}, u32[]{:S(2)}, u32[]{:S(2)}) collective-permute-start(bf16[224,768]{1,0:T(8,128)(2,1)S(1)} %get-tuple-element.408), channel_id=1, source_target_pairs={{0,2},{1,3},{2,0},{3,1},{4,6},{5,7},{6,4},{7,5},{8,10},{9,11},{10,... | collective-permute-start | bytes 1032200 | tf_op jit(solution)/shard_map/ppermute | solution.py:862
  37.0 6.4 %collective-permute-start.4 = (s32[2,4,16,128]{3,2,1,0:T(8,128)S(1)}, s32[2,4,16,128]{3,2,1,0:T(8,128)S(1)}, u32[]{:S(2)}, u32[]{:S(2)}) collective-permute-start(s32[2,4,16,128]{3,2,1,0:T(8,128)S(1)} %pad_add_fusion.1), channel_id=1, source_target_pairs={{0,24},{1,25},{2,26},{3,27},{4,28},{5,29},{6,30},{7,31},{8,16},{9,... | collective-permute-start | bytes 196616 | tf_op jit(solution)/shard_map/ppermute | solution.py:862
  40.7 5.9 %collective-permute-start.5 = (s32[2,4,16,128]{3,2,1,0:T(8,128)S(1)}, s32[2,4,16,128]{3,2,1,0:T(8,128)S(1)}, u32[]{:S(2)}, u32[]{:S(2)}) collective-permute-start(s32[2,4,16,128]{3,2,1,0:T(8,128)S(1)} %pad_add_fusion.1), channel_id=1, source_target_pairs={{0,16},{1,17},{2,18},{3,19},{4,20},{5,21},{6,22},{7,23},{8,24},{9,... | collective-permute-start | bytes 196616 | tf_op jit(solution)/shard_map/ppermute | solution.py:862
  40.7 5.9 %collective-permute-start.6 = (s32[2,4,16,128]{3,2,1,0:T(8,128)S(1)}, s32[2,4,16,128]{3,2,1,0:T(8,128)S(1)}, u32[]{:S(2)}, u32[]{:S(2)}) collective-permute-start(s32[2,4,16,128]{3,2,1,0:T(8,128)S(1)} %pad_add_fusion.1), channel_id=1, source_target_pairs={{0,8},{1,9},{2,10},{3,11},{4,12},{5,13},{6,14},{7,15},{8,0},{9,1},... | collective-permute-start | bytes 196616 | tf_op jit(solution)/shard_map/ppermute | solution.py:862
  43.4 10.3 %collective-permute-start.9 = (bf16[224,768]{1,0:T(8,128)(2,1)S(1)}, bf16[224,768]{1,0:T(8,128)(2,1)S(1)}, u32[]{:S(2)}, u32[]{:S(2)}) collective-permute-start(bf16[224,768]{1,0:T(8,128)(2,1)S(1)} %get-tuple-element.407), channel_id=1, source_target_pairs={{0,3},{1,2},{2,1},{3,0},{4,7},{5,6},{6,5},{7,4},{8,11},{9,10},{10,... | collective-permute-start | bytes 1032200 | tf_op jit(solution)/shard_map/ppermute | solution.py:862
  100.9 6.3 %collective-permute-start.10 = (bf16[16,768]{1,0:T(8,128)(2,1)S(1)}, bf16[16,768]{1,0:T(8,128)(2,1)S(1)}, u32[]{:S(2)}, u32[]{:S(2)}) collective-permute-start(bf16[16,768]{1,0:T(8,128)(2,1)S(1)} %concatenate.96), channel_id=1, source_target_pairs={{0,24},{1,25},{2,26},{3,27},{4,28},{5,29},{6,30},{7,31},{8,16},{9,... | collective-permute-start | bytes 73736 | tf_op jit(solution)/shard_map/ppermute | solution.py:862
  155.8 14.1 %collective-permute-start.17 = (bf16[8,2,192,384]{3,2,1,0:T(8,128)(2,1)}, bf16[8,2,192,384]{3,2,1,0:T(8,128)(2,1)S(1)}, u32[]{:S(2)}, u32[]{:S(2)}) collective-permute-start(bf16[8,2,192,384]{3,2,1,0:T(8,128)(2,1)} %get-tuple-element.295), channel_id=1, source_target_pairs={{0,1},{1,0},{2,3},{3,2},{4,5},{5,4},{6,7},{7,6},{8,9},{9,8},{10,11... | collective-permute-start | bytes 7077896 | tf_op jit(solution)/shard_map/ppermute | solution.py:862
  184.9 36.1 %collective-permute-start.20 = (bf16[4,2,240,384]{3,2,0,1:T(8,128)(2,1)S(1)}, bf16[4,2,240,384]{3,2,0,1:T(8,128)(2,1)S(1)}, u32[]{:S(2)}, u32[]{:S(2)}) collective-permute-start(bf16[4,2,240,384]{3,2,0,1:T(8,128)(2,1)S(1)} %fusion.16), channel_id=1, source_target_pairs={{0,2},{1,3},{2,0},{3,1},{4,6},{5,7},{6,4},{7,5},{8,10},{9,11},{10,... | collective-permute-start | bytes 4423688 | tf_op jit(solution)/shard_map/ppermute | solution.py:862
  186.0 35.0 %collective-permute-start.19 = (bf16[4,2,192,384]{3,2,0,1:T(8,128)(2,1)}, bf16[4,2,192,384]{3,2,0,1:T(8,128)(2,1)}, u32[]{:S(2)}, u32[]{:S(2)}) collective-permute-start(bf16[4,2,192,384]{3,2,0,1:T(8,128)(2,1)} %fusion.17), channel_id=1, source_target_pairs={{0,4},{1,5},{2,6},{3,7},{4,0},{5,1},{6,2},{7,3},{8,12},{9,13},{10,... | collective-permute-start | bytes 3538952 | tf_op jit(solution)/shard_map/ppermute | solution.py:862
  221.1 8.4 %collective-permute-start.21 = (bf16[768,768]{1,0:T(8,128)(2,1)}, bf16[768,768]{1,0:T(8,128)(2,1)}, u32[]{:S(2)}, u32[]{:S(2)}) collective-permute-start(bf16[768,768]{1,0:T(8,128)(2,1)} %get-tuple-element.308), channel_id=1, source_target_pairs={{0,1},{1,0},{2,3},{3,2},{4,5},{5,4},{6,7},{7,6},{8,9},{9,8},{10,11... | collective-permute-start | bytes 3538952 | tf_op jit(solution)/shard_map/ppermute | solution.py:862
  232.5 34.3 %collective-permute-start.27 = (bf16[1344,384]{1,0:T(8,128)(2,1)S(1)}, bf16[1344,384]{1,0:T(8,128)(2,1)S(1)}, u32[]{:S(2)}, u32[]{:S(2)}) collective-permute-start(bf16[1344,384]{1,0:T(8,128)(2,1)S(1)} %pad_maximum_fusion.4), channel_id=1, source_target_pairs={{0,4},{1,5},{2,6},{3,7},{4,0},{5,1},{6,2},{7,3},{8,12},{9,13},{10,... | collective-permute-start | bytes 3096584 | tf_op jit(solution)/shard_map/ppermute | solution.py:862
  233.7 24.7 %collective-permute-start.26 = (bf16[4,192,384]{2,1,0:T(8,128)(2,1)S(1)}, bf16[4,192,384]{2,1,0:T(8,128)(2,1)S(1)}, u32[]{:S(2)}, u32[]{:S(2)}) collective-permute-start(bf16[4,192,384]{2,1,0:T(8,128)(2,1)S(1)} %fusion.31), channel_id=1, source_target_pairs={{0,2},{1,3},{2,0},{3,1},{4,6},{5,7},{6,4},{7,5},{8,10},{9,11},{10,... | collective-permute-start | bytes 1769480 | tf_op jit(solution)/shard_map/ppermute | solution.py:862
  234.8 14.7 %collective-permute-start.23 = (bf16[192,768]{1,0:T(8,128)(2,1)S(1)}, bf16[192,768]{1,0:T(8,128)(2,1)S(1)}, u32[]{:S(2)}, u32[]{:S(2)}) collective-permute-start(bf16[192,768]{1,0:T(8,128)(2,1)S(1)} %get-tuple-element.415), channel_id=1, source_target_pairs={{0,8},{1,13},{2,10},{3,15},{4,12},{5,9},{6,14},{7,11},{8,0},{9,5},... | collective-permute-start | bytes 884744 | tf_op jit(solution)/shard_map/ppermute | solution.py:858
  234.9 23.5 %collective-permute-start.24 = (bf16[192,768]{1,0:T(8,128)(2,1)S(1)}, bf16[192,768]{1,0:T(8,128)(2,1)S(1)}, u32[]{:S(2)}, u32[]{:S(2)}) collective-permute-start(bf16[192,768]{1,0:T(8,128)(2,1)S(1)} %get-tuple-element.414), channel_id=1, source_target_pairs={{0,16},{1,21},{2,18},{3,23},{4,20},{5,17},{6,22},{7,19},{8,24},{9,... | collective-permute-start | bytes 884744 | tf_op jit(solution)/shard_map/ppermute | solution.py:858
  237.0 21.4 %collective-permute-start.25 = (bf16[192,768]{1,0:T(8,128)(2,1)S(1)}, bf16[192,768]{1,0:T(8,128)(2,1)S(1)}, u32[]{:S(2)}, u32[]{:S(2)}) collective-permute-start(bf16[192,768]{1,0:T(8,128)(2,1)S(1)} %get-tuple-element.413), channel_id=1, source_target_pairs={{0,24},{1,29},{2,26},{3,31},{4,28},{5,25},{6,30},{7,27},{8,16},{9,... | collective-permute-start | bytes 884744 | tf_op jit(solution)/shard_map/ppermute | solution.py:858
  268.4 7.4 %collective-permute-start.28 = (bf16[768,768]{1,0:T(8,128)(2,1)S(1)}, bf16[768,768]{1,0:T(8,128)(2,1)S(1)}, u32[]{:S(2)}, u32[]{:S(2)}) collective-permute-start(bf16[768,768]{1,0:T(8,128)(2,1)S(1)} %pad_maximum_fusion.1.refs_0_), channel_id=1, source_target_pairs={{0,1},{1,0},{2,3},{3,2},{4,5},{5,4},{6,7},{7,6},{8,9},{9,8},{10,11... | collective-permute-start | bytes 3538952 | tf_op jit(solution)/shard_map/ppermute | solution.py:862
  268.7 28.3 %collective-permute-start.31 = (bf16[768,768]{1,0:T(8,128)(2,1)S(1)}, bf16[768,768]{1,0:T(8,128)(2,1)}, u32[]{:S(2)}, u32[]{:S(2)}) collective-permute-start(bf16[768,768]{1,0:T(8,128)(2,1)S(1)} %pad_maximum_fusion.1.refs_0_), channel_id=1, source_target_pairs={{0,2},{1,3},{2,0},{3,1},{4,6},{5,7},{6,4},{7,5},{8,10},{9,11},{10,... | collective-permute-start | bytes 3538952 | tf_op jit(solution)/shard_map/ppermute | solution.py:862
  276.8 26.3 %collective-permute-start.30 = (bf16[4,2,176,384]{3,2,0,1:T(8,128)(2,1)}, bf16[4,2,176,384]{3,2,0,1:T(8,128)(2,1)}, u32[]{:S(2)}, u32[]{:S(2)}) collective-permute-start(bf16[4,2,176,384]{3,2,0,1:T(8,128)(2,1)} %pad_maximum_fusion.3), channel_id=1, source_target_pairs={{0,4},{1,5},{2,6},{3,7},{4,0},{5,1},{6,2},{7,3},{8,12},{9,13},{10,... | collective-permute-start | bytes 3244040 | tf_op jit(solution)/shard_map/ppermute | solution.py:862
  307.6 27.1 %collective-permute-start.33 = (bf16[4,176,384]{2,1,0:T(8,128)(2,1)}, bf16[4,176,384]{2,1,0:T(8,128)(2,1)S(1)}, u32[]{:S(2)}, u32[]{:S(2)}) collective-permute-start(bf16[4,176,384]{2,1,0:T(8,128)(2,1)} %pad_maximum_fusion.7), channel_id=1, source_target_pairs={{0,2},{1,3},{2,0},{3,1},{4,6},{5,7},{6,4},{7,5},{8,10},{9,11},{10,... | collective-permute-start | bytes 1622024 | tf_op jit(solution)/shard_map/ppermute | solution.py:862
  308.6 23.6 %collective-permute-start.34 = (bf16[432,384]{1,0:T(8,128)(2,1)}, bf16[432,384]{1,0:T(8,128)(2,1)}, u32[]{:S(2)}, u32[]{:S(2)}) collective-permute-start(bf16[432,384]{1,0:T(8,128)(2,1)} %get-tuple-element.344), channel_id=1, source_target_pairs={{0,8},{1,9},{2,10},{3,11},{4,12},{5,13},{6,14},{7,15},{8,0},{9,1},... | collective-permute-start | bytes 995336 | tf_op jit(solution)/shard_map/ppermute | solution.py:862
  308.6 26.1 %collective-permute-start.35 = (bf16[432,384]{1,0:T(8,128)(2,1)}, bf16[432,384]{1,0:T(8,128)(2,1)}, u32[]{:S(2)}, u32[]{:S(2)}) collective-permute-start(bf16[432,384]{1,0:T(8,128)(2,1)} %get-tuple-element.345), channel_id=1, source_target_pairs={{0,16},{1,17},{2,18},{3,19},{4,20},{5,21},{6,22},{7,23},{8,24},{9,... | collective-permute-start | bytes 995336 | tf_op jit(solution)/shard_map/ppermute | solution.py:862
  310.6 24.1 %collective-permute-start.36 = (bf16[432,384]{1,0:T(8,128)(2,1)S(1)}, bf16[432,384]{1,0:T(8,128)(2,1)}, u32[]{:S(2)}, u32[]{:S(2)}) collective-permute-start(bf16[432,384]{1,0:T(8,128)(2,1)S(1)} %get-tuple-element.346), channel_id=1, source_target_pairs={{0,24},{1,25},{2,26},{3,27},{4,28},{5,29},{6,30},{7,31},{8,16},{9,... | collective-permute-start | bytes 995336 | tf_op jit(solution)/shard_map/ppermute | solution.py:862
  338.8 12.7 %collective-permute-start.39 = (bf16[176,384]{1,0:T(8,128)(2,1)S(1)}, bf16[176,384]{1,0:T(8,128)(2,1)S(1)}, u32[]{:S(2)}, u32[]{:S(2)}) collective-permute-start(bf16[176,384]{1,0:T(8,128)(2,1)S(1)} %pad_maximum_fusion.15), channel_id=1, source_target_pairs={{0,24},{1,25},{2,26},{3,27},{4,28},{5,29},{6,30},{7,31},{8,16},{9,... | collective-permute-start | bytes 405512 | tf_op jit(solution)/shard_map/ppermute | solution.py:862
  342.3 13.9 %collective-permute-start.38 = (bf16[176,384]{1,0:T(8,128)(2,1)S(1)}, bf16[176,384]{1,0:T(8,128)(2,1)S(1)}, u32[]{:S(2)}, u32[]{:S(2)}) collective-permute-start(bf16[176,384]{1,0:T(8,128)(2,1)S(1)} %pad_maximum_fusion.14), channel_id=1, source_target_pairs={{0,16},{1,17},{2,18},{3,19},{4,20},{5,21},{6,22},{7,23},{8,24},{9,... | collective-permute-start | bytes 405512 | tf_op jit(solution)/shard_map/ppermute | solution.py:862
  347.6 8.6 %collective-permute-start.37 = (bf16[176,384]{1,0:T(8,128)(2,1)S(1)}, bf16[176,384]{1,0:T(8,128)(2,1)S(1)}, u32[]{:S(2)}, u32[]{:S(2)}) collective-permute-start(bf16[176,384]{1,0:T(8,128)(2,1)S(1)} %pad_maximum_fusion.13), channel_id=1, source_target_pairs={{0,8},{1,9},{2,10},{3,11},{4,12},{5,13},{6,14},{7,15},{8,0},{9,1},... | collective-permute-start | bytes 405512 | tf_op jit(solution)/shard_map/ppermute | solution.py:862
  350.4 8.5 %collective-permute-start.40 = (bf16[432,384]{1,0:T(8,128)(2,1)}, bf16[432,384]{1,0:T(8,128)(2,1)S(1)}, u32[]{:S(2)}, u32[]{:S(2)}) collective-permute-start(bf16[432,384]{1,0:T(8,128)(2,1)} %get-tuple-element.363.refs_0_), channel_id=1, source_target_pairs={{0,2},{1,3},{2,0},{3,1},{4,6},{5,7},{6,4},{7,5},{8,10},{9,11},{10,... | collective-permute-start | bytes 995336 | tf_op jit(solution)/shard_map/ppermute | solution.py:862
  368.9 6.1 %collective-permute-start.45 = (f32[4,24,384]{2,1,0:T(8,128)S(1)}, f32[4,24,384]{2,1,0:T(8,128)S(1)}, u32[]{:S(2)}, u32[]{:S(2)}) collective-permute-start(f32[4,24,384]{2,1,0:T(8,128)S(1)} %pad_maximum_fusion.12), channel_id=1, source_target_pairs={{0,6},{1,7},{2,4},{3,5},{4,2},{5,3},{6,0},{7,1},{8,14},{9,15},{10,... | collective-permute-start | bytes 442376 | tf_op jit(solution)/shard_map/ppermute | solution.py:862
  379.0 33.8 %collective-permute-start.49 = (bf16[432,384]{1,0:T(8,128)(2,1)}, bf16[432,384]{1,0:T(8,128)(2,1)S(1)}, u32[]{:S(2)}, u32[]{:S(2)}) collective-permute-start(bf16[432,384]{1,0:T(8,128)(2,1)} %get-tuple-element.363.refs_0_), channel_id=1, source_target_pairs={{0,1},{1,0},{2,3},{3,2},{4,5},{5,4},{6,7},{7,6},{8,9},{9,8},{10,11... | collective-permute-start | bytes 995336 | tf_op jit(solution)/shard_map/ppermute | solution.py:862
  379.2 33.6 %collective-permute-start.50 = (bf16[432,384]{1,0:T(8,128)(2,1)S(1)}, bf16[432,384]{1,0:T(8,128)(2,1)S(1)}, u32[]{:S(2)}, u32[]{:S(2)}) collective-permute-start(bf16[432,384]{1,0:T(8,128)(2,1)S(1)} %collective-permute-done.40.refs_2_), channel_id=1, source_target_pairs={{0,1},{1,0},{2,3},{3,2},{4,5},{5,4},{6,7},{7,6},{8,9},{9,8},{10,11... | collective-permute-start | bytes 995336 | tf_op jit(solution)/shard_map/ppermute | solution.py:862
  381.3 31.4 %collective-permute-start.51 = (bf16[144,384]{1,0:T(8,128)(2,1)S(1)}, bf16[144,384]{1,0:T(8,128)(2,1)S(1)}, u32[]{:S(2)}, u32[]{:S(2)}) collective-permute-start(bf16[144,384]{1,0:T(8,128)(2,1)S(1)} %get-tuple-element.365.refs_4_), channel_id=1, source_target_pairs={{0,1},{1,0},{2,3},{3,2},{4,5},{5,4},{6,7},{7,6},{8,9},{9,8},{10,11... | collective-permute-start | bytes 331784 | tf_op jit(solution)/shard_map/ppermute | solution.py:862
  381.5 31.2 %collective-permute-start.52 = (bf16[144,384]{1,0:T(8,128)(2,1)S(1)}, bf16[144,384]{1,0:T(8,128)(2,1)S(1)}, u32[]{:S(2)}, u32[]{:S(2)}) collective-permute-start(bf16[144,384]{1,0:T(8,128)(2,1)S(1)} %collective-permute-done.44.refs_6_), channel_id=1, source_target_pairs={{0,1},{1,0},{2,3},{3,2},{4,5},{5,4},{6,7},{7,6},{8,9},{9,8},{10,11... | collective-permute-start | bytes 331784 | tf_op jit(solution)/shard_map/ppermute | solution.py:862
  (60 other events, 336.8 us)
